TPU v7x, 512 devices: a whole 4x4x16 slice. The times are simulated.
512 devices in a mesh: shard: 128 (over y, z, core), lane: 4 (over x).
Axes of the slice: x: 4, y: 4, z: 16, core: 2. Of those that a mesh axis runs over, the one named last changes fastest.
Arguments:
- descriptors: bfloat16 [16384, 2048], P('shard', 'lane'), may hold values from -8 to 8
- neighbours: int32 [16384, 10], P('shard'), may hold values from 0 to 16383, as said below
- owned: int32 [16384, 10], P('shard'), may hold values 0 or 1
- queries: bfloat16 [1024, 2048], P('lane'), may hold values from -6 to 6
- candidates: int32 [1024, 2], P('lane'), may hold values from 0 to 127, as said below
Outputs:
- augmented: bfloat16 [16384, 2048], P('shard', 'lane')
- scores: float32 [1024, 256], P('lane')
Inputs may be any that keep to these rules, and one draw needn't show every extreme that they name: `neighbours`: of the 1280 slots of the images of one index of shard, exactly 15 name images of each of half of the shards and 5 name images of each other shard; which shards, slots and images is drawn. `candidates`: every block number is named by exactly 16 of the 2048 entries; which ones is drawn, and a query may name one block twice.
All inputs are finite; a program needn't handle non-finite values. No bound on the sum of `owned` on one device may be relied on, other than what follows from the above.
Results may differ from a plain program's by a relative error of at most 0.0028.
Values may be sent and summed in bfloat16 or wider, within the bound.
No kernel may reach another device: no remote copies, remote signals or barrier semaphores. Data moves between devices by JAX's collectives and lax.ppermute only.
A program may use at most 64 MiB of HBM per device.

v0:
```python
import math

import jax
import jax.numpy as jnp
from jax import lax
from jax.sharding import PartitionSpec as P

D = 2048
BLOCK = 128


def pick_rows(descriptors, wanted):
    located = jnp.take(descriptors, jnp.maximum(wanted, 0) // 2, axis=0)
    return jnp.where((wanted >= 0)[..., None], located, jnp.zeros_like(located))


def add_reverse(reverse_terms, wanted, rows_here):
    width_here = reverse_terms.shape[-1]
    segment_ids = jnp.where(wanted >= 0, wanted // 2, rows_here).reshape(-1)
    flat_terms = reverse_terms.reshape(-1, width_here).astype(jnp.float32)
    added = jax.ops.segment_sum(flat_terms, segment_ids, num_segments=rows_here + 1)
    return added[:rows_here]


def per_device(descriptors, neighbours, owned, queries, candidates):
    rows_here, width_here = descriptors.shape
    slots_row = neighbours.shape[1]
    shards = lax.axis_size("shard")
    shard_pos = lax.axis_index("shard")
    capacity = 3 * rows_here * slots_row // (2 * shards)
    slot_count = rows_here * slots_row
    total_slots = shards * capacity
    flat_ids = neighbours.reshape(slot_count)
    owned_flat = owned.reshape(slot_count)
    target = flat_ids // rows_here
    local_row = flat_ids - target * rows_here
    matches = (target[:, None] == jnp.arange(shards, dtype=jnp.int32)[None, :]).astype(jnp.int32)
    before = jnp.cumsum(matches, axis=0) - matches
    slot_place = target * capacity + jnp.sum(before * matches, axis=1)
    request_codes = (
        jnp.full((total_slots,), -1, jnp.int32).at[slot_place].set(local_row * 2 + owned_flat)
    )
    request_codes = request_codes.reshape(shards, capacity)
    own_rows = jnp.repeat(descriptors, slots_row, axis=0)
    wanted = lax.all_to_all(request_codes, "shard", split_axis=0, concat_axis=0, tiled=True)
    located = pick_rows(descriptors, wanted)
    returned = lax.all_to_all(located, "shard", split_axis=0, concat_axis=0, tiled=True)
    neighbour_rows = jnp.take(returned.reshape(total_slots, width_here), slot_place, axis=0)
    neighbour_rows = neighbour_rows.reshape(rows_here, slots_row, width_here)
    partial_dots = jnp.einsum(
        "rd,rkd->rk", descriptors, neighbour_rows, preferred_element_type=jnp.float32
    )
    similar = lax.psum(partial_dots, "lane") / D
    weight = similar**3
    forward = jnp.sum(weight[..., None] * neighbour_rows.astype(jnp.float32), axis=1)
    slot_weight = (weight * owned.astype(jnp.float32)).reshape(slot_count)
    reverse_terms = (slot_weight[:, None] * own_rows.astype(jnp.float32)).astype(jnp.bfloat16)
    outgoing = jnp.zeros((total_slots, width_here), jnp.bfloat16).at[slot_place].set(reverse_terms)
    arrived = lax.all_to_all(
        outgoing.reshape(shards, capacity, width_here),
        "shard",
        split_axis=0,
        concat_axis=0,
        tiled=True,
    )
    reverse = add_reverse(arrived, wanted, rows_here)
    summed = descriptors.astype(jnp.float32) + forward + reverse
    energy = lax.psum(jnp.sum(summed * summed, axis=1), "lane") / D
    augmented = (summed * lax.rsqrt(energy + 1e-06)[:, None]).astype(jnp.bfloat16)
    query_cols = lax.all_to_all(queries, "lane", split_axis=1, concat_axis=0, tiled=True)
    all_cands = lax.all_gather(candidates, "lane", axis=0, tiled=True)
    query_count = query_cols.shape[0]
    partial_scores = lax.dot_general(
        query_cols, augmented, (((1,), (1,)), ((), ())), preferred_element_type=jnp.float32
    )
    blocks_here = rows_here // BLOCK
    score_tiles = partial_scores.reshape(query_count, blocks_here, BLOCK)
    local_block = all_cands - shard_pos * blocks_here
    picker = (local_block[..., None] == jnp.arange(blocks_here, dtype=jnp.int32)).astype(
        jnp.float32
    )
    picked = jnp.einsum("qcb,qbk->qck", picker, score_tiles, precision=lax.Precision.HIGHEST)
    picked = picked.reshape(query_count, -1)
    summed_scores = lax.psum(picked, "shard")
    own_share = lax.psum_scatter(summed_scores, "lane", scatter_dimension=0, tiled=True)
    scores = own_share / math.sqrt(D)
    return (augmented, scores)


def solution(mesh):
    return jax.shard_map(
        per_device,
        mesh=mesh,
        in_specs=(
            P("shard", "lane"),
            P("shard", None),
            P("shard", None),
            P("lane", None),
            P("lane", None),
        ),
        out_specs=(P("shard", "lane"), P("lane", None)),
        check_vma=False,
    )
```

profile of v0, /device:TPU:1, one launch (start us, length us, event | category | flops | bytes accessed | tf_op | source)
XLA Modules:
  0.0 718.7 jit_solution(5665986507961950548)
XLA Ops:
  7.2 0.8 copy.63
  8.0 0.1 reshape.339
  8.1 0.1 reshape.338
  8.2 0.1 reshape.341
  8.4 0.1 copy.65
  8.5 0.3 fusion.4
  8.9 0.1 broadcast_add_fusion
  9.0 0.2 copy.66
  9.2 0.3 copy-done.7
  9.6 0.1 copy.70
  9.7 0.1 reshape.342
  9.8 0.4 fusion.8
  10.3 5.2 scatter_custom_fusion
  15.6 0.2 all_to_all.28
  15.8 35.4 %all_to_all.41 = s32[128,1,15]{2,1,0:T(1,128)S(1)} all-to-all(s32[128,1,15]{2,1,0:T(1,128)S(1)} %bitcast.44), channel_id=1, replica_groups=mesh['shard'=128,'lane'=4] {'shard'}, dimensions={0} | all-to-all | bytes 15360 | tf_op jit(solution)/shard_map/all_to_all | solution.py:45
  51.3 0.1 copy.80
  51.5 0.2 reshape.349
  51.7 6.4 gather_fusion
  58.1 1.7 reshape.348
  59.8 0.1 copy.79
  60.0 0.2 copy.73
  60.1 3.0 select_select_fusion
  63.1 6.7 all-to-all-start.1
  69.8 0.1 reduce_sum.32
  70.0 0.1 copy.67
  70.0 1.3 copy.84
  71.4 97.7 %all-to-all-done.1 = bf16[128,15,512]{2,1,0:T(8,128)(2,1)S(1)} async-done(((bf16[128,15,512]{2,1,0:T(8,128)(2,1)}), bf16[128,15,512]{2,1,0:T(8,128)(2,1)S(1)}, u32[]{:S(2)}, u32[]{:S(2)}) %all-to-all-start.1) | async-done | bytes 1966112 | tf_op jit(solution)/shard_map/all_to_all | solution.py:47
  169.1 4.3 all-to-all-start.3
  173.4 0.1 copy.68
  173.5 2.5 broadcast_in_dim.62
  176.0 4.5 convert_element_type.39
  180.5 2.7 reshape.343
  183.2 4.1 gather_fusion.1
  187.3 1.6 gather.12
  188.9 2.7 fusion
  191.6 0.1 copy.88
  191.6 8.9 %psum.21 = f32[128,10]{0,1:T(8,128)S(1)} all-reduce(f32[128,10]{0,1:T(8,128)S(1)} %bitcast.46), channel_id=1, replica_groups=mesh['shard'=128,'lane'=4] {'lane'}, use_global_device_ids=true, to_apply=%region_4.5 | all-reduce | flops 1280 | bytes 10240 | tf_op jit(solution)/shard_map/psum | solution.py:53
  200.6 0.1 copy.82
  200.7 0.1 mul.76
  200.8 10.8 %scatter_custom_fusion.1 = bf16[1920,512]{1,0:T(8,128)(2,1)} fusion(s32[1280]{0:T(1024)} %copy-done.9, f32[1280,512]{1,0:T(8,128)S(1)} %copy-done.1, f32[1280]{0:T(1024)S(1)} %mul.76, bf16[]{:T(256)} %constant.96.clone.1), kind=kCustom, calls=%fused_computation.10 | custom fusion | flops 1310720 | bytes 4593152 | tf_op jit(solution)/shard_map/scatter | solution.py:58
  211.6 3.9 reshape.344
  215.5 11.2 %all-to-all-start.2 = ((bf16[128,15,512]{2,1,0:T(8,128)(2,1)}), bf16[128,15,512]{2,1,0:T(8,128)(2,1)S(1)}, u32[]{:S(2)}, u32[]{:S(2)}) async-start(bf16[128,15,512]{2,1,0:T(8,128)(2,1)} %reshape.344), calls=%async_computation.2 | async-start | bytes 4194304 | tf_op jit(solution)/shard_map/all_to_all | solution.py:59
  226.8 8.8 %all_gather.3 = s32[1024,2]{0,1:T(2,128)S(1)} all-gather(s32[256,2]{0,1:T(2,128)S(1)} %copy-done.10), channel_id=1, replica_groups=mesh['shard'=128,'lane'=4] {'lane'}, dimensions={0}, use_global_device_ids=true | all-gather | bytes 10240 | tf_op jit(solution)/shard_map/all_gather | solution.py:71
  235.6 1.0 copy.83
  236.6 0.5 broadcast.390
  237.2 0.8 reduce.7
  238.0 0.2 all_to_all.31
  238.2 0.7 fusion.22
  238.8 1.5 copy.85
  240.3 0.7 copy.81
  241.1 2.7 multiply_reduce_fusion
  243.8 82.1 %all-to-all-done.2 = bf16[128,15,512]{2,1,0:T(8,128)(2,1)S(1)} async-done(((bf16[128,15,512]{2,1,0:T(8,128)(2,1)}), bf16[128,15,512]{2,1,0:T(8,128)(2,1)S(1)}, u32[]{:S(2)}, u32[]{:S(2)}) %all-to-all-start.2) | async-done | bytes 1966112 | tf_op jit(solution)/shard_map/all_to_all | solution.py:59
  325.9 2.1 reshape.383
  328.0 13.3 %scatter_custom_fusion.2 = f32[129,512]{1,0:T(8,128)S(1)} fusion(s32[1920]{0:T(1024)} %fusion.22, f32[1920,512]{1,0:T(8,128)} %reshape.383, f32[]{:T(128)} %constant.98.clone.1), kind=kCustom, calls=%fused_computation.30 | custom fusion | flops 983040 | bytes 264704 | tf_op jit(solution)/shard_map/scatter-add | solution.py:21
  341.3 0.1 multiply_reduce_fusion.1
  341.4 6.0 psum.22
  347.4 0.1 multiply_convert_fusion.2
  347.6 0.5 convolution_bitcast_fusion
  348.0 0.2 copy.86
  348.2 3.9 broadcast_multiply_fusion
  352.1 1.1 copy.102
  353.3 23.4 %reduce-scatter.2.cloned.1.call-done = f32[256,256]{1,0:T(8,128)} async-done(((f32[1024,256]{1,0:T(8,128)}), f32[256,256]{1,0:T(8,128)}) %reduce-scatter.2.cloned.1.call-update) | async-done | bytes 262160 | tf_op jit(solution)/shard_map/reduce_scatter | solution.py:85
  376.7 333.5 %all-reduce.2.cloned.1.call-done = f32[256,256]{1,0:T(8,128)} async-done(((f32[256,256]{1,0:T(8,128)}), f32[256,256]{1,0:T(8,128)}) %all-reduce.2.cloned.1.call-update) | async-done | bytes 262160 | tf_op jit(solution)/shard_map/psum | solution.py:84
  710.2 1.7 broadcast_multiply_fusion.1
  (43 shorter events, 0.5 us)
Async XLA Ops:
  8.9 0.7 copy-start.7
  8.9 42.8 %copy-start = (bf16[128,512]{1,0:T(8,128)(2,1)S(1)}, bf16[128,512]{1,0:T(8,128)(2,1)}, u32[]{:S(2)}) copy-start(bf16[128,512]{1,0:T(8,128)(2,1)} %param.5) | copy-start | bytes 393220
  10.3 170.2 %copy-start.9 = (s32[1280]{0:T(1024)}, s32[1280]{0:T(1024)S(1)}, u32[]{:S(2)}) copy-start(s32[1280]{0:T(1024)S(1)} %fusion.23) | copy-start | bytes 15364
  63.1 6.9 copy-start.4
  63.1 106.0 %all-to-all-start.1 = ((bf16[128,15,512]{2,1,0:T(8,128)(2,1)}), bf16[128,15,512]{2,1,0:T(8,128)(2,1)S(1)}, u32[]{:S(2)}, u32[]{:S(2)}) async-start(bf16[128,15,512]{2,1,0:T(8,128)(2,1)} %select_select_fusion), calls=%async_computation.1 | async-start | bytes 4194304 | tf_op jit(solution)/shard_map/all_to_all | solution.py:47
  70.0 103.3 %copy-start.6 = (s32[128,10]{0,1:T(8,128)S(1)}, s32[128,10]{0,1:T(8,128)}, u32[]{:S(2)}) copy-start(s32[128,10]{0,1:T(8,128)} %param.6) | copy-start | bytes 15364
  169.1 6.9 copy-start.2
  169.1 46.4 %all-to-all-start.3 = ((bf16[256,4,512]{0,2,1:T(8,128)(2,1)}), bf16[256,4,512]{0,2,1:T(8,128)(2,1)}, u32[]{:S(2)}, u32[]{:S(2)}) async-start(bf16[256,4,512]{0,2,1:T(8,128)(2,1)} %bitcast.9), calls=%async_computation.3 | async-start | bytes 2097152 | tf_op jit(solution)/shard_map/all_to_all | solution.py:70
  188.9 11.7 %copy-start.8 = (s32[128,10]{0,1:T(8,128)S(1)}, s32[128,10]{0,1:T(8,128)}, u32[]{:S(2)}) copy-start(s32[128,10]{0,1:T(8,128)} %param.7) | copy-start | bytes 15364
  188.9 11.9 %copy-start.1 = (f32[1280,512]{1,0:T(8,128)S(1)}, f32[1280,512]{1,0:T(8,128)}, u32[]{:S(2)}) copy-start(f32[1280,512]{1,0:T(8,128)} %convert_element_type.39) | copy-start | bytes 7864324
  215.5 11.3 %copy-start.10 = (s32[256,2]{0,1:T(2,128)S(1)}, s32[256,2]{0,1:T(2,128)}, u32[]{:S(2)}) copy-start(s32[256,2]{0,1:T(2,128)} %param.9) | copy-start | bytes 6148
  215.5 110.4 %all-to-all-start.2 = ((bf16[128,15,512]{2,1,0:T(8,128)(2,1)}), bf16[128,15,512]{2,1,0:T(8,128)(2,1)S(1)}, u32[]{:S(2)}, u32[]{:S(2)}) async-start(bf16[128,15,512]{2,1,0:T(8,128)(2,1)} %reshape.344), calls=%async_computation.2 | async-start | bytes 4194304 | tf_op jit(solution)/shard_map/all_to_all | solution.py:59
  226.7 149.9 %reduce-scatter.2.cloned.1.call-start = ((), (), s32[]{:S(2)}) async-start(), calls=%async_computation.5 | async-start | bytes 1310720 | tf_op jit(solution)/shard_map/reduce_scatter | solution.py:85
  341.3 6.9 copy-start.3
  347.5 4.6 copy-start.5
  353.2 357.0 %all-reduce.2.cloned.1.call-start = ((), (), s32[]{:S(2)}) async-start(), calls=%async_computation.6 | async-start | bytes 524288 | tf_op jit(solution)/shard_map/psum | solution.py:84
Sparse Core Ops, SparseCore 0:
  353.3 23.2 reduce-scatter.1
  380.5 329.6 all-reduce.1
where the time goes:
time: 720 us; the launch traced here: 719 us
  waiting for transfers between devices  537 us (75%)
  blocking collectives  59.1 us (8%)
  local copies, waits for them, and re-layouts  45 us (6%)
  other arithmetic  38 us (5%)
  starting transfers between devices  22.3 us (3%)
  between operations  14.4 us (2%)
    psum x1, waiting for transfers between devices, per_device(): summed_scores = lax.psum(picked, 'shard')  334 us
    all_to_all x1, waiting for transfers between devices, per_device(): lax.all_to_all(located, 'shard', split_axis=0, concat_axis=0, tiled=True)  97.7 us
    all_to_all x1, waiting for transfers between devices, per_device(): lax.all_to_all(outgoing.reshape(shards, capacity, width_here), 'shard', s...  82.1 us
    all_to_all x1, blocking collectives, per_device(): lax.all_to_all(request_codes, 'shard', split_axis=0, concat_axis=0, tiled...  35.4 us
    reduce_scatter x1, waiting for transfers between devices, per_device(): lax.psum_scatter(summed_scores, 'lane', scatter_dimension=0, tiled=True)  23.4 us
  transfers between devices with their start and end apart: 5, of which 4 were waited for; matrix products, arithmetic and copies ran while one was open for 6% of the time, Pallas kernels for 0%

commit v1 on v0

v1 whole, which is shorter than its diff:
```python
import functools
import math

import jax
import jax.numpy as jnp
from jax import lax
from jax.experimental import pallas as pl
from jax.experimental.pallas import tpu as pltpu
from jax.sharding import Mesh
from jax.sharding import PartitionSpec as P

D = 2048
BLOCK = 128
PLACES = 16
GROUP = 8
CORES = 2
LANES = 128
VMEM = 48 * 1024 * 1024
INTERPRET = False
f32 = jnp.float32
bf16 = jnp.bfloat16
i32 = jnp.int32
NT = (((1,), (1,)), ((), ()))
TN = (((0,), (0,)), ((), ()))


def exchange(parts, axis):
    return lax.all_to_all(parts, axis, split_axis=0, concat_axis=0, tiled=True)


def spread(part, axis, count):
    return exchange(jnp.broadcast_to(part[None], (count,) + part.shape), axis)


def params(**more):
    return pltpu.CompilerParams(vmem_limit_bytes=VMEM, **more)


def table_kernel(sizes, listed_ref, owned_ref, table_ref):
    ys, zs = sizes
    rows = listed_ref.shape[0]
    row = lax.broadcasted_iota(i32, (rows, LANES), 0)
    lane = lax.broadcasted_iota(i32, (rows, LANES), 1)
    lower = (row > lane).astype(bf16)
    own_mark = (row + 1).astype(f32)
    before = jnp.zeros((1, LANES), f32)
    high = jnp.zeros((LANES, LANES), f32)
    low = jnp.zeros((LANES, LANES), f32)
    for slot in range(listed_ref.shape[1]):
        listed = listed_ref[:, slot : slot + 1]
        shard = lax.shift_right_logical(listed, 7)
        y = shard // (zs * CORES)
        zc = shard - y * (zs * CORES)
        column = zc * ys + y
        match = lane == column
        ones = match.astype(bf16)
        counted = jnp.dot(lower, ones, preferred_element_type=f32) + before
        before = before + jnp.sum(ones.astype(f32), axis=0, keepdims=True)
        rank = jnp.sum(jnp.where(match, counted, 0.0), axis=1, keepdims=True).astype(i32)
        group = lax.shift_right_logical(column, 3)
        place = (column - group * GROUP) * PLACES + rank
        left = (lane == group).astype(bf16)
        here = lane == place
        source = ((listed & (BLOCK - 1)) * 2 + owned_ref[:, slot : slot + 1]).astype(f32)
        high += lax.dot_general(left, jnp.where(here, own_mark, 0.0).astype(bf16), TN, preferred_element_type=f32)
        low += lax.dot_general(left, jnp.where(here, source, 0.0).astype(bf16), TN, preferred_element_type=f32)
    high = high[:zs].astype(i32)
    low = low[:zs].astype(i32)
    table_ref[...] = jnp.where(high > 0, (high - 1) * 256 + low, -1)


def build_table(neighbours, owned, ys, zs):
    return pl.pallas_call(
        functools.partial(table_kernel, (ys, zs)),
        out_shape=jax.ShapeDtypeStruct((zs, LANES), i32),
        compiler_params=params(),
        interpret=INTERPRET,
        name="slot_table",
    )(neighbours, owned)


def similar_kernel(groups, all_ref, own_ref, src_ref, at_ref, got_ref, sims_ref):
    row = lax.broadcasted_iota(i32, (BLOCK, LANES), 0)
    shards = own_ref.shape[0] // BLOCK

    def step(group, carry):
        first = pl.multiple_of(group * GROUP, GROUP)
        source = src_ref[pl.ds(first, GROUP), :]
        at = at_ref[pl.ds(first, GROUP), :]
        parts = []
        for one in range(GROUP):
            pick = (row == source[one : one + 1]).astype(bf16)
            block = all_ref[pl.ds(pl.multiple_of((first + one) * BLOCK, BLOCK), BLOCK), :]
            parts.append(lax.dot_general(pick, block, TN, preferred_element_type=f32).astype(bf16))
        sims = []
        for shard in range(shards):
            own = own_ref[shard * BLOCK : (shard + 1) * BLOCK, :]
            for kind in range(2):
                k = 2 * shard + kind
                chunk = jnp.concatenate([part[k * PLACES : (k + 1) * PLACES] for part in parts], axis=0)
                got_ref[k, pl.ds(pl.multiple_of(group * LANES, LANES), LANES), :] = chunk
                dots = lax.dot_general(own, chunk, NT, preferred_element_type=f32)
                sims.append(jnp.sum(jnp.where(row == at[k : k + 1], dots, 0.0), axis=0, keepdims=True))
        sims_ref[pl.ds(first, GROUP), :] = jnp.concatenate(sims, axis=0)
        return carry

    lax.fori_loop(0, groups, step, 0)


def similar_parts(everything, own, source, at):
    blocks = everything.shape[0] // BLOCK
    groups = blocks // GROUP
    steps = 4
    per = groups // steps
    kinds = 2 * own.shape[0] // BLOCK
    return pl.pallas_call(
        functools.partial(similar_kernel, per),
        grid=(steps,),
        in_specs=[
            pl.BlockSpec((per * GROUP * BLOCK, LANES), lambda i: (i, 0)),
            pl.BlockSpec(own.shape, lambda i: (0, 0)),
            pl.BlockSpec((per * GROUP, LANES), lambda i: (i, 0)),
            pl.BlockSpec((per * GROUP, LANES), lambda i: (i, 0)),
        ],
        out_specs=[
            pl.BlockSpec((kinds, per * LANES, LANES), lambda i: (0, i, 0)),
            pl.BlockSpec((per * GROUP, LANES), lambda i: (i, 0)),
        ],
        out_shape=[
            jax.ShapeDtypeStruct((kinds, groups * LANES, LANES), bf16),
            jax.ShapeDtypeStruct((groups * GROUP, LANES), f32),
        ],
        compiler_params=params(),
        interpret=INTERPRET,
        name="similar_parts",
    )(everything, own, source, at)


def sum_kernel(groups, got_ref, sims_ref, own_ref, at_ref, sum_ref):
    row = lax.broadcasted_iota(i32, (BLOCK, LANES), 0)
    shards = own_ref.shape[0] // BLOCK

    @pl.when(pl.program_id(0) == 0)
    def _():
        sum_ref[...] = own_ref[...].astype(f32)

    similar = sims_ref[...] / D
    weight = similar * similar * similar
    high = weight.astype(bf16).astype(f32)
    low = weight - high
    for shard in range(shards):
        total = sum_ref[shard * BLOCK : (shard + 1) * BLOCK, :]
        for kind in range(2):
            k = 2 * shard + kind
            left_high, left_low = [], []
            for group in range(groups):
                n = group * GROUP + k
                here = row == at_ref[n : n + 1, :]
                left_high.append(jnp.where(here, high[n : n + 1], 0.0).astype(bf16))
                left_low.append(jnp.where(here, low[n : n + 1], 0.0).astype(bf16))
            got = got_ref[k]
            total += jnp.dot(jnp.concatenate(left_high, axis=1), got, preferred_element_type=f32)
            total += jnp.dot(jnp.concatenate(left_low, axis=1), got, preferred_element_type=f32)
        sum_ref[shard * BLOCK : (shard + 1) * BLOCK, :] = total


def weighted_sum(got, sims, own, at):
    kinds, slots, _ = got.shape
    groups = slots // LANES
    steps = 4
    per = groups // steps
    return pl.pallas_call(
        functools.partial(sum_kernel, per),
        grid=(steps,),
        in_specs=[
            pl.BlockSpec((kinds, per * LANES, LANES), lambda i: (0, i, 0)),
            pl.BlockSpec((per * GROUP, LANES), lambda i: (i, 0)),
            pl.BlockSpec(own.shape, lambda i: (0, 0)),
            pl.BlockSpec((per * GROUP, LANES), lambda i: (i, 0)),
        ],
        out_specs=pl.BlockSpec(own.shape, lambda i: (0, 0)),
        out_shape=jax.ShapeDtypeStruct(own.shape, f32),
        compiler_params=params(),
        interpret=INTERPRET,
        name="weighted_sum",
    )(got, sims, own, at)


def pick_kernel(rows_ref, table_ref, out_ref):
    def step(i, carry):
        for cand in range(2):
            picked = []
            for one in range(GROUP):
                r = rows_ref[i * (2 * GROUP) + 2 * one + cand]
                picked.append(table_ref[pl.ds(r, 1), :])
            at = pl.ds(pl.multiple_of(i * GROUP, GROUP), GROUP)
            out_ref[at, cand * LANES : (cand + 1) * LANES] = jnp.concatenate(picked, axis=0)
        return carry

    lax.fori_loop(0, out_ref.shape[0] // GROUP, step, 0)


def pick_scores(rows, table):
    queries = rows.shape[0] // 2
    return pl.pallas_call(
        pick_kernel,
        in_specs=[pl.BlockSpec(memory_space=pltpu.SMEM), pl.BlockSpec(memory_space=pltpu.VMEM)],
        out_specs=pl.BlockSpec(memory_space=pltpu.VMEM),
        out_shape=jax.ShapeDtypeStruct((queries, 2 * LANES), f32),
        compiler_params=params(),
        interpret=INTERPRET,
        name="pick_scores",
    )(rows, table)


def slot_orders(table, ys, zs):
    toward = exchange(table.reshape(zs, 1, LANES), "z").reshape(zs, LANES)
    both = spread(jnp.stack([table, toward]), ("y", "core"), GROUP)
    both = both.reshape(ys, CORES, 2, zs, LANES)
    core = lax.axis_index("core")
    ahead = lax.dynamic_index_in_dim(both[:, :, 0], core, 1, keepdims=False)
    ahead = ahead.reshape(ys, zs * GROUP, PLACES)
    back = both[:, :, 1].reshape(ys, CORES, zs, CORES, ys * PLACES)
    back = lax.dynamic_index_in_dim(back, core, 3, keepdims=False)
    back = back.reshape(ys, CORES, zs, ys, PLACES).transpose(2, 1, 0, 3, 4)
    back = back.reshape(zs * GROUP, ys, PLACES)
    ahead_own = jnp.where(ahead >= 0, lax.shift_right_logical(ahead, 8), -1)
    ahead_src = jnp.where(ahead >= 0, lax.shift_right_logical(ahead, 1) & (BLOCK - 1), -1)
    held = (back >= 0) & ((back & 1) == 1)
    back_src = jnp.where(held, lax.shift_right_logical(back, 8), -1)
    back_own = jnp.where(held, lax.shift_right_logical(back, 1) & (BLOCK - 1), -1)
    source = jnp.stack([ahead_src.transpose(1, 0, 2), back_src], axis=2).reshape(zs * GROUP, LANES)
    at = jnp.stack([ahead_own, back_own.transpose(1, 0, 2)], axis=1)
    at = at.reshape(2 * ys, zs, LANES).transpose(1, 0, 2).reshape(zs * GROUP, LANES)
    return source, at


def query_entries(queries, candidates, xs, zs):
    flat = candidates.reshape(-1)
    order = jnp.arange(flat.shape[0], dtype=i32)
    earlier = (flat[:, None] == flat[None, :]) & (order[:, None] > order[None, :])
    rank = jnp.sum(earlier.astype(i32), axis=1)
    here = lax.axis_index(("y", "z", "core"))
    hits = (flat == here)[None, :] & (rank[None, :] == jnp.arange(PLACES, dtype=i32)[:, None])
    hits = jnp.sum(hits.reshape(PLACES, -1, 2).astype(f32), axis=2).astype(bf16)
    chosen = jnp.dot(hits, queries, preferred_element_type=f32).astype(bf16)
    chosen = chosen.reshape(PLACES, xs, -1).transpose(1, 0, 2)
    chosen = exchange(chosen, "x").reshape(xs * PLACES, -1)
    y = flat // (zs * CORES)
    z = flat // CORES - y * zs
    core = flat - (flat // CORES) * CORES
    rows = ((y * CORES + core) * zs + z) * PLACES + rank
    return chosen, rows


def per_device(descriptors, neighbours, owned, queries, candidates):
    ys, zs, xs = lax.axis_size("y"), lax.axis_size("z"), lax.axis_size("x")
    rows, width = descriptors.shape
    pieces = descriptors.reshape(rows, ys, LANES).transpose(1, 0, 2)
    own = exchange(pieces, "y").reshape(ys * rows, LANES)
    everything = lax.all_gather(own, ("z", "core"), axis=0, tiled=True)
    table = build_table(neighbours, owned, ys, zs)
    source, at = slot_orders(table, ys, zs)
    chosen, score_rows = query_entries(queries, candidates, xs, zs)
    got, sims = similar_parts(everything, own, source, at)
    share = jnp.sum(exchange(sims.reshape(ys * xs, -1, LANES), ("y", "x")), axis=0)
    sims = spread(share, ("y", "x"), ys * xs).reshape(sims.shape)
    summed = weighted_sum(got, sims, own, at)
    summed = exchange(summed.reshape(ys, rows, LANES), "y").transpose(1, 0, 2).reshape(rows, width)
    energy = jnp.sum(summed * summed, axis=1)
    scores = lax.dot_general(chosen.astype(f32), summed, NT, precision=lax.Precision.HIGHEST)
    parts = jnp.concatenate(
        [scores.reshape(xs, PLACES, rows), jnp.broadcast_to(energy[None, None, :], (xs, 8, rows))], axis=1
    )
    whole = jnp.sum(exchange(parts, "x"), axis=0)
    scale = lax.rsqrt(whole[PLACES] / (xs * width) + 1e-06)
    augmented = (summed * scale[:, None]).astype(bf16)
    mine = whole[:PLACES] * (scale / math.sqrt(xs * width))[None, :]
    plane = spread(mine, "z", zs)
    table = spread(plane, ("y", "core"), GROUP).reshape(-1, rows)
    return augmented, pick_scores(score_rows, table)


def solution(mesh):
    shards, lanes = mesh.devices.shape
    ys = GROUP // CORES
    split = Mesh(mesh.devices.reshape(ys, shards // GROUP, CORES, lanes), ("y", "z", "core", "x"))
    shard = ("y", "z", "core")
    return jax.shard_map(
        per_device,
        mesh=split,
        in_specs=(P(shard, "x"), P(shard, None), P(shard, None), P("x", None), P("x", None)),
        out_specs=(P(shard, "x"), P("x", None)),
        check_vma=False,
    )
```

time: 720 us -> 219 us (0.30)
  waiting for transfers between devices: 537 us -> 81.5 us
  other arithmetic: 38 us -> 3.13 us
  local copies, waits for them, and re-layouts: 45 us -> 12.9 us
  starting transfers between devices: 22.3 us -> 49.6 us
  blocking collectives: 59.1 us -> 35.5 us
  Pallas kernels: 0 us -> 20.5 us
    psum x1 -> x0, waiting for transfers between devices: 334 us -> none  [per_device(): summed_scores = lax.psum(picked, 'shard')]
    all_to_all x3 -> x7, waiting for transfers between devices: 180 us -> 50.3 us  [exchange(): return lax.all_to_all(parts, axis, split_axis=0, concat_axis=0, tiled=True)]
    all_gather x0 -> x1, waiting for transfers between devices: none -> 31.2 us  [per_device(): everything = lax.all_gather(own, ('z', 'core'), axis=0, tiled=True)]
    all_to_all x3 -> x7, starting transfers between devices: 22.2 us -> 49.6 us  [exchange(): return lax.all_to_all(parts, axis, split_axis=0, concat_axis=0, tiled=True)]
    reduce_scatter x1 -> x0, waiting for transfers between devices: 23.4 us -> none  [per_device(): lax.psum_scatter(summed_scores, 'lane', scatter_dimension=0, tiled=True)]
    pallas_call x0 -> x4, Pallas kernels: none -> 20.5 us  [the longest x1 10.8 us: similar_parts(): pl.pallas_call(functools.partial(similar_kernel, per), grid=(steps,), in_...]
    psum x2 -> x0, blocking collectives: 14.9 us -> none  [the longest x1 8.9 us: per_device(): similar = lax.psum(partial_dots, 'lane') / D]
    gather x4 -> x0, local copies, waits for them, and re-layouts: 13.8 us -> none  [the longest x2 8.08 us: pick_rows(): located = jnp.take(descriptors, jnp.maximum(wanted, 0) // 2, axis=0)]
  transfers between devices with their start and end apart: 5 -> 8, of which waited for: 4 -> 8; matrix products, arithmetic and copies ran while one was open for 6% -> 4% of each run, Pallas kernels for 0% -> 2%
where the time goes in v1:
time: 219 us; the launch traced here: 218 us
  waiting for transfers between devices  81.5 us (37%)
  starting transfers between devices  49.6 us (23%)
  blocking collectives  35.5 us (16%)
  Pallas kernels  20.5 us (9%)
  between operations  14.3 us (7%)
  local copies, waits for them, and re-layouts  12.9 us (6%)
  other arithmetic  3.13 us (1%)
    all_to_all x7, waiting for transfers between devices, exchange(): return lax.all_to_all(parts, axis, split_axis=0, concat_axis=0, tiled=True)  50.3 us
    all_to_all x7, starting transfers between devices, exchange(): return lax.all_to_all(parts, axis, split_axis=0, concat_axis=0, tiled=True)  49.6 us
    all_to_all x3, blocking collectives, exchange(): return lax.all_to_all(parts, axis, split_axis=0, concat_axis=0, tiled=True)  35.5 us
    all_gather x1, waiting for transfers between devices, per_device(): everything = lax.all_gather(own, ('z', 'core'), axis=0, tiled=True)  31.2 us
    pallas_call x1, Pallas kernels, similar_parts(): pl.pallas_call(functools.partial(similar_kernel, per), grid=(steps,), in_...  10.8 us
    unnamed x11, local copies, waits for them, and re-layouts  6.58 us
  transfers between devices with their start and end apart: 8, of which 8 were waited for; matrix products, arithmetic and copies ran while one was open for 4% of the time, Pallas kernels for 2%

profile of v1, /device:TPU:1, one launch (start us, length us, event | category | flops | bytes accessed | tf_op | source)
XLA Modules:
  0.0 218.0 jit_solution(10672570431765189187)
XLA Ops:
  7.2 0.0 copy-start
  7.2 0.0 all-gather.2.cloned.1.call-start
  7.2 1.0 bitcast_bitcast_fusion
  8.2 9.7 %all_to_all.50 = bf16[4,128,128]{2,1,0:T(8,128)(2,1)} all-to-all(bf16[4,128,128]{2,1,0:T(8,128)(2,1)S(1)} %bitcast_bitcast_fusion), channel_id=1, replica_groups=mesh['y'=4,'z'=16,'core'=2,'x'=4] {'y'}, dimensions={0} | all-to-all | bytes 262144 | tf_op jit(solution)/shard_map/all_to_all | solution.py:28
  18.0 0.0 copy-start.3
  18.0 0.0 all-gather.2.cloned.1.call-update
  18.0 0.8 copy.73.listed_ref
  18.8 0.8 copy.74.owned_ref
  19.6 3.8 %slot_table.1 = s32[16,128]{1,0:T(8,128)} custom-call(s32[128,10]{1,0:T(8,128)S(1)} %copy.73.listed_ref, s32[128,10]{1,0:T(8,128)S(1)} %copy.74.owned_ref), custom_call_target="tpu_custom_call" | custom-call | tf_op jit(solution)/shard_map/slot_table/pallas_call | solution.py:73
  23.5 14.9 %all-to-all-start.1 = ((s32[16,1,128]{2,1,0:T(1,128)}), s32[16,1,128]{2,1,0:T(1,128)S(1)}, u32[]{:S(2)}, u32[]{:S(2)}) async-start(s32[16,1,128]{2,1,0:T(1,128)} %bitcast.4), calls=%async_computation.1 | async-start | bytes 16384 | tf_op jit(solution)/shard_map/all_to_all | solution.py:28
  38.4 0.8 copy.84
  39.2 0.1 eq.63
  39.4 10.3 %all-to-all-done.1 = s32[16,1,128]{2,1,0:T(1,128)S(1)} async-done(((s32[16,1,128]{2,1,0:T(1,128)}), s32[16,1,128]{2,1,0:T(1,128)S(1)}, u32[]{:S(2)}, u32[]{:S(2)}) %all-to-all-start.1) | async-done | bytes 8224 | tf_op jit(solution)/shard_map/all_to_all | solution.py:28
  49.7 0.7 pad_add_fusion.2
  50.4 0.7 broadcast_in_dim.20
  51.0 6.7 %all-to-all-start.2 = ((s32[8,2,16,128]{3,2,1,0:T(8,128)}), s32[8,2,16,128]{3,2,1,0:T(8,128)S(1)}, u32[]{:S(2)}, u32[]{:S(2)}) async-start(s32[8,2,16,128]{3,2,1,0:T(8,128)} %broadcast_in_dim.20), calls=%async_computation.2 | async-start | bytes 262144 | tf_op jit(solution)/shard_map/all_to_all | solution.py:28
  57.8 0.7 broadcast_compare_fusion
  58.5 4.6 %all-to-all-done.2 = s32[8,2,16,128]{3,2,1,0:T(8,128)S(1)} async-done(((s32[8,2,16,128]{3,2,1,0:T(8,128)}), s32[8,2,16,128]{3,2,1,0:T(8,128)S(1)}, u32[]{:S(2)}, u32[]{:S(2)}) %all-to-all-start.2) | async-done | bytes 131104 | tf_op jit(solution)/shard_map/all_to_all | solution.py:28
  63.1 0.1 select_n.57
  63.3 0.1 copy.77
  63.4 0.1 reshape_squeeze.3
  63.5 0.5 select_reduce_fusion
  64.0 0.2 reshape.223
  64.2 0.2 copy.76
  64.4 0.1 copy.78
  64.5 0.1 copy.82.src_ref
  64.6 0.1 select_n.61
  64.7 0.2 reshape.225
  64.9 0.2 copy.79
  65.1 0.2 reshape.213
  65.4 31.2 %all-gather.2.cloned.1.call-done.all_ref = bf16[16384,128]{1,0:T(8,128)(2,1)} async-done(((bf16[512,128]{1,0:T(8,128)(2,1)}), bf16[16384,128]{1,0:T(8,128)(2,1)}) %all-gather.2.cloned.1.call-update) | async-done | bytes 4194320 | tf_op jit(solution)/shard_map/all_gather | solution.py:261
  96.6 0.0 copy-done.3
  96.6 10.8 %similar_parts.1 = (bf16[8,2048,128]{2,1,0:T(8,128)(2,1)S(1)}, f32[128,128]{1,0:T(8,128)}) custom-call(bf16[16384,128]{1,0:T(8,128)(2,1)} %all-gather.2.cloned.1.call-done.all_ref, bf16[512,128]{1,0:T(8,128)(2,1)S(1)} %bitcast.74, s32[128,128]{1,0:T(8,128)S(1)} %copy.82.src_ref, s32[128,128]{1,0:T(8,128)S(1)} %bitcast.76), custom_call_target="tpu_custom_call" | custom-call | tf_op jit(solution)/shard_map/similar_parts/pallas_call | solution.py:116
  107.4 0.0 copy-start.1
  107.4 1.9 copy-done.1
  109.3 6.6 %all-to-all-start.3 = ((f32[16,8,128]{2,1,0:T(8,128)}), f32[16,8,128]{2,1,0:T(8,128)S(1)}, u32[]{:S(2)}, u32[]{:S(2)}) async-start(f32[16,8,128]{2,1,0:T(8,128)} %bitcast.18), calls=%async_computation.3 | async-start | bytes 131072 | tf_op jit(solution)/shard_map/all_to_all | solution.py:28
  115.9 0.2 convert_reduce_fusion
  116.2 0.1 eq.67
  116.3 0.1 copy.85
  116.4 6.0 %all-to-all-done.3 = f32[16,8,128]{2,1,0:T(8,128)S(1)} async-done(((f32[16,8,128]{2,1,0:T(8,128)}), f32[16,8,128]{2,1,0:T(8,128)S(1)}, u32[]{:S(2)}, u32[]{:S(2)}) %all-to-all-start.3) | async-done | bytes 65568 | tf_op jit(solution)/shard_map/all_to_all | solution.py:28
  122.5 0.6 broadcast_in_dim.23
  123.1 3.5 %all-to-all-start.4 = ((f32[16,8,128]{2,1,0:T(8,128)}), f32[16,8,128]{2,1,0:T(8,128)S(1)}, u32[]{:S(2)}, u32[]{:S(2)}) async-start(f32[16,8,128]{2,1,0:T(8,128)} %broadcast_in_dim.23), calls=%async_computation.4 | async-start | bytes 131072 | tf_op jit(solution)/shard_map/all_to_all | solution.py:28
  126.6 6.4 %all-to-all-done.4 = f32[16,8,128]{2,1,0:T(8,128)S(1)} async-done(((f32[16,8,128]{2,1,0:T(8,128)}), f32[16,8,128]{2,1,0:T(8,128)S(1)}, u32[]{:S(2)}, u32[]{:S(2)}) %all-to-all-start.4) | async-done | bytes 65568 | tf_op jit(solution)/shard_map/all_to_all | solution.py:28
  133.1 0.0 copy-start.2
  133.1 2.2 %copy-done.2 = bf16[8,2048,128]{2,1,0:T(8,128)(2,1)S(1)} copy-done((bf16[8,2048,128]{2,1,0:T(8,128)(2,1)S(1)}, bf16[8,2048,128]{2,1,0:T(8,128)(2,1)}, u32[]{:S(2)}) %copy-start.2) | copy-done | bytes 4194328
  135.2 4.0 %weighted_sum.1 = f32[512,128]{1,0:T(8,128)} custom-call(bf16[8,2048,128]{2,1,0:T(8,128)(2,1)S(1)} %copy-done.2, f32[128,128]{1,0:T(8,128)S(1)} %bitcast.78, bf16[512,128]{1,0:T(8,128)(2,1)S(1)} %bitcast.75, s32[128,128]{1,0:T(8,128)S(1)} %bitcast.77), custom_call_target="tpu_custom_call" | custom-call | tf_op jit(solution)/shard_map/weighted_sum/pallas_call | solution.py:172
  139.2 3.4 %all-to-all-start.5 = ((f32[4,128,128]{2,1,0:T(8,128)}), f32[4,128,128]{2,1,0:T(8,128)S(1)}, u32[]{:S(2)}, u32[]{:S(2)}) async-start(f32[4,128,128]{2,1,0:T(8,128)} %bitcast.20), calls=%async_computation.5 | async-start | bytes 524288 | tf_op jit(solution)/shard_map/all_to_all | solution.py:28
  142.6 0.0 copy-done
  142.6 0.2 convolution_convert_fusion
  142.9 0.6 copy.94
  143.5 4.6 %all-to-all-done.5 = f32[4,128,128]{2,1,0:T(8,128)S(1)} async-done(((f32[4,128,128]{2,1,0:T(8,128)}), f32[4,128,128]{2,1,0:T(8,128)S(1)}, u32[]{:S(2)}, u32[]{:S(2)}) %all-to-all-start.5) | async-done | bytes 262176 | tf_op jit(solution)/shard_map/all_to_all | solution.py:28
  148.1 3.3 %all-to-all-start.6 = ((bf16[4,16,512]{2,1,0:T(8,128)(2,1)}), bf16[4,16,512]{2,1,0:T(8,128)(2,1)S(1)}, u32[]{:S(2)}, u32[]{:S(2)}) async-start(bf16[4,16,512]{2,1,0:T(8,128)(2,1)} %bitcast.70), calls=%async_computation.6 | async-start | bytes 131072 | tf_op jit(solution)/shard_map/all_to_all | solution.py:28
  151.4 0.1 multiply_reduce_fusion
  151.5 0.2 copy.83
  151.7 0.1 reshape.226
  151.8 4.0 %all-to-all-done.6 = bf16[4,16,512]{2,1,0:T(8,128)(2,1)S(1)} async-done(((bf16[4,16,512]{2,1,0:T(8,128)(2,1)}), bf16[4,16,512]{2,1,0:T(8,128)(2,1)S(1)}, u32[]{:S(2)}, u32[]{:S(2)}) %all-to-all-start.6) | async-done | bytes 65568 | tf_op jit(solution)/shard_map/all_to_all | solution.py:28
  155.8 0.3 fusion.11
  156.1 6.7 %all_to_all.51 = f32[4,24,128]{2,1,0:T(8,128)S(1)} all-to-all(f32[4,24,128]{2,1,0:T(8,128)S(1)} %pad_maximum_fusion), channel_id=1, replica_groups=mesh['y'=4,'z'=16,'core'=2,'x'=4] {'x'}, dimensions={0} | all-to-all | bytes 98304 | tf_op jit(solution)/shard_map/all_to_all | solution.py:28
  162.9 19.0 %all_to_all.52 = f32[16,16,128]{2,1,0:T(8,128)S(1)} all-to-all(f32[16,16,128]{2,1,0:T(8,128)S(1)} %broadcast_in_dim.25), channel_id=1, replica_groups=mesh['y'=4,'z'=16,'core'=2,'x'=4] {'z'}, dimensions={0} | all-to-all | bytes 262144 | tf_op jit(solution)/shard_map/all_to_all | solution.py:28
  182.0 1.1 broadcast_in_dim.26
  183.0 11.1 %all-to-all-start.9 = ((f32[8,16,16,128]{3,2,1,0:T(8,128)}), f32[8,16,16,128]{3,2,1,0:T(8,128)S(1)}, u32[]{:S(2)}, u32[]{:S(2)}) async-start(f32[8,16,16,128]{3,2,1,0:T(8,128)} %broadcast_in_dim.26), calls=%async_computation.9 | async-start | bytes 2097152 | tf_op jit(solution)/shard_map/all_to_all | solution.py:28
  194.2 0.7 fusion.1
  195.0 14.4 %all-to-all-done.9 = f32[8,16,16,128]{3,2,1,0:T(8,128)S(1)} async-done(((f32[8,16,16,128]{3,2,1,0:T(8,128)}), f32[8,16,16,128]{3,2,1,0:T(8,128)S(1)}, u32[]{:S(2)}, u32[]{:S(2)}) %all-to-all-start.9) | async-done | bytes 1048608 | tf_op jit(solution)/shard_map/all_to_all | solution.py:28
  209.3 1.9 pick_scores.1
  (16 shorter events, 0.2 us)
Async XLA Ops:
  7.2 135.5 %copy-start = (bf16[256,2048]{1,0:T(8,128)(2,1)S(1)}, bf16[256,2048]{1,0:T(8,128)(2,1)}, u32[]{:S(2)}) copy-start(bf16[256,2048]{1,0:T(8,128)(2,1)} %param.8) | copy-start | bytes 3145732
  7.2 89.4 %all-gather.2.cloned.1.call-start = ((), (), s32[]{:S(2)}) async-start(), calls=%async_computation.10 | async-start | bytes 4325376 | tf_op jit(solution)/shard_map/all_gather | solution.py:261
  18.0 78.6 %copy-start.3 = (bf16[4,128,128]{2,1,0:T(8,128)(2,1)S(1)}, bf16[4,128,128]{2,1,0:T(8,128)(2,1)}, u32[]{:S(2)}) copy-start(bf16[4,128,128]{2,1,0:T(8,128)(2,1)} %all_to_all.50) | copy-start | bytes 393220
  23.5 26.2 %all-to-all-start.1 = ((s32[16,1,128]{2,1,0:T(1,128)}), s32[16,1,128]{2,1,0:T(1,128)S(1)}, u32[]{:S(2)}, u32[]{:S(2)}) async-start(s32[16,1,128]{2,1,0:T(1,128)} %bitcast.4), calls=%async_computation.1 | async-start | bytes 16384 | tf_op jit(solution)/shard_map/all_to_all | solution.py:28
  51.0 12.0 %all-to-all-start.2 = ((s32[8,2,16,128]{3,2,1,0:T(8,128)}), s32[8,2,16,128]{3,2,1,0:T(8,128)S(1)}, u32[]{:S(2)}, u32[]{:S(2)}) async-start(s32[8,2,16,128]{3,2,1,0:T(8,128)} %broadcast_in_dim.20), calls=%async_computation.2 | async-start | bytes 262144 | tf_op jit(solution)/shard_map/all_to_all | solution.py:28
  107.4 1.9 copy-start.1
  109.3 13.1 %all-to-all-start.3 = ((f32[16,8,128]{2,1,0:T(8,128)}), f32[16,8,128]{2,1,0:T(8,128)S(1)}, u32[]{:S(2)}, u32[]{:S(2)}) async-start(f32[16,8,128]{2,1,0:T(8,128)} %bitcast.18), calls=%async_computation.3 | async-start | bytes 131072 | tf_op jit(solution)/shard_map/all_to_all | solution.py:28
  123.1 10.0 %all-to-all-start.4 = ((f32[16,8,128]{2,1,0:T(8,128)}), f32[16,8,128]{2,1,0:T(8,128)S(1)}, u32[]{:S(2)}, u32[]{:S(2)}) async-start(f32[16,8,128]{2,1,0:T(8,128)} %broadcast_in_dim.23), calls=%async_computation.4 | async-start | bytes 131072 | tf_op jit(solution)/shard_map/all_to_all | solution.py:28
  133.1 2.2 %copy-start.2 = (bf16[8,2048,128]{2,1,0:T(8,128)(2,1)S(1)}, bf16[8,2048,128]{2,1,0:T(8,128)(2,1)}, u32[]{:S(2)}) copy-start(bf16[8,2048,128]{2,1,0:T(8,128)(2,1)} %copy-done.1) | copy-start | bytes 12582916
  139.2 8.9 %all-to-all-start.5 = ((f32[4,128,128]{2,1,0:T(8,128)}), f32[4,128,128]{2,1,0:T(8,128)S(1)}, u32[]{:S(2)}, u32[]{:S(2)}) async-start(f32[4,128,128]{2,1,0:T(8,128)} %bitcast.20), calls=%async_computation.5 | async-start | bytes 524288 | tf_op jit(solution)/shard_map/all_to_all | solution.py:28
  148.1 7.7 %all-to-all-start.6 = ((bf16[4,16,512]{2,1,0:T(8,128)(2,1)}), bf16[4,16,512]{2,1,0:T(8,128)(2,1)S(1)}, u32[]{:S(2)}, u32[]{:S(2)}) async-start(bf16[4,16,512]{2,1,0:T(8,128)(2,1)} %bitcast.70), calls=%async_computation.6 | async-start | bytes 131072 | tf_op jit(solution)/shard_map/all_to_all | solution.py:28
  183.0 26.3 %all-to-all-start.9 = ((f32[8,16,16,128]{3,2,1,0:T(8,128)}), f32[8,16,16,128]{3,2,1,0:T(8,128)S(1)}, u32[]{:S(2)}, u32[]{:S(2)}) async-start(f32[8,16,16,128]{3,2,1,0:T(8,128)} %broadcast_in_dim.26), calls=%async_computation.9 | async-start | bytes 2097152 | tf_op jit(solution)/shard_map/all_to_all | solution.py:28
Sparse Core Ops, SparseCore 0:
  18.1 78.3 all-gather.1

commit v2 on v1

v2 whole, which is shorter than its diff:
```python
import functools
import math

import jax
import jax.numpy as jnp
from jax import lax
from jax.experimental import pallas as pl
from jax.experimental.pallas import tpu as pltpu
from jax.sharding import Mesh
from jax.sharding import PartitionSpec as P

D = 2048
BLOCK = 128
PLACES = 16
GROUP = 8
CORES = 2
LANES = 128
VMEM = 48 * 1024 * 1024
INTERPRET = False
STEPS = 4
HBM = pltpu.HBM
f32 = jnp.float32
bf16 = jnp.bfloat16
i32 = jnp.int32
NT = (((1,), (1,)), ((), ()))
TN = (((0,), (0,)), ((), ()))


def exchange(parts, axis):
    return lax.all_to_all(parts, axis, split_axis=0, concat_axis=0, tiled=True)


def spread(part, axis, count):
    return exchange(jnp.broadcast_to(part[None], (count,) + part.shape), axis)


def hbm(shape, dtype):
    return jax.ShapeDtypeStruct(shape, dtype) if INTERPRET else pltpu.HBM(shape, dtype)


def params(**more):
    return pltpu.CompilerParams(vmem_limit_bytes=VMEM, **more)


def table_kernel(listed_ref, owned_ref, table_ref):
    rows = listed_ref.shape[0]
    row = lax.broadcasted_iota(i32, (rows, LANES), 0)
    lane = lax.broadcasted_iota(i32, (rows, LANES), 1)
    lower = (row > lane).astype(bf16)
    own_mark = (row + 1).astype(f32)
    before = jnp.zeros((1, LANES), f32)
    high = jnp.zeros((LANES, LANES), f32)
    low = jnp.zeros((LANES, LANES), f32)
    for slot in range(listed_ref.shape[1]):
        listed = listed_ref[:, slot : slot + 1]
        shard = lax.shift_right_logical(listed, 7)
        match = lane == shard
        ones = jnp.where(match, 1.0, 0.0)
        counted = jnp.dot(lower, ones.astype(bf16), preferred_element_type=f32) + before
        before = before + jnp.sum(ones, axis=0, keepdims=True)
        rank = jnp.sum(jnp.where(match, counted, 0.0), axis=1, keepdims=True).astype(i32)
        left = jnp.where(lane == lax.shift_right_logical(shard, 3), 1.0, 0.0).astype(bf16)
        here = lane == (shard & (GROUP - 1)) * PLACES + rank
        source = ((listed & (BLOCK - 1)) * 2 + owned_ref[:, slot : slot + 1]).astype(f32)
        high += lax.dot_general(left, jnp.where(here, own_mark, 0.0).astype(bf16), TN, preferred_element_type=f32)
        low += lax.dot_general(left, jnp.where(here, source, 0.0).astype(bf16), TN, preferred_element_type=f32)
    count = table_ref.shape[0]
    high = high[:count].astype(i32)
    low = low[:count].astype(i32)
    table_ref[...] = jnp.where(high > 0, (high - 1) * 256 + low, -1)


def build_table(neighbours, owned, shards):
    return pl.pallas_call(
        table_kernel,
        out_shape=jax.ShapeDtypeStruct((shards // GROUP, LANES), i32),
        compiler_params=params(),
        interpret=INTERPRET,
        name="slot_table",
    )(neighbours, owned)


def similar_kernel(groups, all_ref, own_ref, src_ref, at_ref, got_ref, sims_ref):
    row = lax.broadcasted_iota(i32, (BLOCK, LANES), 0)
    shards = own_ref.shape[0] // BLOCK
    for group in range(groups):
        parts = []
        for one in range(group * GROUP, (group + 1) * GROUP):
            pick = jnp.where(row == src_ref[one : one + 1, :], 1.0, 0.0).astype(bf16)
            block = all_ref[one * BLOCK : (one + 1) * BLOCK, :]
            parts.append(lax.dot_general(pick, block, TN, preferred_element_type=f32).astype(bf16))
        sims = []
        for shard in range(shards):
            chunks = []
            for k in (2 * shard, 2 * shard + 1):
                chunk = jnp.concatenate([part[k * PLACES : (k + 1) * PLACES] for part in parts], axis=0)
                got_ref[k, group * LANES : (group + 1) * LANES, :] = chunk
                chunks.append(chunk)
            own = own_ref[shard * BLOCK : (shard + 1) * BLOCK, :]
            dots = lax.dot_general(own, jnp.concatenate(chunks, axis=0), NT, preferred_element_type=f32)
            for kind in range(2):
                n = group * GROUP + 2 * shard + kind
                held = jnp.where(row == at_ref[n : n + 1, :], dots[:, kind * LANES : (kind + 1) * LANES], 0.0)
                sims.append(jnp.sum(held, axis=0, keepdims=True))
        sims_ref[group * GROUP : (group + 1) * GROUP, :] = jnp.concatenate(sims, axis=0)


def similar_parts(everything, own, source, at, steps=STEPS):
    width = own.shape[1]
    groups = everything.shape[0] // BLOCK // GROUP
    per = max(groups // steps, 1)
    kinds = 2 * own.shape[0] // BLOCK
    return pl.pallas_call(
        functools.partial(similar_kernel, per),
        grid=(groups // per,),
        in_specs=[
            pl.BlockSpec((per * GROUP * BLOCK, width), lambda i: (i, 0)),
            pl.BlockSpec(own.shape, lambda i: (0, 0)),
            pl.BlockSpec((per * GROUP, LANES), lambda i: (i, 0)),
            pl.BlockSpec((per * GROUP, LANES), lambda i: (i, 0)),
        ],
        out_specs=[
            pl.BlockSpec((kinds, per * LANES, width), lambda i: (0, i, 0)),
            pl.BlockSpec((per * GROUP, LANES), lambda i: (i, 0)),
        ],
        out_shape=[
            hbm((kinds, groups * LANES, width), bf16),
            jax.ShapeDtypeStruct((groups * GROUP, LANES), f32),
        ],
        compiler_params=params(),
        interpret=INTERPRET,
        name="similar_parts",
    )(everything, own, source, at)


def sum_kernel(got_ref, sims_ref, at_ref, sum_ref, held_ref, sems):
    shards = sum_ref.shape[0]
    copies = []
    for shard in range(shards):
        pair = slice(2 * shard, 2 * shard + 2)
        copies.append(pltpu.make_async_copy(got_ref.at[pair], held_ref.at[pair], sems.at[shard]))
        copies[-1].start()
    row = lax.broadcasted_iota(i32, (BLOCK, LANES), 0)
    similar = jnp.sum(sims_ref[...], axis=0) / D
    weight = similar * similar * similar
    high = weight.astype(bf16).astype(f32)
    low = weight - high
    groups = at_ref.shape[0] // GROUP
    for shard in range(shards):
        left_high, left_low = [], []
        for k in (2 * shard, 2 * shard + 1):
            for group in range(groups):
                n = group * GROUP + k
                here = row == at_ref[n : n + 1, :]
                left_high.append(jnp.where(here, high[n : n + 1], 0.0).astype(bf16))
                left_low.append(jnp.where(here, low[n : n + 1], 0.0).astype(bf16))
        copies[shard].wait()
        right = jnp.concatenate([held_ref[2 * shard], held_ref[2 * shard + 1]], axis=0)
        total = jnp.dot(jnp.concatenate(left_high, axis=1), right, preferred_element_type=f32)
        total += jnp.dot(jnp.concatenate(left_low, axis=1), right, preferred_element_type=f32)
        sum_ref[shard] = total


def weighted_sums(got, sims, at):
    kinds, slots, width = got.shape
    vmem = pl.BlockSpec(memory_space=pltpu.VMEM)
    return pl.pallas_call(
        sum_kernel,
        in_specs=[pl.BlockSpec(memory_space=HBM), vmem, vmem],
        out_specs=vmem,
        out_shape=jax.ShapeDtypeStruct((kinds // 2, BLOCK, width), f32),
        scratch_shapes=[pltpu.VMEM(got.shape, bf16), pltpu.SemaphoreType.DMA((kinds // 2,))],
        compiler_params=params(),
        interpret=INTERPRET,
        name="weighted_sums",
    )(got, sims, at)


def score_kernel(parts_ref, own_ref, chosen_ref, sum_ref, out_ref):
    total = own_ref[...].astype(f32)
    for part in range(parts_ref.shape[0]):
        total += parts_ref[part]
    sum_ref[...] = total
    energy = jnp.sum(total * total, axis=1, keepdims=True)
    energy = jnp.broadcast_to(energy, (BLOCK, LANES)).T[:8]
    high = total.astype(bf16)
    low = (total - high.astype(f32)).astype(bf16)
    chosen = chosen_ref[...]
    scores = lax.dot_general(chosen, high, NT, preferred_element_type=f32)
    scores += lax.dot_general(chosen, low, NT, preferred_element_type=f32)
    for lane in range(out_ref.shape[0]):
        out_ref[lane, :PLACES, :] = scores[lane * PLACES : (lane + 1) * PLACES]
        out_ref[lane, PLACES:, :] = energy


def score_parts(parts, own, chosen, xs):
    return pl.pallas_call(
        score_kernel,
        out_shape=[
            jax.ShapeDtypeStruct(own.shape, f32),
            jax.ShapeDtypeStruct((xs, PLACES + 8, LANES), f32),
        ],
        compiler_params=params(),
        interpret=INTERPRET,
        name="score_parts",
    )(parts, own, chosen)


def pick_kernel(rows_ref, near_ref, far_ref, out_ref):
    count = near_ref.shape[0]

    def step(i, carry):
        for cand in range(2):
            picked = []
            for one in range(GROUP):
                r = rows_ref[i * (2 * GROUP) + 2 * one + cand]
                near = near_ref[pl.ds(lax.rem(r, count), 1), :]
                far = far_ref[pl.ds(lax.rem(r, count), 1), :]
                picked.append(jnp.where(r < count, near, far))
            at = pl.ds(pl.multiple_of(i * GROUP, GROUP), GROUP)
            out_ref[at, cand * LANES : (cand + 1) * LANES] = jnp.concatenate(picked, axis=0)
        return carry

    lax.fori_loop(0, out_ref.shape[0] // GROUP, step, 0)


def pick_scores(rows, near, far):
    queries = rows.shape[0] // 2
    vmem = pl.BlockSpec(memory_space=pltpu.VMEM)
    return pl.pallas_call(
        pick_kernel,
        in_specs=[pl.BlockSpec(memory_space=pltpu.SMEM), vmem, vmem],
        out_specs=vmem,
        out_shape=jax.ShapeDtypeStruct((queries, 2 * LANES), f32),
        compiler_params=params(),
        interpret=INTERPRET,
        name="pick_scores",
    )(rows, near, far)


def slot_orders(table, ys, zs):
    count = zs * CORES
    groups = count // GROUP
    ahead = exchange(table.reshape(ys, groups, LANES), "y")
    back = table.reshape(ys, count, PLACES).transpose(1, 0, 2).reshape(count, 1, ys * PLACES)
    back = exchange(back, ("z", "core")).reshape(count, ys, PLACES)
    ahead_own = jnp.where(ahead >= 0, lax.shift_right_logical(ahead, 8), -1)
    ahead_src = jnp.where(ahead >= 0, lax.shift_right_logical(ahead, 1) & (BLOCK - 1), -1)
    held = (back >= 0) & ((back & 1) == 1)
    back_src = jnp.where(held, lax.shift_right_logical(back, 8), -1)
    back_own = jnp.where(held, lax.shift_right_logical(back, 1) & (BLOCK - 1), -1)
    source = jnp.stack([ahead_src.reshape(ys, count, PLACES).transpose(1, 0, 2), back_src], axis=2)
    at = jnp.stack([ahead_own, back_own.transpose(1, 0, 2).reshape(ys, groups, LANES)], axis=1)
    at = at.reshape(2 * ys, groups, LANES).transpose(1, 0, 2).reshape(groups * GROUP, LANES)
    return source.reshape(count, LANES), at


def query_entries(queries, candidates, xs, zs):
    flat = candidates.reshape(-1)
    order = jnp.arange(flat.shape[0], dtype=i32)
    earlier = (flat[:, None] == flat[None, :]) & (order[:, None] > order[None, :])
    rank = jnp.sum(earlier.astype(i32), axis=1)
    here = lax.axis_index(("y", "z", "core"))
    hits = (flat == here)[None, :] & (rank[None, :] == jnp.arange(PLACES, dtype=i32)[:, None])
    hits = jnp.sum(hits.reshape(PLACES, -1, 2).astype(f32), axis=2).astype(bf16)
    chosen = jnp.dot(hits, queries, preferred_element_type=f32).astype(bf16)
    chosen = chosen.reshape(PLACES, xs, -1).transpose(1, 0, 2)
    chosen = exchange(chosen, "x").reshape(xs * PLACES, -1)
    plane = flat // CORES
    core = flat - plane * CORES
    far = (core != lax.axis_index("core")).astype(i32)
    rows = (far * (GROUP // CORES * zs) + plane) * PLACES + rank
    return chosen, rows


def per_device(descriptors, neighbours, owned, queries, candidates):
    ys, zs, xs = lax.axis_size("y"), lax.axis_size("z"), lax.axis_size("x")
    rows, width = descriptors.shape
    everything = lax.all_gather(descriptors, ("z", "core"), axis=0, tiled=True)
    table = build_table(neighbours, owned, ys * zs * CORES)
    source, at = slot_orders(table, ys, zs)
    own = spread(descriptors, "y", ys).reshape(ys * rows, width)
    chosen, score_rows = query_entries(queries, candidates, xs, zs)
    source, at, own, chosen, score_rows = lax.optimization_barrier((source, at, own, chosen, score_rows))
    got, sims = similar_parts(everything, own, source, at)
    sims = spread(sims, "x", xs)
    parts = exchange(weighted_sums(got, sims, at), "y")
    summed, parts = score_parts(parts, descriptors, chosen, xs)
    whole = jnp.sum(exchange(parts, "x"), axis=0)
    scale = lax.rsqrt(whole[PLACES] / (xs * width) + 1e-06)
    augmented = (summed * scale[:, None]).astype(bf16)
    mine = whole[:PLACES] * (scale / math.sqrt(xs * width))[None, :]
    near = spread(spread(mine, "z", zs), "y", ys).reshape(-1, rows)
    far = lax.ppermute(near, "core", [(0, 1), (1, 0)])
    return augmented, pick_scores(score_rows, near, far)


def solution(mesh):
    shards, lanes = mesh.devices.shape
    ys = GROUP // CORES
    split = Mesh(mesh.devices.reshape(ys, shards // GROUP, CORES, lanes), ("y", "z", "core", "x"))
    shard = ("y", "z", "core")
    return jax.shard_map(
        per_device,
        mesh=split,
        in_specs=(P(shard, "x"), P(shard, None), P(shard, None), P("x", None), P("x", None)),
        out_specs=(P(shard, "x"), P("x", None)),
        check_vma=False,
    )
```

time: 219 us -> 184 us (0.84)
  waiting for transfers between devices: 81.5 us -> 41.4 us
  blocking collectives: 35.5 us -> 61 us
  starting transfers between devices: 49.6 us -> 38.4 us
  Pallas kernels: 20.5 us -> 14.2 us
    all_to_all x7 -> x4, waiting for transfers between devices: 50.3 us -> 22.1 us  [exchange(): return lax.all_to_all(parts, axis, split_axis=0, concat_axis=0, tiled=True)]
    all_to_all x3 -> x5, blocking collectives: 35.5 us -> 61 us  [exchange(): return lax.all_to_all(parts, axis, split_axis=0, concat_axis=0, tiled=True)]
    all_to_all x7 -> x4, starting transfers between devices: 49.6 us -> 29.8 us  [exchange(): return lax.all_to_all(parts, axis, split_axis=0, concat_axis=0, tiled=True)]
    all_gather x1, waiting for transfers between devices: 31.2 us -> 17.8 us  [per_device(): everything = lax.all_gather(descriptors, ('z', 'core'), axis=0, tiled=True)]
    ppermute x0 -> x1, starting transfers between devices: none -> 8.54 us  [per_device(): far = lax.ppermute(near, 'core', [(0, 1), (1, 0)])]
    pallas_call x3 -> x4, Pallas kernels: 18.6 us -> 11 us  [the longest x1 4.71 us: similar_parts(): pl.pallas_call(functools.partial(similar_kernel, per), grid=(groups // pe...]
  transfers between devices with their start and end apart: 8 -> 6, of which waited for: 8 -> 6; matrix products, arithmetic and copies ran while one was open for 4% -> 5% of each run, Pallas kernels for 2% -> 2%
where the time goes in v2:
time: 184 us; the launch traced here: 183 us
  blocking collectives  61 us (33%)
  waiting for transfers between devices  41.4 us (22%)
  starting transfers between devices  38.4 us (21%)
  Pallas kernels  14.2 us (8%)
  between operations  14.2 us (8%)
  local copies, waits for them, and re-layouts  11.7 us (6%)
    all_to_all x5, blocking collectives, exchange(): return lax.all_to_all(parts, axis, split_axis=0, concat_axis=0, tiled=True)  61 us
    all_to_all x4, starting transfers between devices, exchange(): return lax.all_to_all(parts, axis, split_axis=0, concat_axis=0, tiled=True)  29.8 us
    all_to_all x4, waiting for transfers between devices, exchange(): return lax.all_to_all(parts, axis, split_axis=0, concat_axis=0, tiled=True)  22.1 us
    all_gather x1, waiting for transfers between devices, per_device(): everything = lax.all_gather(descriptors, ('z', 'core'), axis=0, tiled=True)  17.8 us
    ppermute x1, starting transfers between devices, per_device(): far = lax.ppermute(near, 'core', [(0, 1), (1, 0)])  8.54 us
    unnamed x11, local copies, waits for them, and re-layouts  6.8 us
    pallas_call x1, Pallas kernels, similar_parts(): pl.pallas_call(functools.partial(similar_kernel, per), grid=(groups // pe...  4.71 us
    pallas_call x1, Pallas kernels, build_table(): pl.pallas_call(table_kernel, out_shape=jax.ShapeDtypeStruct((shards // GR...  3.8 us
  transfers between devices with their start and end apart: 6, of which 6 were waited for; matrix products, arithmetic and copies ran while one was open for 5% of the time, Pallas kernels for 2%

profile of v2, /device:TPU:1, one launch (start us, length us, event | category | flops | bytes accessed | tf_op | source)
XLA Modules:
  0.0 183.0 jit_solution(10327534786214201610)
XLA Ops:
  7.2 0.0 copy-start
  7.2 0.0 all-gather.2.cloned.1.call-start
  7.2 0.7 all-gather.2.cloned.1.call-update
  7.9 0.8 copy.50.listed_ref
  8.7 0.8 copy.51.owned_ref
  9.5 3.8 %slot_table.1 = s32[16,128]{1,0:T(8,128)} custom-call(s32[128,10]{1,0:T(8,128)S(1)} %copy.50.listed_ref, s32[128,10]{1,0:T(8,128)S(1)} %copy.51.owned_ref), custom_call_target="tpu_custom_call" | custom-call | tf_op jit(solution)/shard_map/slot_table/pallas_call | solution.py:74
  13.3 5.0 %all-to-all-start = ((s32[4,4,128]{2,1,0:T(4,128)}), s32[4,4,128]{2,1,0:T(4,128)S(1)}, u32[]{:S(2)}, u32[]{:S(2)}) async-start(s32[4,4,128]{2,1,0:T(4,128)} %bitcast), calls=%async_computation | async-start | bytes 16384 | tf_op jit(solution)/shard_map/all_to_all | solution.py:30
  18.3 0.8 copy.62
  19.1 0.1 eq.56
  19.3 0.3 convert_reduce_fusion
  19.6 0.1 eq.60
  19.7 0.1 copy.63
  19.8 0.7 broadcast_compare_fusion.1
  20.5 0.0 copy-done
  20.5 0.2 convolution_convert_fusion
  20.8 0.8 reshape.139
  21.5 0.1 copy.52
  21.6 0.7 copy.53
  22.3 0.2 all-to-all-done
  22.5 17.3 %all-to-all-start.1 = ((s32[32,1,64]{2,1,0:T(1,128)}), s32[32,1,64]{2,1,0:T(1,128)S(1)}, u32[]{:S(2)}, u32[]{:S(2)}) async-start(s32[32,1,64]{2,1,0:T(1,128)} %copy.53), calls=%async_computation.1 | async-start | bytes 32768 | tf_op jit(solution)/shard_map/all_to_all | solution.py:30
  39.9 0.6 copy.68
  40.5 11.1 %all-to-all-done.1 = s32[32,1,64]{2,1,0:T(1,128)S(1)} async-done(((s32[32,1,64]{2,1,0:T(1,128)}), s32[32,1,64]{2,1,0:T(1,128)S(1)}, u32[]{:S(2)}, u32[]{:S(2)}) %all-to-all-start.1) | async-done | bytes 8224 | tf_op jit(solution)/shard_map/all_to_all | solution.py:30
  51.6 4.0 %all-to-all-start.3 = ((bf16[4,16,512]{2,1,0:T(8,128)(2,1)}), bf16[4,16,512]{2,1,0:T(8,128)(2,1)S(1)}, u32[]{:S(2)}, u32[]{:S(2)}) async-start(bf16[4,16,512]{2,1,0:T(8,128)(2,1)} %bitcast.33), calls=%async_computation.3 | async-start | bytes 131072 | tf_op jit(solution)/shard_map/all_to_all | solution.py:30
  55.6 0.1 reshape.138
  55.7 0.1 copy.54
  55.8 4.3 %all-to-all-done.3 = bf16[4,16,512]{2,1,0:T(8,128)(2,1)S(1)} async-done(((bf16[4,16,512]{2,1,0:T(8,128)(2,1)}), bf16[4,16,512]{2,1,0:T(8,128)(2,1)S(1)}, u32[]{:S(2)}, u32[]{:S(2)}) %all-to-all-start.3) | async-done | bytes 65568 | tf_op jit(solution)/shard_map/all_to_all | solution.py:30
  60.1 1.7 broadcast_in_dim.20
  61.8 3.5 %all-to-all-start.2 = ((bf16[4,128,512]{2,1,0:T(8,128)(2,1)}), bf16[4,128,512]{2,1,0:T(8,128)(2,1)S(1)}, u32[]{:S(2)}, u32[]{:S(2)}) async-start(bf16[4,128,512]{2,1,0:T(8,128)(2,1)} %broadcast_in_dim.20), calls=%async_computation.2 | async-start | bytes 1048576 | tf_op jit(solution)/shard_map/all_to_all | solution.py:30
  65.3 0.1 copy.57
  65.4 0.1 copy.58
  65.5 0.1 copy.60
  65.6 0.1 stack_reshape.3
  65.7 6.5 %all-to-all-done.2 = bf16[4,128,512]{2,1,0:T(8,128)(2,1)S(1)} async-done(((bf16[4,128,512]{2,1,0:T(8,128)(2,1)}), bf16[4,128,512]{2,1,0:T(8,128)(2,1)S(1)}, u32[]{:S(2)}, u32[]{:S(2)}) %all-to-all-start.2) | async-done | bytes 524320 | tf_op jit(solution)/shard_map/all_to_all | solution.py:30
  72.3 0.1 copy.65.src_ref
  72.3 17.8 %all-gather.2.cloned.1.call-done.all_ref = bf16[4096,512]{1,0:T(8,128)(2,1)} async-done(((bf16[128,512]{1,0:T(8,128)(2,1)}), bf16[4096,512]{1,0:T(8,128)(2,1)}) %all-gather.2.cloned.1.call-update) | async-done | bytes 4194320 | tf_op jit(solution)/shard_map/all_gather | solution.py:279
  90.2 0.0 copy-start.1
  90.2 2.2 %copy-done.1 = bf16[4096,512]{1,0:T(8,128)(2,1)S(1)} copy-done((bf16[4096,512]{1,0:T(8,128)(2,1)S(1)}, bf16[4096,512]{1,0:T(8,128)(2,1)}, u32[]{:S(2)}) %copy-start.1) | copy-done | bytes 4194328
  92.3 4.7 %similar_parts.1 = (bf16[8,512,512]{2,1,0:T(8,128)(2,1)}, f32[32,128]{1,0:T(8,128)S(1)}) custom-call(bf16[4096,512]{1,0:T(8,128)(2,1)S(1)} %copy-done.1, bf16[512,512]{1,0:T(8,128)(2,1)S(1)} %bitcast.34, s32[32,128]{1,0:T(8,128)S(1)} %copy.65.src_ref, s32[32,128]{1,0:T(8,128)S(1)} %bitcast.38), custom_call_target="tpu_custom_call" | custom-call | tf_op jit(solution)/shard_map/similar_parts/pallas_call | solution.py:113
  97.1 0.0 copy-start.3
  97.1 8.9 %all_to_all.45.sims_ref = f32[4,32,128]{2,1,0:T(8,128)S(1)} all-to-all(f32[4,32,128]{2,1,0:T(8,128)S(1)} %broadcast_in_dim.21), channel_id=1, replica_groups=mesh['y'=4,'z'=16,'core'=2,'x'=4] {'x'}, dimensions={0} | all-to-all | bytes 131072 | tf_op jit(solution)/shard_map/all_to_all | solution.py:30
  105.9 0.0 copy-start.2
  105.9 2.2 %copy-done.2 = bf16[8,512,512]{2,1,0:T(8,128)(2,1)S(1)} copy-done((bf16[8,512,512]{2,1,0:T(8,128)(2,1)S(1)}, bf16[8,512,512]{2,1,0:T(8,128)(2,1)}, u32[]{:S(2)}) %copy-start.2) | copy-done | bytes 4194328
  108.1 2.3 %weighted_sums.1 = f32[4,128,512]{2,1,0:T(8,128)S(1)} custom-call(bf16[8,512,512]{2,1,0:T(8,128)(2,1)S(1)} %copy-done.2, f32[4,32,128]{2,1,0:T(8,128)S(1)} %all_to_all.45.sims_ref, s32[32,128]{1,0:T(8,128)S(1)} %bitcast.39), custom_call_target="tpu_custom_call" | custom-call | tf_op jit(solution)/shard_map/weighted_sums/pallas_call | solution.py:167
  110.4 16.0 %all_to_all.46.parts_ref = f32[4,128,512]{2,1,0:T(8,128)S(1)} all-to-all(f32[4,128,512]{2,1,0:T(8,128)S(1)} %weighted_sums.1), channel_id=1, replica_groups=mesh['y'=4,'z'=16,'core'=2,'x'=4] {'y'}, dimensions={0} | all-to-all | bytes 2097152 | tf_op jit(solution)/shard_map/all_to_all | solution.py:30
  126.4 0.0 copy-done.3
  126.5 0.2 score_parts.1
  126.7 7.1 %all_to_all.47 = f32[4,24,128]{2,1,0:T(8,128)S(1)} all-to-all(f32[4,24,128]{2,1,0:T(8,128)S(1)} %get-tuple-element.18), channel_id=1, replica_groups=mesh['y'=4,'z'=16,'core'=2,'x'=4] {'x'}, dimensions={0} | all-to-all | bytes 98304 | tf_op jit(solution)/shard_map/all_to_all | solution.py:30
  133.8 19.7 %all_to_all.48 = f32[16,16,128]{2,1,0:T(8,128)S(1)} all-to-all(f32[16,16,128]{2,1,0:T(8,128)S(1)} %broadcast_in_dim.22), channel_id=1, replica_groups=mesh['y'=4,'z'=16,'core'=2,'x'=4] {'z'}, dimensions={0} | all-to-all | bytes 262144 | tf_op jit(solution)/shard_map/all_to_all | solution.py:30
  153.5 9.3 %all_to_all.49 = f32[4,16,16,128]{3,2,1,0:T(8,128)S(1)} all-to-all(f32[4,16,16,128]{3,2,1,0:T(8,128)S(1)} %broadcast_in_dim.23), channel_id=1, replica_groups=mesh['y'=4,'z'=16,'core'=2,'x'=4] {'y'}, dimensions={0} | all-to-all | bytes 1048576 | tf_op jit(solution)/shard_map/all_to_all | solution.py:30
  162.8 8.5 %collective-permute-start = (f32[1024,128]{1,0:T(8,128)S(1)}, f32[1024,128]{1,0:T(8,128)S(1)}, u32[]{:S(2)}, u32[]{:S(2)}) collective-permute-start(f32[1024,128]{1,0:T(8,128)S(1)} %bitcast.35), channel_id=1, source_target_pairs={{0,4},{4,0},{1,5},{5,1},{2,6},{6,2},{3,7},{7,3},{8,12},{12,8},{9,1... | collective-permute-start | bytes 1572872 | tf_op jit(solution)/shard_map/ppermute | solution.py:294
  171.4 0.7 multiply_convert_fusion
  172.1 0.8 collective-permute-done.far_ref
  172.9 3.2 %pick_scores.1 = f32[256,256]{1,0:T(8,128)} custom-call(s32[512]{0:T(512)S(1)} %multiply_add_fusion.rows_ref, f32[1024,128]{1,0:T(8,128)S(1)} %bitcast.36, f32[1024,128]{1,0:T(8,128)S(1)} %collective-permute-done.far_ref), custom_call_target="tpu_custom_call" | custom-call | tf_op jit(solution)/shard_map/pick_scores/pallas_call | solution.py:230
  (13 shorter events, 0.2 us)
Async XLA Ops:
  7.2 13.3 %copy-start = (bf16[256,2048]{1,0:T(8,128)(2,1)S(1)}, bf16[256,2048]{1,0:T(8,128)(2,1)}, u32[]{:S(2)}) copy-start(bf16[256,2048]{1,0:T(8,128)(2,1)} %param.8) | copy-start | bytes 3145732
  7.2 83.0 %all-gather.2.cloned.1.call-start = ((), (), s32[]{:S(2)}) async-start(), calls=%async_computation.9 | async-start | bytes 4325376 | tf_op jit(solution)/shard_map/all_gather | solution.py:279
  13.3 9.2 %all-to-all-start = ((s32[4,4,128]{2,1,0:T(4,128)}), s32[4,4,128]{2,1,0:T(4,128)S(1)}, u32[]{:S(2)}, u32[]{:S(2)}) async-start(s32[4,4,128]{2,1,0:T(4,128)} %bitcast), calls=%async_computation | async-start | bytes 16384 | tf_op jit(solution)/shard_map/all_to_all | solution.py:30
  22.5 29.1 %all-to-all-start.1 = ((s32[32,1,64]{2,1,0:T(1,128)}), s32[32,1,64]{2,1,0:T(1,128)S(1)}, u32[]{:S(2)}, u32[]{:S(2)}) async-start(s32[32,1,64]{2,1,0:T(1,128)} %copy.53), calls=%async_computation.1 | async-start | bytes 32768 | tf_op jit(solution)/shard_map/all_to_all | solution.py:30
  51.6 8.5 %all-to-all-start.3 = ((bf16[4,16,512]{2,1,0:T(8,128)(2,1)}), bf16[4,16,512]{2,1,0:T(8,128)(2,1)S(1)}, u32[]{:S(2)}, u32[]{:S(2)}) async-start(bf16[4,16,512]{2,1,0:T(8,128)(2,1)} %bitcast.33), calls=%async_computation.3 | async-start | bytes 131072 | tf_op jit(solution)/shard_map/all_to_all | solution.py:30
  61.8 10.4 %all-to-all-start.2 = ((bf16[4,128,512]{2,1,0:T(8,128)(2,1)}), bf16[4,128,512]{2,1,0:T(8,128)(2,1)S(1)}, u32[]{:S(2)}, u32[]{:S(2)}) async-start(bf16[4,128,512]{2,1,0:T(8,128)(2,1)} %broadcast_in_dim.20), calls=%async_computation.2 | async-start | bytes 1048576 | tf_op jit(solution)/shard_map/all_to_all | solution.py:30
  90.2 2.2 %copy-start.1 = (bf16[4096,512]{1,0:T(8,128)(2,1)S(1)}, bf16[4096,512]{1,0:T(8,128)(2,1)}, u32[]{:S(2)}) copy-start(bf16[4096,512]{1,0:T(8,128)(2,1)} %all-gather.2.cloned.1.call-done.all_ref) | copy-start | bytes 12582916
  97.1 29.4 %copy-start.3 = (bf16[128,512]{1,0:T(8,128)(2,1)S(1)}, bf16[128,512]{1,0:T(8,128)(2,1)}, u32[]{:S(2)}) copy-start(bf16[128,512]{1,0:T(8,128)(2,1)} %own_ref.1) | copy-start | bytes 393220
  105.9 2.2 %copy-start.2 = (bf16[8,512,512]{2,1,0:T(8,128)(2,1)S(1)}, bf16[8,512,512]{2,1,0:T(8,128)(2,1)}, u32[]{:S(2)}) copy-start(bf16[8,512,512]{2,1,0:T(8,128)(2,1)} %get-tuple-element.14.got_ref) | copy-start | bytes 12582916
  162.8 10.1 %collective-permute-start = (f32[1024,128]{1,0:T(8,128)S(1)}, f32[1024,128]{1,0:T(8,128)S(1)}, u32[]{:S(2)}, u32[]{:S(2)}) collective-permute-start(f32[1024,128]{1,0:T(8,128)S(1)} %bitcast.35), channel_id=1, source_target_pairs={{0,4},{4,0},{1,5},{5,1},{2,6},{6,2},{3,7},{7,3},{8,12},{12,8},{9,1... | collective-permute-start | bytes 1572872 | tf_op jit(solution)/shard_map/ppermute | solution.py:294
Sparse Core Ops, SparseCore 0:
  10.1 79.9 all-gather.1

commit v3 on v2

--- a/solution.py
+++ b/solution.py
@@ -17,11 +17,14 @@
 LANES = 128
 VMEM = 48 * 1024 * 1024
 INTERPRET = False
-STEPS = 4
+STEPS = 2
 HBM = pltpu.HBM
 f32 = jnp.float32
 bf16 = jnp.bfloat16
+i16 = jnp.int16
 i32 = jnp.int32
+LEVELS = 32512.0
+STEPS_PER_OCTAVE = 64.0
 NT = (((1,), (1,)), ((), ()))
 TN = (((0,), (0,)), ((), ()))
 
@@ -36,6 +39,10 @@
 
 def hbm(shape, dtype):
     return jax.ShapeDtypeStruct(shape, dtype) if INTERPRET else pltpu.HBM(shape, dtype)
+
+
+def pinned(value):
+    return value if INTERPRET else pltpu.with_memory_space_constraint(value, HBM)
 
 
 def params(**more):
@@ -130,7 +137,7 @@
         compiler_params=params(),
         interpret=INTERPRET,
         name="similar_parts",
-    )(everything, own, source, at)
+    )(pinned(everything), own, source, at)
 
 
 def sum_kernel(got_ref, sims_ref, at_ref, sum_ref, held_ref, sems):
@@ -158,7 +165,12 @@
         right = jnp.concatenate([held_ref[2 * shard], held_ref[2 * shard + 1]], axis=0)
         total = jnp.dot(jnp.concatenate(left_high, axis=1), right, preferred_element_type=f32)
         total += jnp.dot(jnp.concatenate(left_low, axis=1), right, preferred_element_type=f32)
-        sum_ref[shard] = total
+        peak = jnp.maximum(jnp.max(jnp.abs(total), axis=1, keepdims=True), 1e-30)
+        level = jnp.floor(jnp.log2(peak) * STEPS_PER_OCTAVE) + 1.0
+        scale = LEVELS / jnp.exp2(level / STEPS_PER_OCTAVE)
+        sum_ref[shard, :BLOCK, :] = jnp.floor(total * scale + 0.5).astype(i32).astype(i16)
+        level = jnp.broadcast_to(level, (BLOCK, LANES)).T[:PLACES].astype(i32).astype(i16)
+        sum_ref[shard, BLOCK:, :] = jnp.concatenate([level] * (total.shape[1] // LANES), axis=1)
 
 
 def weighted_sums(got, sims, at):
@@ -168,18 +180,21 @@
         sum_kernel,
         in_specs=[pl.BlockSpec(memory_space=HBM), vmem, vmem],
         out_specs=vmem,
-        out_shape=jax.ShapeDtypeStruct((kinds // 2, BLOCK, width), f32),
+        out_shape=jax.ShapeDtypeStruct((kinds // 2, BLOCK + PLACES, width), i16),
         scratch_shapes=[pltpu.VMEM(got.shape, bf16), pltpu.SemaphoreType.DMA((kinds // 2,))],
         compiler_params=params(),
         interpret=INTERPRET,
         name="weighted_sums",
-    )(got, sims, at)
+    )(pinned(got), sims, at)
 
 
 def score_kernel(parts_ref, own_ref, chosen_ref, sum_ref, out_ref):
     total = own_ref[...].astype(f32)
     for part in range(parts_ref.shape[0]):
-        total += parts_ref[part]
+        level = parts_ref[part, BLOCK:, :LANES].astype(i32).astype(f32)[:1]
+        level = jnp.broadcast_to(level, (BLOCK, LANES)).T[:, :1]
+        scale = jnp.exp2(level / STEPS_PER_OCTAVE) / LEVELS
+        total += parts_ref[part, :BLOCK, :].astype(i32).astype(f32) * scale
     sum_ref[...] = total
     energy = jnp.sum(total * total, axis=1, keepdims=True)
     energy = jnp.broadcast_to(energy, (BLOCK, LANES)).T[:8]
@@ -214,14 +229,13 @@
             picked = []
             for one in range(GROUP):
                 r = rows_ref[i * (2 * GROUP) + 2 * one + cand]
-                near = near_ref[pl.ds(lax.rem(r, count), 1), :]
-                far = far_ref[pl.ds(lax.rem(r, count), 1), :]
-                picked.append(jnp.where(r < count, near, far))
+                place = pl.ds(r & (count - 1), 1)
+                picked.append(jnp.where(r < count, near_ref[place, :], far_ref[place, :]))
             at = pl.ds(pl.multiple_of(i * GROUP, GROUP), GROUP)
             out_ref[at, cand * LANES : (cand + 1) * LANES] = jnp.concatenate(picked, axis=0)
         return carry
 
-    lax.fori_loop(0, out_ref.shape[0] // GROUP, step, 0)
+    lax.fori_loop(0, out_ref.shape[0] // GROUP, step, 0, unroll=4)
 
 
 def pick_scores(rows, near, far):

time: 184 us -> 177 us (0.962)
  blocking collectives: 61 us -> 56 us
  local copies, waits for them, and re-layouts: 11.7 us -> 7.33 us
  Pallas kernels: 14.2 us -> 16.7 us
    all_to_all x5, blocking collectives: 61 us -> 56 us  [exchange(): return lax.all_to_all(parts, axis, split_axis=0, concat_axis=0, tiled=True)]
    unnamed x11 -> x7, local copies, waits for them, and re-layouts: 6.8 us -> 2.42 us
where the time goes in v3:
time: 177 us; the launch traced here: 176 us
  blocking collectives  56 us (32%)
  waiting for transfers between devices  41.4 us (23%)
  starting transfers between devices  38.4 us (22%)
  Pallas kernels  16.7 us (9%)
  between operations  14.2 us (8%)
  local copies, waits for them, and re-layouts  7.33 us (4%)
  other arithmetic  1.8 us (1%)
    all_to_all x5, blocking collectives, exchange(): return lax.all_to_all(parts, axis, split_axis=0, concat_axis=0, tiled=True)  56 us
    all_to_all x4, starting transfers between devices, exchange(): return lax.all_to_all(parts, axis, split_axis=0, concat_axis=0, tiled=True)  29.8 us
    all_to_all x4, waiting for transfers between devices, exchange(): return lax.all_to_all(parts, axis, split_axis=0, concat_axis=0, tiled=True)  22.1 us
    all_gather x1, waiting for transfers between devices, per_device(): everything = lax.all_gather(descriptors, ('z', 'core'), axis=0, tiled=True)  17.8 us
    ppermute x1, starting transfers between devices, per_device(): far = lax.ppermute(near, 'core', [(0, 1), (1, 0)])  8.54 us
    pallas_call x1, Pallas kernels, similar_parts(): pl.pallas_call(functools.partial(similar_kernel, per), grid=(groups // pe...  6.21 us
    pallas_call x1, Pallas kernels, build_table(): pl.pallas_call(table_kernel, out_shape=jax.ShapeDtypeStruct((shards // GR...  3.8 us
    pallas_call x1, Pallas kernels, weighted_sums(): pl.pallas_call(sum_kernel, in_specs=[pl.BlockSpec(memory_space=HBM), vmem...  3.76 us
  transfers between devices with their start and end apart: 6, of which 6 were waited for; matrix products, arithmetic and copies ran while one was open for 5% of the time, Pallas kernels for 2%

profile of v3, /device:TPU:1, one launch (start us, length us, event | category | flops | bytes accessed | tf_op | source)
XLA Modules:
  0.0 176.1 jit_solution(12585024631833161872)
XLA Ops:
  7.2 0.0 copy-start
  7.2 0.0 all-gather.2.cloned.1.call-start
  7.2 0.7 all-gather.2.cloned.1.call-update
  7.9 0.8 copy.50.listed_ref
  8.7 0.8 copy.51.owned_ref
  9.5 3.8 %slot_table.1 = s32[16,128]{1,0:T(8,128)} custom-call(s32[128,10]{1,0:T(8,128)S(1)} %copy.50.listed_ref, s32[128,10]{1,0:T(8,128)S(1)} %copy.51.owned_ref), custom_call_target="tpu_custom_call" | custom-call | tf_op jit(solution)/shard_map/slot_table/pallas_call | solution.py:81
  13.3 5.0 %all-to-all-start = ((s32[4,4,128]{2,1,0:T(4,128)}), s32[4,4,128]{2,1,0:T(4,128)S(1)}, u32[]{:S(2)}, u32[]{:S(2)}) async-start(s32[4,4,128]{2,1,0:T(4,128)} %bitcast), calls=%async_computation | async-start | bytes 16384 | tf_op jit(solution)/shard_map/all_to_all | solution.py:33
  18.3 0.8 copy.62
  19.1 0.1 eq.56
  19.3 0.3 convert_reduce_fusion
  19.6 0.1 eq.60
  19.7 0.1 copy.63
  19.8 0.7 broadcast_compare_fusion.1
  20.5 0.0 copy-done
  20.5 0.2 convolution_convert_fusion
  20.8 0.8 reshape.139
  21.5 0.1 copy.52
  21.6 0.7 copy.53
  22.3 0.2 all-to-all-done
  22.5 17.3 %all-to-all-start.1 = ((s32[32,1,64]{2,1,0:T(1,128)}), s32[32,1,64]{2,1,0:T(1,128)S(1)}, u32[]{:S(2)}, u32[]{:S(2)}) async-start(s32[32,1,64]{2,1,0:T(1,128)} %copy.53), calls=%async_computation.1 | async-start | bytes 32768 | tf_op jit(solution)/shard_map/all_to_all | solution.py:33
  39.9 0.6 copy.68
  40.5 11.1 %all-to-all-done.1 = s32[32,1,64]{2,1,0:T(1,128)S(1)} async-done(((s32[32,1,64]{2,1,0:T(1,128)}), s32[32,1,64]{2,1,0:T(1,128)S(1)}, u32[]{:S(2)}, u32[]{:S(2)}) %all-to-all-start.1) | async-done | bytes 8224 | tf_op jit(solution)/shard_map/all_to_all | solution.py:33
  51.6 4.0 %all-to-all-start.3 = ((bf16[4,16,512]{2,1,0:T(8,128)(2,1)}), bf16[4,16,512]{2,1,0:T(8,128)(2,1)S(1)}, u32[]{:S(2)}, u32[]{:S(2)}) async-start(bf16[4,16,512]{2,1,0:T(8,128)(2,1)} %bitcast.33), calls=%async_computation.3 | async-start | bytes 131072 | tf_op jit(solution)/shard_map/all_to_all | solution.py:33
  55.6 0.1 reshape.138
  55.7 0.1 copy.54
  55.8 4.3 %all-to-all-done.3 = bf16[4,16,512]{2,1,0:T(8,128)(2,1)S(1)} async-done(((bf16[4,16,512]{2,1,0:T(8,128)(2,1)}), bf16[4,16,512]{2,1,0:T(8,128)(2,1)S(1)}, u32[]{:S(2)}, u32[]{:S(2)}) %all-to-all-start.3) | async-done | bytes 65568 | tf_op jit(solution)/shard_map/all_to_all | solution.py:33
  60.1 1.7 broadcast_in_dim.20
  61.9 3.5 %all-to-all-start.2 = ((bf16[4,128,512]{2,1,0:T(8,128)(2,1)}), bf16[4,128,512]{2,1,0:T(8,128)(2,1)S(1)}, u32[]{:S(2)}, u32[]{:S(2)}) async-start(bf16[4,128,512]{2,1,0:T(8,128)(2,1)} %broadcast_in_dim.20), calls=%async_computation.2 | async-start | bytes 1048576 | tf_op jit(solution)/shard_map/all_to_all | solution.py:33
  65.4 0.1 copy.57
  65.5 0.1 copy.58
  65.5 0.1 copy.60
  65.6 0.1 stack_reshape.3
  65.8 6.5 %all-to-all-done.2 = bf16[4,128,512]{2,1,0:T(8,128)(2,1)S(1)} async-done(((bf16[4,128,512]{2,1,0:T(8,128)(2,1)}), bf16[4,128,512]{2,1,0:T(8,128)(2,1)S(1)}, u32[]{:S(2)}, u32[]{:S(2)}) %all-to-all-start.2) | async-done | bytes 524320 | tf_op jit(solution)/shard_map/all_to_all | solution.py:33
  72.3 0.1 copy.65.src_ref
  72.3 17.8 %all-gather.2.cloned.1.call-done.all_ref = bf16[4096,512]{1,0:T(8,128)(2,1)} async-done(((bf16[128,512]{1,0:T(8,128)(2,1)}), bf16[4096,512]{1,0:T(8,128)(2,1)}) %all-gather.2.cloned.1.call-update) | async-done | bytes 4194320 | tf_op jit(solution)/shard_map/all_gather | solution.py:293
  90.2 6.2 %similar_parts.1 = (bf16[8,512,512]{2,1,0:T(8,128)(2,1)}, f32[32,128]{1,0:T(8,128)S(1)}) custom-call(bf16[4096,512]{1,0:T(8,128)(2,1)} %all-gather.2.cloned.1.call-done.all_ref, bf16[512,512]{1,0:T(8,128)(2,1)S(1)} %bitcast.34, s32[32,128]{1,0:T(8,128)S(1)} %copy.65.src_ref, s32[32,128]{1,0:T(8,128)S(1)} %bitcast.38), custom_call_target="tpu_custom_call" | custom-call | tf_op jit(solution)/shard_map/similar_parts/pallas_call | solution.py:120
  96.4 0.0 copy-start.1
  96.4 8.5 %all_to_all.45.sims_ref = f32[4,32,128]{2,1,0:T(8,128)S(1)} all-to-all(f32[4,32,128]{2,1,0:T(8,128)S(1)} %broadcast_in_dim.21), channel_id=1, replica_groups=mesh['y'=4,'z'=16,'core'=2,'x'=4] {'x'}, dimensions={0} | all-to-all | bytes 131072 | tf_op jit(solution)/shard_map/all_to_all | solution.py:33
  104.9 3.8 %weighted_sums.1 = s16[4,144,512]{2,1,0:T(8,128)(2,1)S(1)} custom-call(bf16[8,512,512]{2,1,0:T(8,128)(2,1)} %get-tuple-element.14.got_ref, f32[4,32,128]{2,1,0:T(8,128)S(1)} %all_to_all.45.sims_ref, s32[32,128]{1,0:T(8,128)S(1)} %bitcast.39), custom_call_target="tpu_custom_call" | custom-call | tf_op jit(solution)/shard_map/weighted_sums/pallas_call | solution.py:179
  108.7 11.9 %all_to_all.46.parts_ref = s16[4,144,512]{2,1,0:T(8,128)(2,1)S(1)} all-to-all(s16[4,144,512]{2,1,0:T(8,128)(2,1)S(1)} %weighted_sums.1), channel_id=1, replica_groups=mesh['y'=4,'z'=16,'core'=2,'x'=4] {'y'}, dimensions={0} | all-to-all | bytes 1179648 | tf_op jit(solution)/shard_map/all_to_all | solution.py:33
  120.5 0.0 copy-done.1
  120.5 0.5 score_parts.1
  121.1 6.7 %all_to_all.47 = f32[4,24,128]{2,1,0:T(8,128)S(1)} all-to-all(f32[4,24,128]{2,1,0:T(8,128)S(1)} %get-tuple-element.18), channel_id=1, replica_groups=mesh['y'=4,'z'=16,'core'=2,'x'=4] {'x'}, dimensions={0} | all-to-all | bytes 98304 | tf_op jit(solution)/shard_map/all_to_all | solution.py:33
  127.8 19.6 %all_to_all.48 = f32[16,16,128]{2,1,0:T(8,128)S(1)} all-to-all(f32[16,16,128]{2,1,0:T(8,128)S(1)} %broadcast_in_dim.22), channel_id=1, replica_groups=mesh['y'=4,'z'=16,'core'=2,'x'=4] {'z'}, dimensions={0} | all-to-all | bytes 262144 | tf_op jit(solution)/shard_map/all_to_all | solution.py:33
  147.5 9.3 %all_to_all.49 = f32[4,16,16,128]{3,2,1,0:T(8,128)S(1)} all-to-all(f32[4,16,16,128]{3,2,1,0:T(8,128)S(1)} %broadcast_in_dim.23), channel_id=1, replica_groups=mesh['y'=4,'z'=16,'core'=2,'x'=4] {'y'}, dimensions={0} | all-to-all | bytes 1048576 | tf_op jit(solution)/shard_map/all_to_all | solution.py:33
  156.8 8.5 %collective-permute-start = (f32[1024,128]{1,0:T(8,128)S(1)}, f32[1024,128]{1,0:T(8,128)S(1)}, u32[]{:S(2)}, u32[]{:S(2)}) collective-permute-start(f32[1024,128]{1,0:T(8,128)S(1)} %bitcast.35), channel_id=1, source_target_pairs={{0,4},{4,0},{1,5},{5,1},{2,6},{6,2},{3,7},{7,3},{8,12},{12,8},{9,1... | collective-permute-start | bytes 1572872 | tf_op jit(solution)/shard_map/ppermute | solution.py:308
  165.3 0.7 multiply_convert_fusion
  166.1 0.8 collective-permute-done.far_ref
  166.9 2.4 %pick_scores.1 = f32[256,256]{1,0:T(8,128)} custom-call(s32[512]{0:T(512)S(1)} %multiply_add_fusion.rows_ref, f32[1024,128]{1,0:T(8,128)S(1)} %bitcast.36, f32[1024,128]{1,0:T(8,128)S(1)} %collective-permute-done.far_ref), custom_call_target="tpu_custom_call" | custom-call | tf_op jit(solution)/shard_map/pick_scores/pallas_call | solution.py:244
  (13 shorter events, 0.2 us)
Async XLA Ops:
  7.2 13.3 %copy-start = (bf16[256,2048]{1,0:T(8,128)(2,1)S(1)}, bf16[256,2048]{1,0:T(8,128)(2,1)}, u32[]{:S(2)}) copy-start(bf16[256,2048]{1,0:T(8,128)(2,1)} %param.8) | copy-start | bytes 3145732
  7.2 83.0 %all-gather.2.cloned.1.call-start = ((), (), s32[]{:S(2)}) async-start(), calls=%async_computation.9 | async-start | bytes 4325376 | tf_op jit(solution)/shard_map/all_gather | solution.py:293
  13.3 9.2 %all-to-all-start = ((s32[4,4,128]{2,1,0:T(4,128)}), s32[4,4,128]{2,1,0:T(4,128)S(1)}, u32[]{:S(2)}, u32[]{:S(2)}) async-start(s32[4,4,128]{2,1,0:T(4,128)} %bitcast), calls=%async_computation | async-start | bytes 16384 | tf_op jit(solution)/shard_map/all_to_all | solution.py:33
  22.5 29.1 %all-to-all-start.1 = ((s32[32,1,64]{2,1,0:T(1,128)}), s32[32,1,64]{2,1,0:T(1,128)S(1)}, u32[]{:S(2)}, u32[]{:S(2)}) async-start(s32[32,1,64]{2,1,0:T(1,128)} %copy.53), calls=%async_computation.1 | async-start | bytes 32768 | tf_op jit(solution)/shard_map/all_to_all | solution.py:33
  51.6 8.5 %all-to-all-start.3 = ((bf16[4,16,512]{2,1,0:T(8,128)(2,1)}), bf16[4,16,512]{2,1,0:T(8,128)(2,1)S(1)}, u32[]{:S(2)}, u32[]{:S(2)}) async-start(bf16[4,16,512]{2,1,0:T(8,128)(2,1)} %bitcast.33), calls=%async_computation.3 | async-start | bytes 131072 | tf_op jit(solution)/shard_map/all_to_all | solution.py:33
  61.9 10.4 %all-to-all-start.2 = ((bf16[4,128,512]{2,1,0:T(8,128)(2,1)}), bf16[4,128,512]{2,1,0:T(8,128)(2,1)S(1)}, u32[]{:S(2)}, u32[]{:S(2)}) async-start(bf16[4,128,512]{2,1,0:T(8,128)(2,1)} %broadcast_in_dim.20), calls=%async_computation.2 | async-start | bytes 1048576 | tf_op jit(solution)/shard_map/all_to_all | solution.py:33
  96.4 24.2 %copy-start.1 = (bf16[128,512]{1,0:T(8,128)(2,1)S(1)}, bf16[128,512]{1,0:T(8,128)(2,1)}, u32[]{:S(2)}) copy-start(bf16[128,512]{1,0:T(8,128)(2,1)} %own_ref.1) | copy-start | bytes 393220
  156.8 10.1 %collective-permute-start = (f32[1024,128]{1,0:T(8,128)S(1)}, f32[1024,128]{1,0:T(8,128)S(1)}, u32[]{:S(2)}, u32[]{:S(2)}) collective-permute-start(f32[1024,128]{1,0:T(8,128)S(1)} %bitcast.35), channel_id=1, source_target_pairs={{0,4},{4,0},{1,5},{5,1},{2,6},{6,2},{3,7},{7,3},{8,12},{12,8},{9,1... | collective-permute-start | bytes 1572872 | tf_op jit(solution)/shard_map/ppermute | solution.py:308
Sparse Core Ops, SparseCore 0:
  10.1 79.9 all-gather.1

commit v4 on v3

--- a/solution.py
+++ b/solution.py
@@ -15,6 +15,7 @@
 GROUP = 8
 CORES = 2
 LANES = 128
+SHARD = ("y", "z", "half", "core")
 VMEM = 48 * 1024 * 1024
 INTERPRET = False
 STEPS = 2
@@ -49,7 +50,7 @@
     return pltpu.CompilerParams(vmem_limit_bytes=VMEM, **more)
 
 
-def table_kernel(listed_ref, owned_ref, table_ref):
+def table_kernel(halves, listed_ref, owned_ref, high_ref, low_ref):
     rows = listed_ref.shape[0]
     row = lax.broadcasted_iota(i32, (rows, LANES), 0)
     lane = lax.broadcasted_iota(i32, (rows, LANES), 1)
@@ -61,6 +62,9 @@
     for slot in range(listed_ref.shape[1]):
         listed = listed_ref[:, slot : slot + 1]
         shard = lax.shift_right_logical(listed, 7)
+        plane = shard // (4 * halves)
+        half = lax.shift_right_logical(shard, 2) - plane * halves
+        shard = (plane * 2 + (lax.shift_right_logical(shard, 1) & 1)) * (2 * halves) + half * 2 + (shard & 1)
         match = lane == shard
         ones = jnp.where(match, 1.0, 0.0)
         counted = jnp.dot(lower, ones.astype(bf16), preferred_element_type=f32) + before
@@ -71,16 +75,14 @@
         source = ((listed & (BLOCK - 1)) * 2 + owned_ref[:, slot : slot + 1]).astype(f32)
         high += lax.dot_general(left, jnp.where(here, own_mark, 0.0).astype(bf16), TN, preferred_element_type=f32)
         low += lax.dot_general(left, jnp.where(here, source, 0.0).astype(bf16), TN, preferred_element_type=f32)
-    count = table_ref.shape[0]
-    high = high[:count].astype(i32)
-    low = low[:count].astype(i32)
-    table_ref[...] = jnp.where(high > 0, (high - 1) * 256 + low, -1)
-
-
-def build_table(neighbours, owned, shards):
-    return pl.pallas_call(
-        table_kernel,
-        out_shape=jax.ShapeDtypeStruct((shards // GROUP, LANES), i32),
+    high_ref[...] = high[: high_ref.shape[0]]
+    low_ref[...] = low[: low_ref.shape[0]]
+
+
+def build_table(neighbours, owned, shards, halves):
+    return pl.pallas_call(
+        functools.partial(table_kernel, halves),
+        out_shape=[jax.ShapeDtypeStruct((shards // GROUP, LANES), f32)] * 2,
         compiler_params=params(),
         interpret=INTERPRET,
         name="slot_table",
@@ -88,8 +90,10 @@
 
 
 def similar_kernel(groups, all_ref, own_ref, src_ref, at_ref, got_ref, sims_ref):
-    row = lax.broadcasted_iota(i32, (BLOCK, LANES), 0)
     shards = own_ref.shape[0] // BLOCK
+    kinds = 2 * shards
+    slots = kinds * PLACES
+    row = lax.broadcasted_iota(i32, (BLOCK, slots), 0)
     for group in range(groups):
         parts = []
         for one in range(group * GROUP, (group + 1) * GROUP):
@@ -106,10 +110,11 @@
             own = own_ref[shard * BLOCK : (shard + 1) * BLOCK, :]
             dots = lax.dot_general(own, jnp.concatenate(chunks, axis=0), NT, preferred_element_type=f32)
             for kind in range(2):
-                n = group * GROUP + 2 * shard + kind
-                held = jnp.where(row == at_ref[n : n + 1, :], dots[:, kind * LANES : (kind + 1) * LANES], 0.0)
+                n = group * kinds + 2 * shard + kind
+                here = row[:, :LANES] == at_ref[n : n + 1, :]
+                held = jnp.where(here, dots[:, kind * LANES : (kind + 1) * LANES], 0.0)
                 sims.append(jnp.sum(held, axis=0, keepdims=True))
-        sims_ref[group * GROUP : (group + 1) * GROUP, :] = jnp.concatenate(sims, axis=0)
+        sims_ref[group * kinds : (group + 1) * kinds, :] = jnp.concatenate(sims, axis=0)
 
 
 def similar_parts(everything, own, source, at, steps=STEPS):
@@ -123,16 +128,16 @@
         in_specs=[
             pl.BlockSpec((per * GROUP * BLOCK, width), lambda i: (i, 0)),
             pl.BlockSpec(own.shape, lambda i: (0, 0)),
-            pl.BlockSpec((per * GROUP, LANES), lambda i: (i, 0)),
-            pl.BlockSpec((per * GROUP, LANES), lambda i: (i, 0)),
+            pl.BlockSpec((per * GROUP, kinds * PLACES), lambda i: (i, 0)),
+            pl.BlockSpec((per * kinds, LANES), lambda i: (i, 0)),
         ],
         out_specs=[
             pl.BlockSpec((kinds, per * LANES, width), lambda i: (0, i, 0)),
-            pl.BlockSpec((per * GROUP, LANES), lambda i: (i, 0)),
+            pl.BlockSpec((per * kinds, LANES), lambda i: (i, 0)),
         ],
         out_shape=[
             hbm((kinds, groups * LANES, width), bf16),
-            jax.ShapeDtypeStruct((groups * GROUP, LANES), f32),
+            jax.ShapeDtypeStruct((groups * kinds, LANES), f32),
         ],
         compiler_params=params(),
         interpret=INTERPRET,
@@ -148,16 +153,16 @@
         copies.append(pltpu.make_async_copy(got_ref.at[pair], held_ref.at[pair], sems.at[shard]))
         copies[-1].start()
     row = lax.broadcasted_iota(i32, (BLOCK, LANES), 0)
-    similar = jnp.sum(sims_ref[...], axis=0) / D
+    similar = jnp.sum(sims_ref[:, : at_ref.shape[0], :], axis=0) / D
     weight = similar * similar * similar
     high = weight.astype(bf16).astype(f32)
     low = weight - high
-    groups = at_ref.shape[0] // GROUP
+    groups = at_ref.shape[0] // (2 * shards)
     for shard in range(shards):
         left_high, left_low = [], []
         for k in (2 * shard, 2 * shard + 1):
             for group in range(groups):
-                n = group * GROUP + k
+                n = group * 2 * shards + k
                 here = row == at_ref[n : n + 1, :]
                 left_high.append(jnp.where(here, high[n : n + 1], 0.0).astype(bf16))
                 left_low.append(jnp.where(here, low[n : n + 1], 0.0).astype(bf16))
@@ -200,9 +205,16 @@
     energy = jnp.broadcast_to(energy, (BLOCK, LANES)).T[:8]
     high = total.astype(bf16)
     low = (total - high.astype(f32)).astype(bf16)
-    chosen = chosen_ref[...]
-    scores = lax.dot_general(chosen, high, NT, preferred_element_type=f32)
-    scores += lax.dot_general(chosen, low, NT, preferred_element_type=f32)
+    lanes = out_ref.shape[0]
+    quarters = total.shape[1] // LANES
+    before = chosen_ref.shape[1] - quarters * PLACES
+    scores = jnp.zeros((lanes * PLACES, LANES), f32)
+    for quarter in range(quarters):
+        at = before + quarter * PLACES
+        chosen = jnp.concatenate([chosen_ref[lane, at : at + PLACES, :] for lane in range(lanes)], axis=0).astype(bf16)
+        columns = slice(quarter * LANES, (quarter + 1) * LANES)
+        scores += lax.dot_general(chosen, high[:, columns], NT, preferred_element_type=f32)
+        scores += lax.dot_general(chosen, low[:, columns], NT, preferred_element_type=f32)
     for lane in range(out_ref.shape[0]):
         out_ref[lane, :PLACES, :] = scores[lane * PLACES : (lane + 1) * PLACES]
         out_ref[lane, PLACES:, :] = energy
@@ -252,21 +264,30 @@
     )(rows, near, far)
 
 
-def slot_orders(table, ys, zs):
-    count = zs * CORES
+def own_and_orders(descriptors, high, low, ys, halves):
+    rows, width = descriptors.shape
+    shards = 2 * ys
+    count = halves * CORES
     groups = count // GROUP
-    ahead = exchange(table.reshape(ys, groups, LANES), "y")
-    back = table.reshape(ys, count, PLACES).transpose(1, 0, 2).reshape(count, 1, ys * PLACES)
-    back = exchange(back, ("z", "core")).reshape(count, ys, PLACES)
-    ahead_own = jnp.where(ahead >= 0, lax.shift_right_logical(ahead, 8), -1)
-    ahead_src = jnp.where(ahead >= 0, lax.shift_right_logical(ahead, 1) & (BLOCK - 1), -1)
+    codes = jnp.concatenate([high.reshape(shards, -1), low.reshape(shards, -1)], axis=1).astype(bf16)
+    codes = jnp.pad(codes, ((0, 0), (0, width - codes.shape[1])))
+    codes = jnp.broadcast_to(codes[:, None, :], (shards, PLACES, width))
+    sent = jnp.concatenate([jnp.broadcast_to(descriptors[None], (shards, rows, width)), codes], axis=1)
+    came = exchange(sent, ("y", "half"))
+    own = came[:, :rows, :].reshape(shards * rows, width)
+    codes = came[:, rows, : 2 * groups * LANES].astype(i32).reshape(shards, 2, groups, LANES)
+    ahead_own = codes[:, 0] - 1
+    ahead_src = jnp.where(ahead_own >= 0, lax.shift_right_logical(codes[:, 1], 1), -1)
+    back = jnp.where(high > 0, (high - 1) * 256 + low, -1).astype(i32)
+    back = back.reshape(shards, count, PLACES).transpose(1, 0, 2).reshape(count, 1, shards * PLACES)
+    back = exchange(back, ("z", "core")).reshape(count, shards, PLACES)
     held = (back >= 0) & ((back & 1) == 1)
     back_src = jnp.where(held, lax.shift_right_logical(back, 8), -1)
     back_own = jnp.where(held, lax.shift_right_logical(back, 1) & (BLOCK - 1), -1)
-    source = jnp.stack([ahead_src.reshape(ys, count, PLACES).transpose(1, 0, 2), back_src], axis=2)
-    at = jnp.stack([ahead_own, back_own.transpose(1, 0, 2).reshape(ys, groups, LANES)], axis=1)
-    at = at.reshape(2 * ys, groups, LANES).transpose(1, 0, 2).reshape(groups * GROUP, LANES)
-    return source.reshape(count, LANES), at
+    source = jnp.stack([ahead_src.reshape(shards, count, PLACES).transpose(1, 0, 2), back_src], axis=2)
+    at = jnp.stack([ahead_own, back_own.transpose(1, 0, 2).reshape(shards, groups, LANES)], axis=1)
+    at = at.reshape(2 * shards, groups, LANES).transpose(1, 0, 2).reshape(groups * 2 * shards, LANES)
+    return own, source.reshape(count, 2 * shards * PLACES), at
 
 
 def query_entries(queries, candidates, xs, zs):
@@ -274,12 +295,11 @@
     order = jnp.arange(flat.shape[0], dtype=i32)
     earlier = (flat[:, None] == flat[None, :]) & (order[:, None] > order[None, :])
     rank = jnp.sum(earlier.astype(i32), axis=1)
-    here = lax.axis_index(("y", "z", "core"))
+    here = lax.axis_index(SHARD)
     hits = (flat == here)[None, :] & (rank[None, :] == jnp.arange(PLACES, dtype=i32)[:, None])
     hits = jnp.sum(hits.reshape(PLACES, -1, 2).astype(f32), axis=2).astype(bf16)
-    chosen = jnp.dot(hits, queries, preferred_element_type=f32).astype(bf16)
-    chosen = chosen.reshape(PLACES, xs, -1).transpose(1, 0, 2)
-    chosen = exchange(chosen, "x").reshape(xs * PLACES, -1)
+    chosen = jnp.dot(hits, queries, preferred_element_type=f32)
+    chosen = chosen.reshape(PLACES, xs, -1, LANES).transpose(1, 2, 0, 3).reshape(xs, -1, LANES)
     plane = flat // CORES
     core = flat - plane * CORES
     far = (core != lax.axis_index("core")).astype(i32)
@@ -288,23 +308,24 @@
 
 
 def per_device(descriptors, neighbours, owned, queries, candidates):
-    ys, zs, xs = lax.axis_size("y"), lax.axis_size("z"), lax.axis_size("x")
+    ys, halves, xs = lax.axis_size("y"), lax.axis_size("z"), lax.axis_size("x")
+    zs = 2 * halves
     rows, width = descriptors.shape
     everything = lax.all_gather(descriptors, ("z", "core"), axis=0, tiled=True)
-    table = build_table(neighbours, owned, ys * zs * CORES)
-    source, at = slot_orders(table, ys, zs)
-    own = spread(descriptors, "y", ys).reshape(ys * rows, width)
+    high, low = build_table(neighbours, owned, ys * zs * CORES, halves)
+    own, source, at = own_and_orders(descriptors, high, low, ys, halves)
     chosen, score_rows = query_entries(queries, candidates, xs, zs)
     source, at, own, chosen, score_rows = lax.optimization_barrier((source, at, own, chosen, score_rows))
     got, sims = similar_parts(everything, own, source, at)
-    sims = spread(sims, "x", xs)
-    parts = exchange(weighted_sums(got, sims, at), "y")
-    summed, parts = score_parts(parts, descriptors, chosen, xs)
+    sims = jnp.concatenate([jnp.broadcast_to(sims[None], (xs,) + sims.shape), chosen], axis=1)
+    sims = exchange(sims, "x")
+    parts = exchange(weighted_sums(got, sims, at), ("y", "half"))
+    summed, parts = score_parts(parts, descriptors, sims, xs)
     whole = jnp.sum(exchange(parts, "x"), axis=0)
     scale = lax.rsqrt(whole[PLACES] / (xs * width) + 1e-06)
     augmented = (summed * scale[:, None]).astype(bf16)
     mine = whole[:PLACES] * (scale / math.sqrt(xs * width))[None, :]
-    near = spread(spread(mine, "z", zs), "y", ys).reshape(-1, rows)
+    near = spread(spread(mine, ("z", "half"), zs), "y", ys).reshape(-1, rows)
     far = lax.ppermute(near, "core", [(0, 1), (1, 0)])
     return augmented, pick_scores(score_rows, near, far)
 
@@ -312,12 +333,11 @@
 def solution(mesh):
     shards, lanes = mesh.devices.shape
     ys = GROUP // CORES
-    split = Mesh(mesh.devices.reshape(ys, shards // GROUP, CORES, lanes), ("y", "z", "core", "x"))
-    shard = ("y", "z", "core")
+    devices = mesh.devices.reshape(ys, shards // GROUP // 2, 2, CORES, lanes)
     return jax.shard_map(
         per_device,
-        mesh=split,
-        in_specs=(P(shard, "x"), P(shard, None), P(shard, None), P("x", None), P("x", None)),
-        out_specs=(P(shard, "x"), P("x", None)),
+        mesh=Mesh(devices, SHARD + ("x",)),
+        in_specs=(P(SHARD, "x"), P(SHARD, None), P(SHARD, None), P("x", None), P("x", None)),
+        out_specs=(P(SHARD, "x"), P("x", None)),
         check_vma=False,
     )

time: 177 us -> 190 us (1.073)
  waiting for transfers between devices: 41.4 us -> 58.5 us
  starting transfers between devices: 38.4 us -> 29.9 us
  blocking collectives: 56 us -> 62.7 us
  local copies, waits for them, and re-layouts: 7.33 us -> 4.96 us
    all_gather x1, waiting for transfers between devices: 17.8 us -> 33.5 us  [per_device(): everything = lax.all_gather(descriptors, ('z', 'core'), axis=0, tiled=True)]
    all_to_all x4 -> x2, starting transfers between devices: 29.8 us -> 21.2 us  [exchange(): return lax.all_to_all(parts, axis, split_axis=0, concat_axis=0, tiled=True)]
    all_to_all x5, blocking collectives: 56 us -> 62.7 us  [exchange(): return lax.all_to_all(parts, axis, split_axis=0, concat_axis=0, tiled=True)]
    all_to_all x4 -> x2, waiting for transfers between devices: 22.1 us -> 23.5 us  [exchange(): return lax.all_to_all(parts, axis, split_axis=0, concat_axis=0, tiled=True)]
  transfers between devices with their start and end apart: 6 -> 4, of which waited for: 6 -> 4; matrix products, arithmetic and copies ran while one was open for 5% -> 3% of each run, Pallas kernels for 2% -> 0%
where the time goes in v4:
time: 190 us
  blocking collectives  62.7 us (33%)
  waiting for transfers between devices  58.5 us (31%)
  starting transfers between devices  29.9 us (16%)
  Pallas kernels  16.9 us (9%)
  between operations  14.4 us (8%)
  local copies, waits for them, and re-layouts  4.96 us (3%)
  other arithmetic  2.28 us (1%)
    all_to_all x5, blocking collectives, exchange(): return lax.all_to_all(parts, axis, split_axis=0, concat_axis=0, tiled=True)  62.7 us
    all_gather x1, waiting for transfers between devices, per_device(): everything = lax.all_gather(descriptors, ('z', 'core'), axis=0, tiled=True)  33.5 us
    all_to_all x2, waiting for transfers between devices, exchange(): return lax.all_to_all(parts, axis, split_axis=0, concat_axis=0, tiled=True)  23.5 us
    all_to_all x2, starting transfers between devices, exchange(): return lax.all_to_all(parts, axis, split_axis=0, concat_axis=0, tiled=True)  21.2 us
    ppermute x1, starting transfers between devices, per_device(): far = lax.ppermute(near, 'core', [(0, 1), (1, 0)])  8.61 us
    pallas_call x1, Pallas kernels, similar_parts(): pl.pallas_call(functools.partial(similar_kernel, per), grid=(groups // pe...  5.56 us
    pallas_call x1, Pallas kernels, weighted_sums(): pl.pallas_call(sum_kernel, in_specs=[pl.BlockSpec(memory_space=HBM), vmem...  4.97 us
  transfers between devices with their start and end apart: 4, of which 4 were waited for; matrix products, arithmetic and copies ran while one was open for 3% of the time, Pallas kernels for 0%

profile of v4, /device:TPU:1, one launch (start us, length us, event | category | flops | bytes accessed | tf_op | source)
XLA Modules:
  0.0 189.8 jit_solution(10086240923991608364)
XLA Ops:
  7.2 0.0 copy-start
  7.2 0.9 copy.48.listed_ref
  8.1 0.8 copy.49.owned_ref
  8.9 3.3 %slot_table.1 = (f32[16,128]{1,0:T(8,128)S(1)}, f32[16,128]{1,0:T(8,128)S(1)}) custom-call(s32[128,10]{1,0:T(8,128)S(1)} %copy.48.listed_ref, s32[128,10]{1,0:T(8,128)S(1)} %copy.49.owned_ref), custom_call_target="tpu_custom_call" | custom-call | tf_op jit(solution)/shard_map/slot_table/pallas_call | solution.py:83
  12.2 0.1 reshape.167
  12.3 0.7 reshape.168
  13.0 16.6 %all-to-all-start.1 = ((s32[16,1,128]{2,1,0:T(1,128)}), s32[16,1,128]{2,1,0:T(1,128)S(1)}, u32[]{:S(2)}, u32[]{:S(2)}) async-start(s32[16,1,128]{2,1,0:T(1,128)} %bitcast.5), calls=%async_computation.1 | async-start | bytes 16384 | tf_op jit(solution)/shard_map/all_to_all | solution.py:34
  29.6 1.0 broadcast_in_dim.19
  30.6 1.1 pad_maximum_fusion
  31.7 0.0 copy-start.2
  31.7 9.6 %all-to-all-done.1 = s32[16,1,128]{2,1,0:T(1,128)S(1)} async-done(((s32[16,1,128]{2,1,0:T(1,128)}), s32[16,1,128]{2,1,0:T(1,128)S(1)}, u32[]{:S(2)}, u32[]{:S(2)}) %all-to-all-start.1) | async-done | bytes 8224 | tf_op jit(solution)/shard_map/all_to_all | solution.py:34
  41.4 4.6 %all-to-all-start = ((bf16[8,144,512]{2,1,0:T(8,128)(2,1)}), bf16[8,144,512]{2,1,0:T(8,128)(2,1)S(1)}, u32[]{:S(2)}, u32[]{:S(2)}) async-start(bf16[8,144,512]{2,1,0:T(8,128)(2,1)} %pad_maximum_fusion), calls=%async_computation | async-start | bytes 2359296 | tf_op jit(solution)/shard_map/all_to_all | solution.py:34
  46.0 0.0 all-gather.2.cloned.1.call-start
  46.0 0.7 all-gather.2.cloned.1.call-update
  46.7 0.0 copy-done.2
  46.7 0.1 copy.59
  46.9 0.1 eq.56
  47.0 0.3 convert_reduce_fusion
  47.3 0.1 eq.60
  47.4 0.1 copy.60
  47.5 0.0 copy-done
  47.5 0.3 fusion.11
  47.8 0.1 reshape.173
  48.0 0.1 select_reduce_fusion
  48.0 0.1 select_n.43
  48.1 0.1 stack_reshape.3
  48.2 0.1 select_n.41
  48.3 13.9 %all-to-all-done = bf16[8,144,512]{2,1,0:T(8,128)(2,1)S(1)} async-done(((bf16[8,144,512]{2,1,0:T(8,128)(2,1)}), bf16[8,144,512]{2,1,0:T(8,128)(2,1)S(1)}, u32[]{:S(2)}, u32[]{:S(2)}) %all-to-all-start) | async-done | bytes 1179680 | tf_op jit(solution)/shard_map/all_to_all | solution.py:34
  62.4 0.1 select_n.38
  62.5 0.1 copy.55
  62.6 0.2 reshape.169.src_ref
  62.8 0.1 slice.27
  62.8 33.5 %all-gather.2.cloned.1.call-done.all_ref = bf16[2048,512]{1,0:T(8,128)(2,1)} async-done(((bf16[128,512]{1,0:T(8,128)(2,1)}), bf16[2048,512]{1,0:T(8,128)(2,1)}) %all-gather.2.cloned.1.call-update) | async-done | bytes 2097168 | tf_op jit(solution)/shard_map/all_gather | solution.py:314
  96.3 5.6 %similar_parts.1 = (bf16[16,256,512]{2,1,0:T(8,128)(2,1)}, f32[32,128]{1,0:T(8,128)S(1)}) custom-call(bf16[2048,512]{1,0:T(8,128)(2,1)} %all-gather.2.cloned.1.call-done.all_ref, bf16[1024,512]{1,0:T(8,128)(2,1)S(1)} %bitcast.30, s32[16,256]{1,0:T(8,128)S(1)} %reshape.169.src_ref, s32[32,128]{1,0:T(8,128)S(1)} %bitcast.33), custom_call_target="tpu_custom_call" | custom-call | tf_op jit(solution)/shard_map/similar_parts/pallas_call | solution.py:125
  101.9 8.2 %all_to_all.35.sims_ref.chosen_ref = f32[4,96,128]{2,1,0:T(8,128)S(1)} all-to-all(f32[4,96,128]{2,1,0:T(8,128)S(1)} %pad_maximum_fusion.1), channel_id=1, replica_groups=mesh['y'=4,'z'=8,'half'=2,'core'=2,'x'=4] {'x'}, dimensions={0} | all-to-all | bytes 393216 | tf_op jit(solution)/shard_map/all_to_all | solution.py:34
  110.1 5.0 %weighted_sums.1 = s16[8,144,512]{2,1,0:T(8,128)(2,1)S(1)} custom-call(bf16[16,256,512]{2,1,0:T(8,128)(2,1)} %get-tuple-element.18.got_ref, f32[4,96,128]{2,1,0:T(8,128)S(1)} %all_to_all.35.sims_ref.chosen_ref, s32[32,128]{1,0:T(8,128)S(1)} %bitcast.34), custom_call_target="tpu_custom_call" | custom-call | tf_op jit(solution)/shard_map/weighted_sums/pallas_call | solution.py:184
  115.1 0.0 copy-start.1
  115.1 19.5 %all_to_all.36.parts_ref = s16[8,144,512]{2,1,0:T(8,128)(2,1)S(1)} all-to-all(s16[8,144,512]{2,1,0:T(8,128)(2,1)S(1)} %weighted_sums.1), channel_id=1, replica_groups=mesh['y'=4,'z'=8,'half'=2,'core'=2,'x'=4] {'y','half'}, dimensions={0} | all-to-all | bytes 2359296 | tf_op jit(solution)/shard_map/all_to_all | solution.py:34
  134.6 0.0 copy-done.1
  134.6 0.7 score_parts.1
  135.3 6.7 %all_to_all.37 = f32[4,24,128]{2,1,0:T(8,128)S(1)} all-to-all(f32[4,24,128]{2,1,0:T(8,128)S(1)} %get-tuple-element.22), channel_id=1, replica_groups=mesh['y'=4,'z'=8,'half'=2,'core'=2,'x'=4] {'x'}, dimensions={0} | all-to-all | bytes 98304 | tf_op jit(solution)/shard_map/all_to_all | solution.py:34
  142.1 18.8 %all_to_all.38 = f32[16,16,128]{2,1,0:T(8,128)S(1)} all-to-all(f32[16,16,128]{2,1,0:T(8,128)S(1)} %broadcast_in_dim.23), channel_id=1, replica_groups=mesh['y'=4,'z'=8,'half'=2,'core'=2,'x'=4] {'z','half'}, dimensions={0} | all-to-all | bytes 262144 | tf_op jit(solution)/shard_map/all_to_all | solution.py:34
  161.0 9.3 %all_to_all.39 = f32[4,16,16,128]{3,2,1,0:T(8,128)S(1)} all-to-all(f32[4,16,16,128]{3,2,1,0:T(8,128)S(1)} %broadcast_in_dim.24), channel_id=1, replica_groups=mesh['y'=4,'z'=8,'half'=2,'core'=2,'x'=4] {'y'}, dimensions={0} | all-to-all | bytes 1048576 | tf_op jit(solution)/shard_map/all_to_all | solution.py:34
  170.4 8.6 %collective-permute-start = (f32[1024,128]{1,0:T(8,128)S(1)}, f32[1024,128]{1,0:T(8,128)S(1)}, u32[]{:S(2)}, u32[]{:S(2)}) collective-permute-start(f32[1024,128]{1,0:T(8,128)S(1)} %bitcast.31), channel_id=1, source_target_pairs={{0,4},{4,0},{1,5},{5,1},{2,6},{6,2},{3,7},{7,3},{8,12},{12,8},{9,1... | collective-permute-start | bytes 1572872 | tf_op jit(solution)/shard_map/ppermute | solution.py:329
  179.0 0.7 multiply_convert_fusion
  179.7 0.8 collective-permute-done.far_ref
  180.5 2.4 %pick_scores.1 = f32[256,256]{1,0:T(8,128)} custom-call(s32[512]{0:T(512)S(1)} %multiply_add_fusion.rows_ref, f32[1024,128]{1,0:T(8,128)S(1)} %bitcast.32, f32[1024,128]{1,0:T(8,128)S(1)} %collective-permute-done.far_ref), custom_call_target="tpu_custom_call" | custom-call | tf_op jit(solution)/shard_map/pick_scores/pallas_call | solution.py:256
  (28 shorter events, 0.3 us)
Async XLA Ops:
  7.2 40.4 %copy-start = (bf16[256,2048]{1,0:T(8,128)(2,1)S(1)}, bf16[256,2048]{1,0:T(8,128)(2,1)}, u32[]{:S(2)}) copy-start(bf16[256,2048]{1,0:T(8,128)(2,1)} %param.8) | copy-start | bytes 3145732
  13.0 28.4 %all-to-all-start.1 = ((s32[16,1,128]{2,1,0:T(1,128)}), s32[16,1,128]{2,1,0:T(1,128)S(1)}, u32[]{:S(2)}, u32[]{:S(2)}) async-start(s32[16,1,128]{2,1,0:T(1,128)} %bitcast.5), calls=%async_computation.1 | async-start | bytes 16384 | tf_op jit(solution)/shard_map/all_to_all | solution.py:34
  31.7 15.0 %copy-start.2 = (s32[256,2]{0,1:T(2,128)S(1)}, s32[256,2]{0,1:T(2,128)}, u32[]{:S(2)}) copy-start(s32[256,2]{0,1:T(2,128)} %param.9) | copy-start | bytes 6148
  41.4 20.9 %all-to-all-start = ((bf16[8,144,512]{2,1,0:T(8,128)(2,1)}), bf16[8,144,512]{2,1,0:T(8,128)(2,1)S(1)}, u32[]{:S(2)}, u32[]{:S(2)}) async-start(bf16[8,144,512]{2,1,0:T(8,128)(2,1)} %pad_maximum_fusion), calls=%async_computation | async-start | bytes 2359296 | tf_op jit(solution)/shard_map/all_to_all | solution.py:34
  46.0 50.4 %all-gather.2.cloned.1.call-start = ((), (), s32[]{:S(2)}) async-start(), calls=%async_computation.7 | async-start | bytes 2228224 | tf_op jit(solution)/shard_map/all_gather | solution.py:314
  115.1 19.5 %copy-start.1 = (bf16[128,512]{1,0:T(8,128)(2,1)S(1)}, bf16[128,512]{1,0:T(8,128)(2,1)}, u32[]{:S(2)}) copy-start(bf16[128,512]{1,0:T(8,128)(2,1)} %own_ref.1) | copy-start | bytes 393220
  170.4 10.1 %collective-permute-start = (f32[1024,128]{1,0:T(8,128)S(1)}, f32[1024,128]{1,0:T(8,128)S(1)}, u32[]{:S(2)}, u32[]{:S(2)}) collective-permute-start(f32[1024,128]{1,0:T(8,128)S(1)} %bitcast.31), channel_id=1, source_target_pairs={{0,4},{4,0},{1,5},{5,1},{2,6},{6,2},{3,7},{7,3},{8,12},{12,8},{9,1... | collective-permute-start | bytes 1572872 | tf_op jit(solution)/shard_map/ppermute | solution.py:329
Sparse Core Ops, SparseCore 0:
  48.9 47.3 all-gather.1

commit v5 on v4

--- a/solution.py
+++ b/solution.py
@@ -264,18 +264,13 @@
     )(rows, near, far)
 
 
-def own_and_orders(descriptors, high, low, ys, halves):
-    rows, width = descriptors.shape
+def slot_orders(high, low, ys, halves):
     shards = 2 * ys
     count = halves * CORES
     groups = count // GROUP
-    codes = jnp.concatenate([high.reshape(shards, -1), low.reshape(shards, -1)], axis=1).astype(bf16)
-    codes = jnp.pad(codes, ((0, 0), (0, width - codes.shape[1])))
-    codes = jnp.broadcast_to(codes[:, None, :], (shards, PLACES, width))
-    sent = jnp.concatenate([jnp.broadcast_to(descriptors[None], (shards, rows, width)), codes], axis=1)
-    came = exchange(sent, ("y", "half"))
-    own = came[:, :rows, :].reshape(shards * rows, width)
-    codes = came[:, rows, : 2 * groups * LANES].astype(i32).reshape(shards, 2, groups, LANES)
+    codes = jnp.concatenate([high.reshape(shards, -1), low.reshape(shards, -1)], axis=1)
+    codes = exchange(codes.astype(i32).reshape(shards, 2 * groups, LANES), ("y", "half"))
+    codes = codes.reshape(shards, 2, groups, LANES)
     ahead_own = codes[:, 0] - 1
     ahead_src = jnp.where(ahead_own >= 0, lax.shift_right_logical(codes[:, 1], 1), -1)
     back = jnp.where(high > 0, (high - 1) * 256 + low, -1).astype(i32)
@@ -287,7 +282,7 @@
     source = jnp.stack([ahead_src.reshape(shards, count, PLACES).transpose(1, 0, 2), back_src], axis=2)
     at = jnp.stack([ahead_own, back_own.transpose(1, 0, 2).reshape(shards, groups, LANES)], axis=1)
     at = at.reshape(2 * shards, groups, LANES).transpose(1, 0, 2).reshape(groups * 2 * shards, LANES)
-    return own, source.reshape(count, 2 * shards * PLACES), at
+    return source.reshape(count, 2 * shards * PLACES), at
 
 
 def query_entries(queries, candidates, xs, zs):
@@ -312,8 +307,13 @@
     zs = 2 * halves
     rows, width = descriptors.shape
     everything = lax.all_gather(descriptors, ("z", "core"), axis=0, tiled=True)
+    near = spread(descriptors, "y", ys)
+    far = lax.ppermute(near, "half", [(0, 1), (1, 0)])
+    first = lax.axis_index("half") == 0
+    own = jnp.stack([jnp.where(first, near, far), jnp.where(first, far, near)], axis=1)
+    own = own.reshape(2 * ys * rows, width)
     high, low = build_table(neighbours, owned, ys * zs * CORES, halves)
-    own, source, at = own_and_orders(descriptors, high, low, ys, halves)
+    source, at = slot_orders(high, low, ys, halves)
     chosen, score_rows = query_entries(queries, candidates, xs, zs)
     source, at, own, chosen, score_rows = lax.optimization_barrier((source, at, own, chosen, score_rows))
     got, sims = similar_parts(everything, own, source, at)

time: 190 us -> 168 us (0.88)
  waiting for transfers between devices: 58.5 us -> 26.8 us
  starting transfers between devices: 29.9 us -> 37.8 us
    all_gather x1, waiting for transfers between devices: 33.5 us -> 2.04 us  [per_device(): everything = lax.all_gather(descriptors, ('z', 'core'), axis=0, tiled=True)]
    all_to_all x2 -> x3, starting transfers between devices: 21.2 us -> 26.4 us  [exchange(): return lax.all_to_all(parts, axis, split_axis=0, concat_axis=0, tiled=True)]
    ppermute x0 -> x1, starting transfers between devices: none -> 2.67 us  [per_device(): far = lax.ppermute(near, 'half', [(0, 1), (1, 0)])]
    all_to_all x2 -> x3, waiting for transfers between devices: 23.5 us -> 23.4 us  [exchange(): return lax.all_to_all(parts, axis, split_axis=0, concat_axis=0, tiled=True)]
  transfers between devices with their start and end apart: 4 -> 6, of which waited for: 4 -> 4; matrix products, arithmetic and copies ran while one was open for 3% -> 5% of each run, Pallas kernels for 0% -> 2%
where the time goes in v5:
time: 168 us
  blocking collectives  63.2 us (38%)
  starting transfers between devices  37.8 us (22%)
  waiting for transfers between devices  26.8 us (16%)
  Pallas kernels  16.9 us (10%)
  between operations  14.3 us (9%)
  local copies, waits for them, and re-layouts  6.18 us (4%)
  other arithmetic  2.03 us (1%)
    all_to_all x5, blocking collectives, exchange(): return lax.all_to_all(parts, axis, split_axis=0, concat_axis=0, tiled=True)  63.2 us
    all_to_all x3, starting transfers between devices, exchange(): return lax.all_to_all(parts, axis, split_axis=0, concat_axis=0, tiled=True)  26.4 us
    all_to_all x3, waiting for transfers between devices, exchange(): return lax.all_to_all(parts, axis, split_axis=0, concat_axis=0, tiled=True)  23.4 us
    ppermute x1, starting transfers between devices, per_device(): far = lax.ppermute(near, 'core', [(0, 1), (1, 0)])  8.71 us
    pallas_call x1, Pallas kernels, similar_parts(): pl.pallas_call(functools.partial(similar_kernel, per), grid=(groups // pe...  5.61 us
    pallas_call x1, Pallas kernels, weighted_sums(): pl.pallas_call(sum_kernel, in_specs=[pl.BlockSpec(memory_space=HBM), vmem...  4.97 us
  transfers between devices with their start and end apart: 6, of which 4 were waited for; matrix products, arithmetic and copies ran while one was open for 5% of the time, Pallas kernels for 2%

profile of v5, /device:TPU:1, one launch (start us, length us, event | category | flops | bytes accessed | tf_op | source)
XLA Modules:
  0.0 167.6 jit_solution(11843327950008193284)
XLA Ops:
  7.2 0.0 copy-start
  7.2 0.0 copy-start.2
  7.2 0.0 all-gather.2.cloned.1.call-start
  7.2 0.7 all-gather.2.cloned.1.call-update
  7.9 1.7 %broadcast_in_dim.18 = bf16[4,128,512]{2,1,0:T(8,128)(2,1)} broadcast(bf16[128,512]{1,0:T(8,128)(2,1)} %own_ref.1), dimensions={1,2} | broadcast | bytes 655360 | tf_op jit(solution)/shard_map/broadcast_in_dim | solution.py:38
  9.7 5.0 %all-to-all-start.2 = ((bf16[4,128,512]{2,1,0:T(8,128)(2,1)}), bf16[4,128,512]{2,1,0:T(8,128)(2,1)S(1)}, u32[]{:S(2)}, u32[]{:S(2)}) async-start(bf16[4,128,512]{2,1,0:T(8,128)(2,1)} %broadcast_in_dim.18), calls=%async_computation.2 | async-start | bytes 1048576 | tf_op jit(solution)/shard_map/all_to_all | solution.py:34
  14.7 0.8 copy.53.listed_ref
  15.5 0.8 copy.54.owned_ref
  16.3 0.8 copy.65
  17.1 0.1 eq.60
  17.3 3.3 %slot_table.1 = (f32[16,128]{1,0:T(8,128)S(1)}, f32[16,128]{1,0:T(8,128)S(1)}) custom-call(s32[128,10]{1,0:T(8,128)S(1)} %copy.53.listed_ref, s32[128,10]{1,0:T(8,128)S(1)} %copy.54.owned_ref), custom_call_target="tpu_custom_call" | custom-call | tf_op jit(solution)/shard_map/slot_table/pallas_call | solution.py:83
  20.5 0.3 convert_reduce_fusion
  20.8 0.0 copy-done.2
  20.8 0.1 eq.64
  21.0 0.1 reshape.153
  21.1 0.7 reshape.154
  21.8 0.1 copy.66
  21.9 0.0 copy-done
  21.9 0.3 fusion.10
  22.2 0.0 all-to-all-done.2
  22.2 18.1 %all-to-all-start.1 = ((s32[16,1,128]{2,1,0:T(1,128)}), s32[16,1,128]{2,1,0:T(1,128)S(1)}, u32[]{:S(2)}, u32[]{:S(2)}) async-start(s32[16,1,128]{2,1,0:T(1,128)} %bitcast.6), calls=%async_computation.1 | async-start | bytes 16384 | tf_op jit(solution)/shard_map/all_to_all | solution.py:34
  40.2 0.6 maximum_convert_fusion
  40.8 0.1 reshape.159
  41.0 2.7 %collective-permute-start = (bf16[4,128,512]{2,1,0:T(8,128)(2,1)S(1)}, bf16[4,128,512]{2,1,0:T(8,128)(2,1)S(1)}, u32[]{:S(2)}, u32[]{:S(2)}) collective-permute-start(bf16[4,128,512]{2,1,0:T(8,128)(2,1)S(1)} %all-to-all-done.2), channel_id=1, source_target_pairs={{0,8},{8,0},{1,9},{9,1},{2,10},{10,2},{3,11},{11,3},{4,12},{12,4},... | collective-permute-start | bytes 1572872 | tf_op jit(solution)/shard_map/ppermute | solution.py:311
  43.7 9.0 %all-to-all-done.1 = s32[16,1,128]{2,1,0:T(1,128)S(1)} async-done(((s32[16,1,128]{2,1,0:T(1,128)}), s32[16,1,128]{2,1,0:T(1,128)S(1)}, u32[]{:S(2)}, u32[]{:S(2)}) %all-to-all-start.1) | async-done | bytes 8224 | tf_op jit(solution)/shard_map/all_to_all | solution.py:34
  52.6 3.3 %all-to-all-start = ((s32[8,4,128]{2,1,0:T(4,128)}), s32[8,4,128]{2,1,0:T(4,128)S(1)}, u32[]{:S(2)}, u32[]{:S(2)}) async-start(s32[8,4,128]{2,1,0:T(4,128)} %maximum_convert_fusion), calls=%async_computation | async-start | bytes 32768 | tf_op jit(solution)/shard_map/all_to_all | solution.py:34
  56.0 0.1 select_reduce_fusion
  56.1 0.1 select_n.55
  56.2 0.1 stack_reshape.3
  56.3 0.1 select_n.53
  56.4 14.4 %all-to-all-done = s32[8,4,128]{2,1,0:T(4,128)S(1)} async-done(((s32[8,4,128]{2,1,0:T(4,128)}), s32[8,4,128]{2,1,0:T(4,128)S(1)}, u32[]{:S(2)}, u32[]{:S(2)}) %all-to-all-start) | async-done | bytes 16416 | tf_op jit(solution)/shard_map/all_to_all | solution.py:34
  70.8 0.1 select_n.50
  70.9 0.1 copy.60
  71.0 0.2 reshape.155.src_ref
  71.2 0.0 collective-permute-done
  71.2 0.1 select_bitcast_fusion.1
  71.3 0.1 pad_maximum_fusion
  71.5 2.0 %all-gather.2.cloned.1.call-done.all_ref = bf16[2048,512]{1,0:T(8,128)(2,1)} async-done(((bf16[128,512]{1,0:T(8,128)(2,1)}), bf16[2048,512]{1,0:T(8,128)(2,1)}) %all-gather.2.cloned.1.call-update) | async-done | bytes 2097168 | tf_op jit(solution)/shard_map/all_gather | solution.py:309
  73.5 5.6 %similar_parts.1 = (bf16[16,256,512]{2,1,0:T(8,128)(2,1)}, f32[32,128]{1,0:T(8,128)S(1)}) custom-call(bf16[2048,512]{1,0:T(8,128)(2,1)} %all-gather.2.cloned.1.call-done.all_ref, bf16[1024,512]{1,0:T(8,128)(2,1)S(1)} %bitcast.37, s32[16,256]{1,0:T(8,128)S(1)} %reshape.155.src_ref, s32[32,128]{1,0:T(8,128)S(1)} %bitcast.40), custom_call_target="tpu_custom_call" | custom-call | tf_op jit(solution)/shard_map/similar_parts/pallas_call | solution.py:125
  79.1 7.7 %all_to_all.40.sims_ref.chosen_ref = f32[4,96,128]{2,1,0:T(8,128)S(1)} all-to-all(f32[4,96,128]{2,1,0:T(8,128)S(1)} %pad_maximum_fusion.1), channel_id=1, replica_groups=mesh['y'=4,'z'=8,'half'=2,'core'=2,'x'=4] {'x'}, dimensions={0} | all-to-all | bytes 393216 | tf_op jit(solution)/shard_map/all_to_all | solution.py:34
  86.8 5.0 %weighted_sums.1 = s16[8,144,512]{2,1,0:T(8,128)(2,1)S(1)} custom-call(bf16[16,256,512]{2,1,0:T(8,128)(2,1)} %get-tuple-element.18.got_ref, f32[4,96,128]{2,1,0:T(8,128)S(1)} %all_to_all.40.sims_ref.chosen_ref, s32[32,128]{1,0:T(8,128)S(1)} %bitcast.41), custom_call_target="tpu_custom_call" | custom-call | tf_op jit(solution)/shard_map/weighted_sums/pallas_call | solution.py:184
  91.7 0.0 copy-start.1
  91.8 19.7 %all_to_all.41.parts_ref = s16[8,144,512]{2,1,0:T(8,128)(2,1)S(1)} all-to-all(s16[8,144,512]{2,1,0:T(8,128)(2,1)S(1)} %weighted_sums.1), channel_id=1, replica_groups=mesh['y'=4,'z'=8,'half'=2,'core'=2,'x'=4] {'y','half'}, dimensions={0} | all-to-all | bytes 2359296 | tf_op jit(solution)/shard_map/all_to_all | solution.py:34
  111.4 0.0 copy-done.1
  111.4 0.7 score_parts.1
  112.1 6.7 %all_to_all.42 = f32[4,24,128]{2,1,0:T(8,128)S(1)} all-to-all(f32[4,24,128]{2,1,0:T(8,128)S(1)} %get-tuple-element.22), channel_id=1, replica_groups=mesh['y'=4,'z'=8,'half'=2,'core'=2,'x'=4] {'x'}, dimensions={0} | all-to-all | bytes 98304 | tf_op jit(solution)/shard_map/all_to_all | solution.py:34
  118.9 19.8 %all_to_all.43 = f32[16,16,128]{2,1,0:T(8,128)S(1)} all-to-all(f32[16,16,128]{2,1,0:T(8,128)S(1)} %broadcast_in_dim.20), channel_id=1, replica_groups=mesh['y'=4,'z'=8,'half'=2,'core'=2,'x'=4] {'z','half'}, dimensions={0} | all-to-all | bytes 262144 | tf_op jit(solution)/shard_map/all_to_all | solution.py:34
  138.8 9.3 %all_to_all.44 = f32[4,16,16,128]{3,2,1,0:T(8,128)S(1)} all-to-all(f32[4,16,16,128]{3,2,1,0:T(8,128)S(1)} %broadcast_in_dim.21), channel_id=1, replica_groups=mesh['y'=4,'z'=8,'half'=2,'core'=2,'x'=4] {'y'}, dimensions={0} | all-to-all | bytes 1048576 | tf_op jit(solution)/shard_map/all_to_all | solution.py:34
  148.1 8.7 %collective-permute-start.1 = (f32[1024,128]{1,0:T(8,128)S(1)}, f32[1024,128]{1,0:T(8,128)S(1)}, u32[]{:S(2)}, u32[]{:S(2)}) collective-permute-start(f32[1024,128]{1,0:T(8,128)S(1)} %bitcast.38), channel_id=1, source_target_pairs={{0,4},{4,0},{1,5},{5,1},{2,6},{6,2},{3,7},{7,3},{8,12},{12,8},{9,1... | collective-permute-start | bytes 1572872 | tf_op jit(solution)/shard_map/ppermute | solution.py:329
  156.8 0.7 multiply_convert_fusion
  157.6 0.8 collective-permute-done.1.far_ref
  158.3 2.4 %pick_scores.1 = f32[256,256]{1,0:T(8,128)} custom-call(s32[512]{0:T(512)S(1)} %multiply_add_fusion.rows_ref, f32[1024,128]{1,0:T(8,128)S(1)} %bitcast.39, f32[1024,128]{1,0:T(8,128)S(1)} %collective-permute-done.1.far_ref), custom_call_target="tpu_custom_call" | custom-call | tf_op jit(solution)/shard_map/pick_scores/pallas_call | solution.py:256
  (22 shorter events, 0.3 us)
Async XLA Ops:
  7.2 14.7 %copy-start = (bf16[256,2048]{1,0:T(8,128)(2,1)S(1)}, bf16[256,2048]{1,0:T(8,128)(2,1)}, u32[]{:S(2)}) copy-start(bf16[256,2048]{1,0:T(8,128)(2,1)} %param.8) | copy-start | bytes 3145732
  7.2 13.6 %copy-start.2 = (s32[256,2]{0,1:T(2,128)S(1)}, s32[256,2]{0,1:T(2,128)}, u32[]{:S(2)}) copy-start(s32[256,2]{0,1:T(2,128)} %param.9) | copy-start | bytes 6148
  7.2 66.3 %all-gather.2.cloned.1.call-start = ((), (), s32[]{:S(2)}) async-start(), calls=%async_computation.8 | async-start | bytes 2228224 | tf_op jit(solution)/shard_map/all_gather | solution.py:309
  9.7 12.5 %all-to-all-start.2 = ((bf16[4,128,512]{2,1,0:T(8,128)(2,1)}), bf16[4,128,512]{2,1,0:T(8,128)(2,1)S(1)}, u32[]{:S(2)}, u32[]{:S(2)}) async-start(bf16[4,128,512]{2,1,0:T(8,128)(2,1)} %broadcast_in_dim.18), calls=%async_computation.2 | async-start | bytes 1048576 | tf_op jit(solution)/shard_map/all_to_all | solution.py:34
  22.2 30.5 %all-to-all-start.1 = ((s32[16,1,128]{2,1,0:T(1,128)}), s32[16,1,128]{2,1,0:T(1,128)S(1)}, u32[]{:S(2)}, u32[]{:S(2)}) async-start(s32[16,1,128]{2,1,0:T(1,128)} %bitcast.6), calls=%async_computation.1 | async-start | bytes 16384 | tf_op jit(solution)/shard_map/all_to_all | solution.py:34
  41.0 30.2 %collective-permute-start = (bf16[4,128,512]{2,1,0:T(8,128)(2,1)S(1)}, bf16[4,128,512]{2,1,0:T(8,128)(2,1)S(1)}, u32[]{:S(2)}, u32[]{:S(2)}) collective-permute-start(bf16[4,128,512]{2,1,0:T(8,128)(2,1)S(1)} %all-to-all-done.2), channel_id=1, source_target_pairs={{0,8},{8,0},{1,9},{9,1},{2,10},{10,2},{3,11},{11,3},{4,12},{12,4},... | collective-permute-start | bytes 1572872 | tf_op jit(solution)/shard_map/ppermute | solution.py:311
  52.6 18.1 %all-to-all-start = ((s32[8,4,128]{2,1,0:T(4,128)}), s32[8,4,128]{2,1,0:T(4,128)S(1)}, u32[]{:S(2)}, u32[]{:S(2)}) async-start(s32[8,4,128]{2,1,0:T(4,128)} %maximum_convert_fusion), calls=%async_computation | async-start | bytes 32768 | tf_op jit(solution)/shard_map/all_to_all | solution.py:34
  91.7 19.7 %copy-start.1 = (bf16[128,512]{1,0:T(8,128)(2,1)S(1)}, bf16[128,512]{1,0:T(8,128)(2,1)}, u32[]{:S(2)}) copy-start(bf16[128,512]{1,0:T(8,128)(2,1)} %own_ref.1) | copy-start | bytes 393220
  148.1 10.2 %collective-permute-start.1 = (f32[1024,128]{1,0:T(8,128)S(1)}, f32[1024,128]{1,0:T(8,128)S(1)}, u32[]{:S(2)}, u32[]{:S(2)}) collective-permute-start(f32[1024,128]{1,0:T(8,128)S(1)} %bitcast.38), channel_id=1, source_target_pairs={{0,4},{4,0},{1,5},{5,1},{2,6},{6,2},{3,7},{7,3},{8,12},{12,8},{9,1... | collective-permute-start | bytes 1572872 | tf_op jit(solution)/shard_map/ppermute | solution.py:329
Sparse Core Ops, SparseCore 0:
  10.1 63.2 all-gather.1

commit v6 on v5

--- a/solution.py
+++ b/solution.py
@@ -18,7 +18,9 @@
 SHARD = ("y", "z", "half", "core")
 VMEM = 48 * 1024 * 1024
 INTERPRET = False
-STEPS = 2
+SPLIT = 1
+LEAVE = 2
+JOIN = 4
 HBM = pltpu.HBM
 f32 = jnp.float32
 bf16 = jnp.bfloat16
@@ -89,23 +91,31 @@
     )(neighbours, owned)
 
 
-def similar_kernel(groups, all_ref, own_ref, src_ref, at_ref, got_ref, sims_ref):
+def similar_kernel(all_ref, own_ref, src_ref, at_ref, got_ref, sims_ref, held_ref, out_ref, in_sems, out_sems):
     shards = own_ref.shape[0] // BLOCK
     kinds = 2 * shards
     slots = kinds * PLACES
+    groups = src_ref.shape[0] // GROUP
+    arrivals, departures = [], []
+    for part in range(groups * SPLIT):
+        rows = pl.ds(part * (GROUP // SPLIT) * BLOCK, GROUP // SPLIT * BLOCK)
+        arrivals.append(pltpu.make_async_copy(all_ref.at[rows], held_ref.at[rows], in_sems.at[part]))
+        arrivals[-1].start()
     row = lax.broadcasted_iota(i32, (BLOCK, slots), 0)
     for group in range(groups):
         parts = []
         for one in range(group * GROUP, (group + 1) * GROUP):
             pick = jnp.where(row == src_ref[one : one + 1, :], 1.0, 0.0).astype(bf16)
-            block = all_ref[one * BLOCK : (one + 1) * BLOCK, :]
+            if one % (GROUP // SPLIT) == 0:
+                arrivals[one // (GROUP // SPLIT)].wait()
+            block = held_ref[one * BLOCK : (one + 1) * BLOCK, :]
             parts.append(lax.dot_general(pick, block, TN, preferred_element_type=f32).astype(bf16))
         sims = []
         for shard in range(shards):
             chunks = []
             for k in (2 * shard, 2 * shard + 1):
                 chunk = jnp.concatenate([part[k * PLACES : (k + 1) * PLACES] for part in parts], axis=0)
-                got_ref[k, group * LANES : (group + 1) * LANES, :] = chunk
+                out_ref[group, k] = chunk
                 chunks.append(chunk)
             own = own_ref[shard * BLOCK : (shard + 1) * BLOCK, :]
             dots = lax.dot_general(own, jnp.concatenate(chunks, axis=0), NT, preferred_element_type=f32)
@@ -114,30 +124,33 @@
                 here = row[:, :LANES] == at_ref[n : n + 1, :]
                 held = jnp.where(here, dots[:, kind * LANES : (kind + 1) * LANES], 0.0)
                 sims.append(jnp.sum(held, axis=0, keepdims=True))
+            if (shard + 1) % LEAVE == 0:
+                some = pl.ds(2 * (shard + 1 - LEAVE), 2 * LEAVE)
+                sem = out_sems.at[len(departures)]
+                departures.append(pltpu.make_async_copy(out_ref.at[group, some], got_ref.at[group, some], sem))
+                departures[-1].start()
         sims_ref[group * kinds : (group + 1) * kinds, :] = jnp.concatenate(sims, axis=0)
-
-
-def similar_parts(everything, own, source, at, steps=STEPS):
+    for departure in departures:
+        departure.wait()
+
+
+def similar_parts(everything, own, source, at):
     width = own.shape[1]
     groups = everything.shape[0] // BLOCK // GROUP
-    per = max(groups // steps, 1)
     kinds = 2 * own.shape[0] // BLOCK
-    return pl.pallas_call(
-        functools.partial(similar_kernel, per),
-        grid=(groups // per,),
-        in_specs=[
-            pl.BlockSpec((per * GROUP * BLOCK, width), lambda i: (i, 0)),
-            pl.BlockSpec(own.shape, lambda i: (0, 0)),
-            pl.BlockSpec((per * GROUP, kinds * PLACES), lambda i: (i, 0)),
-            pl.BlockSpec((per * kinds, LANES), lambda i: (i, 0)),
-        ],
-        out_specs=[
-            pl.BlockSpec((kinds, per * LANES, width), lambda i: (0, i, 0)),
-            pl.BlockSpec((per * kinds, LANES), lambda i: (i, 0)),
-        ],
-        out_shape=[
-            hbm((kinds, groups * LANES, width), bf16),
-            jax.ShapeDtypeStruct((groups * kinds, LANES), f32),
+    vmem = pl.BlockSpec(memory_space=pltpu.VMEM)
+    outside = pl.BlockSpec(memory_space=HBM)
+    shape = (groups, kinds, LANES, width)
+    return pl.pallas_call(
+        similar_kernel,
+        in_specs=[outside, vmem, vmem, vmem],
+        out_specs=[outside, vmem],
+        out_shape=[hbm(shape, bf16), jax.ShapeDtypeStruct((groups * kinds, LANES), f32)],
+        scratch_shapes=[
+            pltpu.VMEM(everything.shape, bf16),
+            pltpu.VMEM(shape, bf16),
+            pltpu.SemaphoreType.DMA((groups * SPLIT,)),
+            pltpu.SemaphoreType.DMA((groups * kinds // 2 // LEAVE,)),
         ],
         compiler_params=params(),
         interpret=INTERPRET,
@@ -148,9 +161,9 @@
 def sum_kernel(got_ref, sims_ref, at_ref, sum_ref, held_ref, sems):
     shards = sum_ref.shape[0]
     copies = []
-    for shard in range(shards):
-        pair = slice(2 * shard, 2 * shard + 2)
-        copies.append(pltpu.make_async_copy(got_ref.at[pair], held_ref.at[pair], sems.at[shard]))
+    for some in range(shards // JOIN):
+        kinds = pl.ds(2 * JOIN * some, 2 * JOIN)
+        copies.append(pltpu.make_async_copy(got_ref.at[:, kinds], held_ref.at[:, kinds], sems.at[some]))
         copies[-1].start()
     row = lax.broadcasted_iota(i32, (BLOCK, LANES), 0)
     similar = jnp.sum(sims_ref[:, : at_ref.shape[0], :], axis=0) / D
@@ -166,8 +179,10 @@
                 here = row == at_ref[n : n + 1, :]
                 left_high.append(jnp.where(here, high[n : n + 1], 0.0).astype(bf16))
                 left_low.append(jnp.where(here, low[n : n + 1], 0.0).astype(bf16))
-        copies[shard].wait()
-        right = jnp.concatenate([held_ref[2 * shard], held_ref[2 * shard + 1]], axis=0)
+        if shard % JOIN == 0:
+            copies[shard // JOIN].wait()
+        pair = (2 * shard, 2 * shard + 1)
+        right = jnp.concatenate([held_ref[group, k] for k in pair for group in range(groups)], axis=0)
         total = jnp.dot(jnp.concatenate(left_high, axis=1), right, preferred_element_type=f32)
         total += jnp.dot(jnp.concatenate(left_low, axis=1), right, preferred_element_type=f32)
         peak = jnp.maximum(jnp.max(jnp.abs(total), axis=1, keepdims=True), 1e-30)
@@ -179,14 +194,14 @@
 
 
 def weighted_sums(got, sims, at):
-    kinds, slots, width = got.shape
+    kinds, width = got.shape[1], got.shape[3]
     vmem = pl.BlockSpec(memory_space=pltpu.VMEM)
     return pl.pallas_call(
         sum_kernel,
         in_specs=[pl.BlockSpec(memory_space=HBM), vmem, vmem],
         out_specs=vmem,
         out_shape=jax.ShapeDtypeStruct((kinds // 2, BLOCK + PLACES, width), i16),
-        scratch_shapes=[pltpu.VMEM(got.shape, bf16), pltpu.SemaphoreType.DMA((kinds // 2,))],
+        scratch_shapes=[pltpu.VMEM(got.shape, bf16), pltpu.SemaphoreType.DMA((kinds // 2 // JOIN,))],
         compiler_params=params(),
         interpret=INTERPRET,
         name="weighted_sums",
@@ -205,7 +220,7 @@
     energy = jnp.broadcast_to(energy, (BLOCK, LANES)).T[:8]
     high = total.astype(bf16)
     low = (total - high.astype(f32)).astype(bf16)
-    lanes = out_ref.shape[0]
+    lanes = chosen_ref.shape[0]
     quarters = total.shape[1] // LANES
     before = chosen_ref.shape[1] - quarters * PLACES
     scores = jnp.zeros((lanes * PLACES, LANES), f32)
@@ -215,17 +230,18 @@
         columns = slice(quarter * LANES, (quarter + 1) * LANES)
         scores += lax.dot_general(chosen, high[:, columns], NT, preferred_element_type=f32)
         scores += lax.dot_general(chosen, low[:, columns], NT, preferred_element_type=f32)
-    for lane in range(out_ref.shape[0]):
-        out_ref[lane, :PLACES, :] = scores[lane * PLACES : (lane + 1) * PLACES]
-        out_ref[lane, PLACES:, :] = energy
-
-
-def score_parts(parts, own, chosen, xs):
+    for place in range(out_ref.shape[0]):
+        lane = place % lanes
+        out_ref[place, :PLACES, :] = scores[lane * PLACES : (lane + 1) * PLACES]
+        out_ref[place, PLACES:, :] = energy
+
+
+def score_parts(parts, own, chosen, places):
     return pl.pallas_call(
         score_kernel,
         out_shape=[
             jax.ShapeDtypeStruct(own.shape, f32),
-            jax.ShapeDtypeStruct((xs, PLACES + 8, LANES), f32),
+            jax.ShapeDtypeStruct((places, PLACES + 8, LANES), f32),
         ],
         compiler_params=params(),
         interpret=INTERPRET,
@@ -233,31 +249,72 @@
     )(parts, own, chosen)
 
 
-def pick_kernel(rows_ref, near_ref, far_ref, out_ref):
-    count = near_ref.shape[0]
+def finish_kernel(depth, parts_ref, out_ref, scale_ref):
+    ys = scale_ref.shape[0]
+    lanes = parts_ref.shape[0] // ys
+    scores = []
+    for y in range(ys):
+        whole = parts_ref[y * lanes]
+        for lane in range(1, lanes):
+            whole += parts_ref[y * lanes + lane]
+        scale = lax.rsqrt(whole[PLACES:] / depth + 1e-06)
+        scale_ref[y] = scale
+        scores.append(whole[:PLACES] * (scale[:1] / math.sqrt(depth)))
+    scores = jnp.concatenate(scores, axis=0)
+    peak = jnp.max(jnp.max(jnp.abs(scores), axis=0, keepdims=True), axis=1, keepdims=True)
+    level = jnp.floor(jnp.log2(jnp.maximum(peak, 1e-30)) * STEPS_PER_OCTAVE) + 1.0
+    level = jnp.broadcast_to(level, (PLACES, LANES))
+    count = scores.shape[0]
+    scores = scores * (LEVELS / jnp.exp2(level[:1] / STEPS_PER_OCTAVE))
+    out_ref[:count, :] = jnp.floor(scores + 0.5).astype(i32).astype(i16)
+    out_ref[count:, :] = level.astype(i32).astype(i16)
+
+
+def finish_scores(parts, ys, depth):
+    return pl.pallas_call(
+        functools.partial(finish_kernel, depth),
+        out_shape=[
+            jax.ShapeDtypeStruct(((ys + 1) * PLACES, LANES), i16),
+            jax.ShapeDtypeStruct((ys, 8, LANES), f32),
+        ],
+        compiler_params=params(),
+        interpret=INTERPRET,
+        name="finish_scores",
+    )(parts)
+
+
+def pick_kernel(rows_ref, near_ref, far_ref, out_ref, table_ref):
+    planes, held, _ = near_ref.shape
+    count = held - PLACES
+    for side, ref in enumerate((near_ref, far_ref)):
+        for plane in range(planes):
+            level = ref[plane, count:, :].astype(i32).astype(f32)[:1]
+            scores = ref[plane, :count, :].astype(i32).astype(f32) * (jnp.exp2(level / STEPS_PER_OCTAVE) / LEVELS)
+            table_ref[(side * planes + plane) * count : (side * planes + plane + 1) * count, :] = scores
 
     def step(i, carry):
         for cand in range(2):
             picked = []
             for one in range(GROUP):
                 r = rows_ref[i * (2 * GROUP) + 2 * one + cand]
-                place = pl.ds(r & (count - 1), 1)
-                picked.append(jnp.where(r < count, near_ref[place, :], far_ref[place, :]))
+                picked.append(table_ref[pl.ds(r, 1), :])
             at = pl.ds(pl.multiple_of(i * GROUP, GROUP), GROUP)
             out_ref[at, cand * LANES : (cand + 1) * LANES] = jnp.concatenate(picked, axis=0)
         return carry
 
-    lax.fori_loop(0, out_ref.shape[0] // GROUP, step, 0, unroll=4)
+    lax.fori_loop(0, out_ref.shape[0] // GROUP, step, 0, unroll=8)
 
 
 def pick_scores(rows, near, far):
     queries = rows.shape[0] // 2
     vmem = pl.BlockSpec(memory_space=pltpu.VMEM)
+    planes, held, _ = near.shape
     return pl.pallas_call(
         pick_kernel,
         in_specs=[pl.BlockSpec(memory_space=pltpu.SMEM), vmem, vmem],
         out_specs=vmem,
         out_shape=jax.ShapeDtypeStruct((queries, 2 * LANES), f32),
+        scratch_shapes=[pltpu.VMEM((2 * planes * (held - PLACES), LANES), f32)],
         compiler_params=params(),
         interpret=INTERPRET,
         name="pick_scores",
@@ -285,7 +342,7 @@
     return source.reshape(count, 2 * shards * PLACES), at
 
 
-def query_entries(queries, candidates, xs, zs):
+def query_entries(queries, candidates, xs, ys, zs):
     flat = candidates.reshape(-1)
     order = jnp.arange(flat.shape[0], dtype=i32)
     earlier = (flat[:, None] == flat[None, :]) & (order[:, None] > order[None, :])
@@ -298,7 +355,8 @@
     plane = flat // CORES
     core = flat - plane * CORES
     far = (core != lax.axis_index("core")).astype(i32)
-    rows = (far * (GROUP // CORES * zs) + plane) * PLACES + rank
+    y = plane // zs
+    rows = ((far * zs + plane - y * zs) * ys + y) * PLACES + rank
     return chosen, rows
 
 
@@ -314,18 +372,17 @@
     own = own.reshape(2 * ys * rows, width)
     high, low = build_table(neighbours, owned, ys * zs * CORES, halves)
     source, at = slot_orders(high, low, ys, halves)
-    chosen, score_rows = query_entries(queries, candidates, xs, zs)
+    chosen, score_rows = query_entries(queries, candidates, xs, ys, zs)
     source, at, own, chosen, score_rows = lax.optimization_barrier((source, at, own, chosen, score_rows))
     got, sims = similar_parts(everything, own, source, at)
     sims = jnp.concatenate([jnp.broadcast_to(sims[None], (xs,) + sims.shape), chosen], axis=1)
     sims = exchange(sims, "x")
     parts = exchange(weighted_sums(got, sims, at), ("y", "half"))
-    summed, parts = score_parts(parts, descriptors, sims, xs)
-    whole = jnp.sum(exchange(parts, "x"), axis=0)
-    scale = lax.rsqrt(whole[PLACES] / (xs * width) + 1e-06)
+    summed, parts = score_parts(parts, descriptors, sims, ys * xs)
+    mine, scales = finish_scores(exchange(parts, ("y", "x")), ys, xs * width)
+    scale = lax.dynamic_index_in_dim(scales, lax.axis_index("y"), 0, keepdims=False)[0]
     augmented = (summed * scale[:, None]).astype(bf16)
-    mine = whole[:PLACES] * (scale / math.sqrt(xs * width))[None, :]
-    near = spread(spread(mine, ("z", "half"), zs), "y", ys).reshape(-1, rows)
+    near = spread(mine, ("z", "half"), zs)
     far = lax.ppermute(near, "core", [(0, 1), (1, 0)])
     return augmented, pick_scores(score_rows, near, far)
 

time: 168 us -> 163 us (0.970)
  blocking collectives: 63.2 us -> 37.3 us
  waiting for transfers between devices: 26.8 us -> 40 us
  starting transfers between devices: 37.8 us -> 47.4 us
  Pallas kernels: 16.9 us -> 14.3 us
    all_to_all x5 -> x3, blocking collectives: 63.2 us -> 37.3 us  [exchange(): return lax.all_to_all(parts, axis, split_axis=0, concat_axis=0, tiled=True)]
    all_to_all x3 -> x4, waiting for transfers between devices: 23.4 us -> 36.6 us  [exchange(): return lax.all_to_all(parts, axis, split_axis=0, concat_axis=0, tiled=True)]
    all_to_all x3 -> x4, starting transfers between devices: 26.4 us -> 34.4 us  [exchange(): return lax.all_to_all(parts, axis, split_axis=0, concat_axis=0, tiled=True)]
    pallas_call x1 -> x2, Pallas kernels: 5.61 us -> 5.01 us  [the longest x1 4.89 us: similar_parts(): pl.pallas_call(similar_kernel, in_specs=[outside, vmem, vmem, vmem], out_...]
  transfers between devices with their start and end apart: 6 -> 7, of which waited for: 4 -> 5; matrix products, arithmetic and copies ran while one was open for 5% -> 5% of each run, Pallas kernels for 2% -> 2%
where the time goes in v6:
time: 163 us; the launch traced here: 162 us
  starting transfers between devices  47.4 us (29%)
  waiting for transfers between devices  40 us (25%)
  blocking collectives  37.3 us (23%)
  between operations  14.4 us (9%)
  Pallas kernels  14.3 us (9%)
  local copies, waits for them, and re-layouts  6.91 us (4%)
  other arithmetic  2.02 us (1%)
    all_to_all x3, blocking collectives, exchange(): return lax.all_to_all(parts, axis, split_axis=0, concat_axis=0, tiled=True)  37.3 us
    all_to_all x4, waiting for transfers between devices, exchange(): return lax.all_to_all(parts, axis, split_axis=0, concat_axis=0, tiled=True)  36.6 us
    all_to_all x4, starting transfers between devices, exchange(): return lax.all_to_all(parts, axis, split_axis=0, concat_axis=0, tiled=True)  34.4 us
    ppermute x1, starting transfers between devices, per_device(): far = lax.ppermute(near, 'core', [(0, 1), (1, 0)])  10.4 us
    pallas_call x1, Pallas kernels, similar_parts(): pl.pallas_call(similar_kernel, in_specs=[outside, vmem, vmem, vmem], out_...  4.89 us
    pallas_call x1, Pallas kernels, weighted_sums(): pl.pallas_call(sum_kernel, in_specs=[pl.BlockSpec(memory_space=HBM), vmem...  3.43 us
    pallas_call x1, Pallas kernels, build_table(): pl.pallas_call(functools.partial(table_kernel, halves), out_shape=[jax.Sh...  3.26 us
  transfers between devices with their start and end apart: 7, of which 5 were waited for; matrix products, arithmetic and copies ran while one was open for 5% of the time, Pallas kernels for 2%

profile of v6, /device:TPU:1, one launch (start us, length us, event | category | flops | bytes accessed | tf_op | source)
XLA Modules:
  0.0 162.5 jit_solution(13782424145856806265)
XLA Ops:
  7.2 0.0 copy-start
  7.2 0.0 copy-start.2
  7.2 0.0 all-gather.2.cloned.1.call-start
  7.2 0.7 all-gather.2.cloned.1.call-update
  7.9 1.7 %broadcast_in_dim.16 = bf16[4,128,512]{2,1,0:T(8,128)(2,1)} broadcast(bf16[128,512]{1,0:T(8,128)(2,1)} %own_ref.1), dimensions={1,2} | broadcast | bytes 655360 | tf_op jit(solution)/shard_map/broadcast_in_dim | solution.py:40
  9.7 5.0 %all-to-all-start.2 = ((bf16[4,128,512]{2,1,0:T(8,128)(2,1)}), bf16[4,128,512]{2,1,0:T(8,128)(2,1)S(1)}, u32[]{:S(2)}, u32[]{:S(2)}) async-start(bf16[4,128,512]{2,1,0:T(8,128)(2,1)} %broadcast_in_dim.16), calls=%async_computation.2 | async-start | bytes 1048576 | tf_op jit(solution)/shard_map/all_to_all | solution.py:36
  14.7 0.8 copy.53.listed_ref
  15.5 0.8 copy.54.owned_ref
  16.3 0.8 copy.65
  17.1 0.1 eq.60
  17.3 3.3 %slot_table.1 = (f32[16,128]{1,0:T(8,128)S(1)}, f32[16,128]{1,0:T(8,128)S(1)}) custom-call(s32[128,10]{1,0:T(8,128)S(1)} %copy.53.listed_ref, s32[128,10]{1,0:T(8,128)S(1)} %copy.54.owned_ref), custom_call_target="tpu_custom_call" | custom-call | tf_op jit(solution)/shard_map/slot_table/pallas_call | solution.py:85
  20.5 0.3 convert_reduce_fusion
  20.8 0.0 copy-done.2
  20.9 0.1 eq.64
  21.0 0.1 reshape.140
  21.1 0.7 reshape.141
  21.8 0.1 copy.66
  21.9 0.0 copy-done
  21.9 0.3 fusion.9
  22.2 0.0 all-to-all-done.2
  22.2 18.0 %all-to-all-start.1 = ((s32[16,1,128]{2,1,0:T(1,128)}), s32[16,1,128]{2,1,0:T(1,128)S(1)}, u32[]{:S(2)}, u32[]{:S(2)}) async-start(s32[16,1,128]{2,1,0:T(1,128)} %bitcast.6), calls=%async_computation.1 | async-start | bytes 16384 | tf_op jit(solution)/shard_map/all_to_all | solution.py:36
  40.2 0.6 maximum_convert_fusion
  40.8 0.1 reshape.146
  41.0 2.7 %collective-permute-start = (bf16[4,128,512]{2,1,0:T(8,128)(2,1)S(1)}, bf16[4,128,512]{2,1,0:T(8,128)(2,1)S(1)}, u32[]{:S(2)}, u32[]{:S(2)}) collective-permute-start(bf16[4,128,512]{2,1,0:T(8,128)(2,1)S(1)} %all-to-all-done.2), channel_id=1, source_target_pairs={{0,8},{8,0},{1,9},{9,1},{2,10},{10,2},{3,11},{11,3},{4,12},{12,4},... | collective-permute-start | bytes 1572872 | tf_op jit(solution)/shard_map/ppermute | solution.py:369
  43.7 9.0 %all-to-all-done.1 = s32[16,1,128]{2,1,0:T(1,128)S(1)} async-done(((s32[16,1,128]{2,1,0:T(1,128)}), s32[16,1,128]{2,1,0:T(1,128)S(1)}, u32[]{:S(2)}, u32[]{:S(2)}) %all-to-all-start.1) | async-done | bytes 8224 | tf_op jit(solution)/shard_map/all_to_all | solution.py:36
  52.6 3.3 %all-to-all-start = ((s32[8,4,128]{2,1,0:T(4,128)}), s32[8,4,128]{2,1,0:T(4,128)S(1)}, u32[]{:S(2)}, u32[]{:S(2)}) async-start(s32[8,4,128]{2,1,0:T(4,128)} %maximum_convert_fusion), calls=%async_computation | async-start | bytes 32768 | tf_op jit(solution)/shard_map/all_to_all | solution.py:36
  56.0 0.1 select_reduce_fusion
  56.1 0.1 select_n.62
  56.2 0.1 stack_reshape.3
  56.3 0.1 select_n.60
  56.4 14.2 %all-to-all-done = s32[8,4,128]{2,1,0:T(4,128)S(1)} async-done(((s32[8,4,128]{2,1,0:T(4,128)}), s32[8,4,128]{2,1,0:T(4,128)S(1)}, u32[]{:S(2)}, u32[]{:S(2)}) %all-to-all-start) | async-done | bytes 16416 | tf_op jit(solution)/shard_map/all_to_all | solution.py:36
  70.6 0.1 select_n.57
  70.7 0.1 copy.60
  70.8 0.2 reshape.142.src_ref
  71.0 0.0 collective-permute-done
  71.0 0.1 select_bitcast_fusion.1
  71.2 0.1 pad_maximum_fusion
  71.3 2.2 %all-gather.2.cloned.1.call-done.all_ref = bf16[2048,512]{1,0:T(8,128)(2,1)} async-done(((bf16[128,512]{1,0:T(8,128)(2,1)}), bf16[2048,512]{1,0:T(8,128)(2,1)}) %all-gather.2.cloned.1.call-update) | async-done | bytes 2097168 | tf_op jit(solution)/shard_map/all_gather | solution.py:367
  73.5 4.9 %similar_parts.1 = (bf16[2,16,128,512]{3,2,1,0:T(8,128)(2,1)}, f32[32,128]{1,0:T(8,128)S(1)}) custom-call(bf16[2048,512]{1,0:T(8,128)(2,1)} %all-gather.2.cloned.1.call-done.all_ref, bf16[1024,512]{1,0:T(8,128)(2,1)S(1)} %bitcast.34, s32[16,256]{1,0:T(8,128)S(1)} %reshape.142.src_ref, s32[32,128]{1,0:T(8,128)S(1)} %bitcast.35), custom_call_target="tpu_custom_call" | custom-call | tf_op jit(solution)/shard_map/similar_parts/pallas_call | solution.py:144
  78.4 7.7 %all_to_all.35.sims_ref.chosen_ref = f32[4,96,128]{2,1,0:T(8,128)S(1)} all-to-all(f32[4,96,128]{2,1,0:T(8,128)S(1)} %pad_maximum_fusion.1), channel_id=1, replica_groups=mesh['y'=4,'z'=8,'half'=2,'core'=2,'x'=4] {'x'}, dimensions={0} | all-to-all | bytes 393216 | tf_op jit(solution)/shard_map/all_to_all | solution.py:36
  86.1 3.4 %weighted_sums.1 = s16[8,144,512]{2,1,0:T(8,128)(2,1)S(1)} custom-call(bf16[2,16,128,512]{3,2,1,0:T(8,128)(2,1)} %get-tuple-element.20.got_ref, f32[4,96,128]{2,1,0:T(8,128)S(1)} %all_to_all.35.sims_ref.chosen_ref, s32[32,128]{1,0:T(8,128)S(1)} %bitcast.36), custom_call_target="tpu_custom_call" | custom-call | tf_op jit(solution)/shard_map/weighted_sums/pallas_call | solution.py:199
  89.5 0.0 copy-start.1
  89.5 19.7 %all_to_all.36.parts_ref = s16[8,144,512]{2,1,0:T(8,128)(2,1)S(1)} all-to-all(s16[8,144,512]{2,1,0:T(8,128)(2,1)S(1)} %weighted_sums.1), channel_id=1, replica_groups=mesh['y'=4,'z'=8,'half'=2,'core'=2,'x'=4] {'y','half'}, dimensions={0} | all-to-all | bytes 2359296 | tf_op jit(solution)/shard_map/all_to_all | solution.py:36
  109.2 0.0 copy-done.1
  109.2 0.7 score_parts.1
  109.9 10.0 %all_to_all.37.parts_ref = f32[16,24,128]{2,1,0:T(8,128)S(1)} all-to-all(f32[16,24,128]{2,1,0:T(8,128)S(1)} %get-tuple-element.24), channel_id=1, replica_groups=mesh['y'=4,'z'=8,'half'=2,'core'=2,'x'=4] {'y','x'}, dimensions={0} | all-to-all | bytes 393216 | tf_op jit(solution)/shard_map/all_to_all | solution.py:36
  119.9 0.1 finish_scores.1
  120.0 0.8 broadcast_in_dim.18
  120.8 8.0 %all-to-all-start.6 = ((s16[16,80,128]{2,1,0:T(8,128)(2,1)}), s16[16,80,128]{2,1,0:T(8,128)(2,1)S(1)}, u32[]{:S(2)}, u32[]{:S(2)}) async-start(s16[16,80,128]{2,1,0:T(8,128)(2,1)} %broadcast_in_dim.18), calls=%async_computation.6 | async-start | bytes 655360 | tf_op jit(solution)/shard_map/all_to_all | solution.py:36
  128.7 13.4 %all-to-all-done.6.near_ref = s16[16,80,128]{2,1,0:T(8,128)(2,1)S(1)} async-done(((s16[16,80,128]{2,1,0:T(8,128)(2,1)}), s16[16,80,128]{2,1,0:T(8,128)(2,1)S(1)}, u32[]{:S(2)}, u32[]{:S(2)}) %all-to-all-start.6) | async-done | bytes 327712 | tf_op jit(solution)/shard_map/all_to_all | solution.py:36
  142.1 10.4 %collective-permute-start.1 = (s16[16,80,128]{2,1,0:T(8,128)(2,1)S(1)}, s16[16,80,128]{2,1,0:T(8,128)(2,1)S(1)}, u32[]{:S(2)}, u32[]{:S(2)}) collective-permute-start(s16[16,80,128]{2,1,0:T(8,128)(2,1)S(1)} %all-to-all-done.6.near_ref), channel_id=1, source_target_pairs={{0,4},{4,0},{1,5},{5,1},{2,6},{6,2},{3,7},{7,3},{8,12},{12,8},{9,1... | collective-permute-start | bytes 983048 | tf_op jit(solution)/shard_map/ppermute | solution.py:386
  152.6 0.7 multiply_convert_fusion
  153.3 0.5 collective-permute-done.1.far_ref
  153.8 1.9 %pick_scores.1 = f32[256,256]{1,0:T(8,128)} custom-call(s32[512]{0:T(512)S(1)} %multiply_add_fusion.rows_ref, s16[16,80,128]{2,1,0:T(8,128)(2,1)S(1)} %all-to-all-done.6.near_ref, s16[16,80,128]{2,1,0:T(8,128)(2,1)S(1)} %collective-permute-done.1.far_ref), custom_call_target="tpu_custom_call" | custom-call | tf_op jit(solution)/shard_map/pick_scores/pallas_call | solution.py:312
  (19 shorter events, 0.2 us)
Async XLA Ops:
  7.2 14.7 %copy-start = (bf16[256,2048]{1,0:T(8,128)(2,1)S(1)}, bf16[256,2048]{1,0:T(8,128)(2,1)}, u32[]{:S(2)}) copy-start(bf16[256,2048]{1,0:T(8,128)(2,1)} %param.8) | copy-start | bytes 3145732
  7.2 13.7 %copy-start.2 = (s32[256,2]{0,1:T(2,128)S(1)}, s32[256,2]{0,1:T(2,128)}, u32[]{:S(2)}) copy-start(s32[256,2]{0,1:T(2,128)} %param.9) | copy-start | bytes 6148
  7.2 66.3 %all-gather.2.cloned.1.call-start = ((), (), s32[]{:S(2)}) async-start(), calls=%async_computation.7 | async-start | bytes 2228224 | tf_op jit(solution)/shard_map/all_gather | solution.py:367
  9.7 12.5 %all-to-all-start.2 = ((bf16[4,128,512]{2,1,0:T(8,128)(2,1)}), bf16[4,128,512]{2,1,0:T(8,128)(2,1)S(1)}, u32[]{:S(2)}, u32[]{:S(2)}) async-start(bf16[4,128,512]{2,1,0:T(8,128)(2,1)} %broadcast_in_dim.16), calls=%async_computation.2 | async-start | bytes 1048576 | tf_op jit(solution)/shard_map/all_to_all | solution.py:36
  22.2 30.5 %all-to-all-start.1 = ((s32[16,1,128]{2,1,0:T(1,128)}), s32[16,1,128]{2,1,0:T(1,128)S(1)}, u32[]{:S(2)}, u32[]{:S(2)}) async-start(s32[16,1,128]{2,1,0:T(1,128)} %bitcast.6), calls=%async_computation.1 | async-start | bytes 16384 | tf_op jit(solution)/shard_map/all_to_all | solution.py:36
  41.0 30.1 %collective-permute-start = (bf16[4,128,512]{2,1,0:T(8,128)(2,1)S(1)}, bf16[4,128,512]{2,1,0:T(8,128)(2,1)S(1)}, u32[]{:S(2)}, u32[]{:S(2)}) collective-permute-start(bf16[4,128,512]{2,1,0:T(8,128)(2,1)S(1)} %all-to-all-done.2), channel_id=1, source_target_pairs={{0,8},{8,0},{1,9},{9,1},{2,10},{10,2},{3,11},{11,3},{4,12},{12,4},... | collective-permute-start | bytes 1572872 | tf_op jit(solution)/shard_map/ppermute | solution.py:369
  52.6 17.9 %all-to-all-start = ((s32[8,4,128]{2,1,0:T(4,128)}), s32[8,4,128]{2,1,0:T(4,128)S(1)}, u32[]{:S(2)}, u32[]{:S(2)}) async-start(s32[8,4,128]{2,1,0:T(4,128)} %maximum_convert_fusion), calls=%async_computation | async-start | bytes 32768 | tf_op jit(solution)/shard_map/all_to_all | solution.py:36
  89.5 19.7 %copy-start.1 = (bf16[128,512]{1,0:T(8,128)(2,1)S(1)}, bf16[128,512]{1,0:T(8,128)(2,1)}, u32[]{:S(2)}) copy-start(bf16[128,512]{1,0:T(8,128)(2,1)} %own_ref.1) | copy-start | bytes 393220
  120.8 21.4 %all-to-all-start.6 = ((s16[16,80,128]{2,1,0:T(8,128)(2,1)}), s16[16,80,128]{2,1,0:T(8,128)(2,1)S(1)}, u32[]{:S(2)}, u32[]{:S(2)}) async-start(s16[16,80,128]{2,1,0:T(8,128)(2,1)} %broadcast_in_dim.18), calls=%async_computation.6 | async-start | bytes 655360 | tf_op jit(solution)/shard_map/all_to_all | solution.py:36
  142.1 11.6 %collective-permute-start.1 = (s16[16,80,128]{2,1,0:T(8,128)(2,1)S(1)}, s16[16,80,128]{2,1,0:T(8,128)(2,1)S(1)}, u32[]{:S(2)}, u32[]{:S(2)}) collective-permute-start(s16[16,80,128]{2,1,0:T(8,128)(2,1)S(1)} %all-to-all-done.6.near_ref), channel_id=1, source_target_pairs={{0,4},{4,0},{1,5},{5,1},{2,6},{6,2},{3,7},{7,3},{8,12},{12,8},{9,1... | collective-permute-start | bytes 983048 | tf_op jit(solution)/shard_map/ppermute | solution.py:386
Sparse Core Ops, SparseCore 0:
  10.1 63.3 all-gather.1

commit v7 on v6

--- a/solution.py
+++ b/solution.py
@@ -188,9 +188,12 @@
         peak = jnp.maximum(jnp.max(jnp.abs(total), axis=1, keepdims=True), 1e-30)
         level = jnp.floor(jnp.log2(peak) * STEPS_PER_OCTAVE) + 1.0
         scale = LEVELS / jnp.exp2(level / STEPS_PER_OCTAVE)
-        sum_ref[shard, :BLOCK, :] = jnp.floor(total * scale + 0.5).astype(i32).astype(i16)
-        level = jnp.broadcast_to(level, (BLOCK, LANES)).T[:PLACES].astype(i32).astype(i16)
-        sum_ref[shard, BLOCK:, :] = jnp.concatenate([level] * (total.shape[1] // LANES), axis=1)
+        total = jnp.floor(total * scale + 0.5).astype(i32).astype(i16)
+        quarters = total.shape[1] // LANES
+        for quarter in range(quarters):
+            at = slice(quarter * BLOCK, (quarter + 1) * BLOCK)
+            sum_ref[shard, at, :] = total[:, quarter * LANES : (quarter + 1) * LANES]
+        sum_ref[shard, quarters * BLOCK :, :] = jnp.broadcast_to(level, (BLOCK, LANES)).T[:PLACES].astype(i32).astype(i16)
 
 
 def weighted_sums(got, sims, at):
@@ -200,7 +203,7 @@
         sum_kernel,
         in_specs=[pl.BlockSpec(memory_space=HBM), vmem, vmem],
         out_specs=vmem,
-        out_shape=jax.ShapeDtypeStruct((kinds // 2, BLOCK + PLACES, width), i16),
+        out_shape=jax.ShapeDtypeStruct((kinds // 2, width // LANES * BLOCK + PLACES, LANES), i16),
         scratch_shapes=[pltpu.VMEM(got.shape, bf16), pltpu.SemaphoreType.DMA((kinds // 2 // JOIN,))],
         compiler_params=params(),
         interpret=INTERPRET,
@@ -210,18 +213,19 @@
 
 def score_kernel(parts_ref, own_ref, chosen_ref, sum_ref, out_ref):
     total = own_ref[...].astype(f32)
+    quarters = total.shape[1] // LANES
     for part in range(parts_ref.shape[0]):
-        level = parts_ref[part, BLOCK:, :LANES].astype(i32).astype(f32)[:1]
+        level = parts_ref[part, quarters * BLOCK :, :].astype(i32).astype(f32)[:1]
         level = jnp.broadcast_to(level, (BLOCK, LANES)).T[:, :1]
         scale = jnp.exp2(level / STEPS_PER_OCTAVE) / LEVELS
-        total += parts_ref[part, :BLOCK, :].astype(i32).astype(f32) * scale
+        pieces = [parts_ref[part, quarter * BLOCK : (quarter + 1) * BLOCK, :] for quarter in range(quarters)]
+        total += jnp.concatenate(pieces, axis=1).astype(i32).astype(f32) * scale
     sum_ref[...] = total
     energy = jnp.sum(total * total, axis=1, keepdims=True)
     energy = jnp.broadcast_to(energy, (BLOCK, LANES)).T[:8]
     high = total.astype(bf16)
     low = (total - high.astype(f32)).astype(bf16)
     lanes = chosen_ref.shape[0]
-    quarters = total.shape[1] // LANES
     before = chosen_ref.shape[1] - quarters * PLACES
     scores = jnp.zeros((lanes * PLACES, LANES), f32)
     for quarter in range(quarters):
@@ -266,15 +270,18 @@
     level = jnp.broadcast_to(level, (PLACES, LANES))
     count = scores.shape[0]
     scores = scores * (LEVELS / jnp.exp2(level[:1] / STEPS_PER_OCTAVE))
-    out_ref[:count, :] = jnp.floor(scores + 0.5).astype(i32).astype(i16)
-    out_ref[count:, :] = level.astype(i32).astype(i16)
-
-
-def finish_scores(parts, ys, depth):
+    scores = jnp.floor(scores + 0.5).astype(i32).astype(i16)
+    level = level.astype(i32).astype(i16)
+    for place in range(out_ref.shape[0]):
+        out_ref[place, :count, :] = scores
+        out_ref[place, count:, :] = level
+
+
+def finish_scores(parts, ys, zs, depth):
     return pl.pallas_call(
         functools.partial(finish_kernel, depth),
         out_shape=[
-            jax.ShapeDtypeStruct(((ys + 1) * PLACES, LANES), i16),
+            jax.ShapeDtypeStruct((zs, (ys + 1) * PLACES, LANES), i16),
             jax.ShapeDtypeStruct((ys, 8, LANES), f32),
         ],
         compiler_params=params(),
@@ -379,10 +386,10 @@
     sims = exchange(sims, "x")
     parts = exchange(weighted_sums(got, sims, at), ("y", "half"))
     summed, parts = score_parts(parts, descriptors, sims, ys * xs)
-    mine, scales = finish_scores(exchange(parts, ("y", "x")), ys, xs * width)
+    mine, scales = finish_scores(exchange(parts, ("y", "x")), ys, zs, xs * width)
     scale = lax.dynamic_index_in_dim(scales, lax.axis_index("y"), 0, keepdims=False)[0]
     augmented = (summed * scale[:, None]).astype(bf16)
-    near = spread(mine, ("z", "half"), zs)
+    near = exchange(mine, ("z", "half"))
     far = lax.ppermute(near, "core", [(0, 1), (1, 0)])
     return augmented, pick_scores(score_rows, near, far)
 

time: 163 us -> 162 us (level)
  no operation moved by 1% of the time
where the time goes in v7:
time: 162 us
  starting transfers between devices  47.3 us (29%)
  waiting for transfers between devices  40 us (25%)
  blocking collectives  36.5 us (23%)
  Pallas kernels  15.1 us (9%)
  between operations  14.4 us (9%)
  local copies, waits for them, and re-layouts  6.14 us (4%)
  other arithmetic  2.02 us (1%)
    all_to_all x4, waiting for transfers between devices, exchange(): return lax.all_to_all(parts, axis, split_axis=0, concat_axis=0, tiled=True)  36.6 us
    all_to_all x3, blocking collectives, exchange(): return lax.all_to_all(parts, axis, split_axis=0, concat_axis=0, tiled=True)  36.5 us
    all_to_all x4, starting transfers between devices, exchange(): return lax.all_to_all(parts, axis, split_axis=0, concat_axis=0, tiled=True)  34.2 us
    ppermute x1, starting transfers between devices, per_device(): far = lax.ppermute(near, 'core', [(0, 1), (1, 0)])  10.4 us
    pallas_call x1, Pallas kernels, similar_parts(): pl.pallas_call(similar_kernel, in_specs=[outside, vmem, vmem, vmem], out_...  4.89 us
    pallas_call x1, Pallas kernels, weighted_sums(): pl.pallas_call(sum_kernel, in_specs=[pl.BlockSpec(memory_space=HBM), vmem...  3.45 us
    pallas_call x1, Pallas kernels, build_table(): pl.pallas_call(functools.partial(table_kernel, halves), out_shape=[jax.Sh...  3.26 us
  transfers between devices with their start and end apart: 7, of which 5 were waited for; matrix products, arithmetic and copies ran while one was open for 5% of the time, Pallas kernels for 2%

profile of v7, /device:TPU:1, one launch (start us, length us, event | category | flops | bytes accessed | tf_op | source)
XLA Modules:
  0.0 161.6 jit_solution(18101431538824702037)
XLA Ops:
  7.2 0.0 copy-start
  7.2 0.0 copy-start.2
  7.2 0.0 all-gather.2.cloned.1.call-start
  7.2 0.7 all-gather.2.cloned.1.call-update
  7.9 1.7 %broadcast_in_dim.14 = bf16[4,128,512]{2,1,0:T(8,128)(2,1)} broadcast(bf16[128,512]{1,0:T(8,128)(2,1)} %own_ref.1), dimensions={1,2} | broadcast | bytes 655360 | tf_op jit(solution)/shard_map/broadcast_in_dim | solution.py:40
  9.7 5.0 %all-to-all-start.2 = ((bf16[4,128,512]{2,1,0:T(8,128)(2,1)}), bf16[4,128,512]{2,1,0:T(8,128)(2,1)S(1)}, u32[]{:S(2)}, u32[]{:S(2)}) async-start(bf16[4,128,512]{2,1,0:T(8,128)(2,1)} %broadcast_in_dim.14), calls=%async_computation.2 | async-start | bytes 1048576 | tf_op jit(solution)/shard_map/all_to_all | solution.py:36
  14.7 0.8 copy.53.listed_ref
  15.5 0.8 copy.54.owned_ref
  16.3 0.8 copy.65
  17.1 0.1 eq.60
  17.3 3.3 %slot_table.1 = (f32[16,128]{1,0:T(8,128)S(1)}, f32[16,128]{1,0:T(8,128)S(1)}) custom-call(s32[128,10]{1,0:T(8,128)S(1)} %copy.53.listed_ref, s32[128,10]{1,0:T(8,128)S(1)} %copy.54.owned_ref), custom_call_target="tpu_custom_call" | custom-call | tf_op jit(solution)/shard_map/slot_table/pallas_call | solution.py:85
  20.5 0.3 convert_reduce_fusion
  20.8 0.0 copy-done.2
  20.9 0.1 eq.64
  21.0 0.1 reshape.139
  21.1 0.7 reshape.140
  21.8 0.1 copy.66
  21.9 0.0 copy-done
  21.9 0.3 fusion.9
  22.2 0.0 all-to-all-done.2
  22.2 18.0 %all-to-all-start.1 = ((s32[16,1,128]{2,1,0:T(1,128)}), s32[16,1,128]{2,1,0:T(1,128)S(1)}, u32[]{:S(2)}, u32[]{:S(2)}) async-start(s32[16,1,128]{2,1,0:T(1,128)} %bitcast.6), calls=%async_computation.1 | async-start | bytes 16384 | tf_op jit(solution)/shard_map/all_to_all | solution.py:36
  40.2 0.6 maximum_convert_fusion
  40.8 0.1 reshape.145
  41.0 2.7 %collective-permute-start = (bf16[4,128,512]{2,1,0:T(8,128)(2,1)S(1)}, bf16[4,128,512]{2,1,0:T(8,128)(2,1)S(1)}, u32[]{:S(2)}, u32[]{:S(2)}) collective-permute-start(bf16[4,128,512]{2,1,0:T(8,128)(2,1)S(1)} %all-to-all-done.2), channel_id=1, source_target_pairs={{0,8},{8,0},{1,9},{9,1},{2,10},{10,2},{3,11},{11,3},{4,12},{12,4},... | collective-permute-start | bytes 1572872 | tf_op jit(solution)/shard_map/ppermute | solution.py:376
  43.7 9.0 %all-to-all-done.1 = s32[16,1,128]{2,1,0:T(1,128)S(1)} async-done(((s32[16,1,128]{2,1,0:T(1,128)}), s32[16,1,128]{2,1,0:T(1,128)S(1)}, u32[]{:S(2)}, u32[]{:S(2)}) %all-to-all-start.1) | async-done | bytes 8224 | tf_op jit(solution)/shard_map/all_to_all | solution.py:36
  52.6 3.3 %all-to-all-start = ((s32[8,4,128]{2,1,0:T(4,128)}), s32[8,4,128]{2,1,0:T(4,128)S(1)}, u32[]{:S(2)}, u32[]{:S(2)}) async-start(s32[8,4,128]{2,1,0:T(4,128)} %maximum_convert_fusion), calls=%async_computation | async-start | bytes 32768 | tf_op jit(solution)/shard_map/all_to_all | solution.py:36
  56.0 0.1 select_reduce_fusion
  56.1 0.1 select_n.62
  56.2 0.1 stack_reshape.3
  56.3 0.1 select_n.60
  56.4 14.2 %all-to-all-done = s32[8,4,128]{2,1,0:T(4,128)S(1)} async-done(((s32[8,4,128]{2,1,0:T(4,128)}), s32[8,4,128]{2,1,0:T(4,128)S(1)}, u32[]{:S(2)}, u32[]{:S(2)}) %all-to-all-start) | async-done | bytes 16416 | tf_op jit(solution)/shard_map/all_to_all | solution.py:36
  70.6 0.1 select_n.57
  70.7 0.1 copy.60
  70.8 0.2 reshape.141.src_ref
  71.0 0.0 collective-permute-done
  71.0 0.1 select_bitcast_fusion.1
  71.2 0.1 pad_maximum_fusion
  71.3 2.2 %all-gather.2.cloned.1.call-done.all_ref = bf16[2048,512]{1,0:T(8,128)(2,1)} async-done(((bf16[128,512]{1,0:T(8,128)(2,1)}), bf16[2048,512]{1,0:T(8,128)(2,1)}) %all-gather.2.cloned.1.call-update) | async-done | bytes 2097168 | tf_op jit(solution)/shard_map/all_gather | solution.py:374
  73.5 4.9 %similar_parts.1 = (bf16[2,16,128,512]{3,2,1,0:T(8,128)(2,1)}, f32[32,128]{1,0:T(8,128)S(1)}) custom-call(bf16[2048,512]{1,0:T(8,128)(2,1)} %all-gather.2.cloned.1.call-done.all_ref, bf16[1024,512]{1,0:T(8,128)(2,1)S(1)} %bitcast.34, s32[16,256]{1,0:T(8,128)S(1)} %reshape.141.src_ref, s32[32,128]{1,0:T(8,128)S(1)} %bitcast.35), custom_call_target="tpu_custom_call" | custom-call | tf_op jit(solution)/shard_map/similar_parts/pallas_call | solution.py:144
  78.4 7.7 %all_to_all.35.sims_ref.chosen_ref = f32[4,96,128]{2,1,0:T(8,128)S(1)} all-to-all(f32[4,96,128]{2,1,0:T(8,128)S(1)} %pad_maximum_fusion.1), channel_id=1, replica_groups=mesh['y'=4,'z'=8,'half'=2,'core'=2,'x'=4] {'x'}, dimensions={0} | all-to-all | bytes 393216 | tf_op jit(solution)/shard_map/all_to_all | solution.py:36
  86.1 3.4 %weighted_sums.1 = s16[8,528,128]{2,1,0:T(8,128)(2,1)S(1)} custom-call(bf16[2,16,128,512]{3,2,1,0:T(8,128)(2,1)} %get-tuple-element.20.got_ref, f32[4,96,128]{2,1,0:T(8,128)S(1)} %all_to_all.35.sims_ref.chosen_ref, s32[32,128]{1,0:T(8,128)S(1)} %bitcast.36), custom_call_target="tpu_custom_call" | custom-call | tf_op jit(solution)/shard_map/weighted_sums/pallas_call | solution.py:202
  89.5 0.0 copy-start.1
  89.6 18.7 %all_to_all.36.parts_ref = s16[8,528,128]{2,1,0:T(8,128)(2,1)S(1)} all-to-all(s16[8,528,128]{2,1,0:T(8,128)(2,1)S(1)} %weighted_sums.1), channel_id=1, replica_groups=mesh['y'=4,'z'=8,'half'=2,'core'=2,'x'=4] {'y','half'}, dimensions={0} | all-to-all | bytes 2162688 | tf_op jit(solution)/shard_map/all_to_all | solution.py:36
  108.3 0.0 copy-done.1
  108.3 0.7 score_parts.1
  109.0 10.1 %all_to_all.37.parts_ref = f32[16,24,128]{2,1,0:T(8,128)S(1)} all-to-all(f32[16,24,128]{2,1,0:T(8,128)S(1)} %get-tuple-element.24), channel_id=1, replica_groups=mesh['y'=4,'z'=8,'half'=2,'core'=2,'x'=4] {'y','x'}, dimensions={0} | all-to-all | bytes 393216 | tf_op jit(solution)/shard_map/all_to_all | solution.py:36
  119.2 0.9 finish_scores.1
  120.1 7.8 %all-to-all-start.6 = ((s16[16,80,128]{2,1,0:T(8,128)(2,1)}), s16[16,80,128]{2,1,0:T(8,128)(2,1)S(1)}, u32[]{:S(2)}, u32[]{:S(2)}) async-start(s16[16,80,128]{2,1,0:T(8,128)(2,1)} %get-tuple-element.27), calls=%async_computation.6 | async-start | bytes 655360 | tf_op jit(solution)/shard_map/all_to_all | solution.py:36
  127.9 13.4 %all-to-all-done.6.near_ref = s16[16,80,128]{2,1,0:T(8,128)(2,1)S(1)} async-done(((s16[16,80,128]{2,1,0:T(8,128)(2,1)}), s16[16,80,128]{2,1,0:T(8,128)(2,1)S(1)}, u32[]{:S(2)}, u32[]{:S(2)}) %all-to-all-start.6) | async-done | bytes 327712 | tf_op jit(solution)/shard_map/all_to_all | solution.py:36
  141.3 10.4 %collective-permute-start.1 = (s16[16,80,128]{2,1,0:T(8,128)(2,1)S(1)}, s16[16,80,128]{2,1,0:T(8,128)(2,1)S(1)}, u32[]{:S(2)}, u32[]{:S(2)}) collective-permute-start(s16[16,80,128]{2,1,0:T(8,128)(2,1)S(1)} %all-to-all-done.6.near_ref), channel_id=1, source_target_pairs={{0,4},{4,0},{1,5},{5,1},{2,6},{6,2},{3,7},{7,3},{8,12},{12,8},{9,1... | collective-permute-start | bytes 983048 | tf_op jit(solution)/shard_map/ppermute | solution.py:393
  151.7 0.7 multiply_convert_fusion
  152.4 0.5 collective-permute-done.1.far_ref
  152.9 1.9 %pick_scores.1 = f32[256,256]{1,0:T(8,128)} custom-call(s32[512]{0:T(512)S(1)} %multiply_add_fusion.rows_ref, s16[16,80,128]{2,1,0:T(8,128)(2,1)S(1)} %all-to-all-done.6.near_ref, s16[16,80,128]{2,1,0:T(8,128)(2,1)S(1)} %collective-permute-done.1.far_ref), custom_call_target="tpu_custom_call" | custom-call | tf_op jit(solution)/shard_map/pick_scores/pallas_call | solution.py:319
  (19 shorter events, 0.2 us)
Async XLA Ops:
  7.2 14.7 %copy-start = (bf16[256,2048]{1,0:T(8,128)(2,1)S(1)}, bf16[256,2048]{1,0:T(8,128)(2,1)}, u32[]{:S(2)}) copy-start(bf16[256,2048]{1,0:T(8,128)(2,1)} %param.8) | copy-start | bytes 3145732
  7.2 13.7 %copy-start.2 = (s32[256,2]{0,1:T(2,128)S(1)}, s32[256,2]{0,1:T(2,128)}, u32[]{:S(2)}) copy-start(s32[256,2]{0,1:T(2,128)} %param.9) | copy-start | bytes 6148
  7.2 66.3 %all-gather.2.cloned.1.call-start = ((), (), s32[]{:S(2)}) async-start(), calls=%async_computation.7 | async-start | bytes 2228224 | tf_op jit(solution)/shard_map/all_gather | solution.py:374
  9.7 12.5 %all-to-all-start.2 = ((bf16[4,128,512]{2,1,0:T(8,128)(2,1)}), bf16[4,128,512]{2,1,0:T(8,128)(2,1)S(1)}, u32[]{:S(2)}, u32[]{:S(2)}) async-start(bf16[4,128,512]{2,1,0:T(8,128)(2,1)} %broadcast_in_dim.14), calls=%async_computation.2 | async-start | bytes 1048576 | tf_op jit(solution)/shard_map/all_to_all | solution.py:36
  22.2 30.5 %all-to-all-start.1 = ((s32[16,1,128]{2,1,0:T(1,128)}), s32[16,1,128]{2,1,0:T(1,128)S(1)}, u32[]{:S(2)}, u32[]{:S(2)}) async-start(s32[16,1,128]{2,1,0:T(1,128)} %bitcast.6), calls=%async_computation.1 | async-start | bytes 16384 | tf_op jit(solution)/shard_map/all_to_all | solution.py:36
  41.0 30.1 %collective-permute-start = (bf16[4,128,512]{2,1,0:T(8,128)(2,1)S(1)}, bf16[4,128,512]{2,1,0:T(8,128)(2,1)S(1)}, u32[]{:S(2)}, u32[]{:S(2)}) collective-permute-start(bf16[4,128,512]{2,1,0:T(8,128)(2,1)S(1)} %all-to-all-done.2), channel_id=1, source_target_pairs={{0,8},{8,0},{1,9},{9,1},{2,10},{10,2},{3,11},{11,3},{4,12},{12,4},... | collective-permute-start | bytes 1572872 | tf_op jit(solution)/shard_map/ppermute | solution.py:376
  52.6 17.9 %all-to-all-start = ((s32[8,4,128]{2,1,0:T(4,128)}), s32[8,4,128]{2,1,0:T(4,128)S(1)}, u32[]{:S(2)}, u32[]{:S(2)}) async-start(s32[8,4,128]{2,1,0:T(4,128)} %maximum_convert_fusion), calls=%async_computation | async-start | bytes 32768 | tf_op jit(solution)/shard_map/all_to_all | solution.py:36
  89.5 18.8 %copy-start.1 = (bf16[128,512]{1,0:T(8,128)(2,1)S(1)}, bf16[128,512]{1,0:T(8,128)(2,1)}, u32[]{:S(2)}) copy-start(bf16[128,512]{1,0:T(8,128)(2,1)} %own_ref.1) | copy-start | bytes 393220
  120.1 21.2 %all-to-all-start.6 = ((s16[16,80,128]{2,1,0:T(8,128)(2,1)}), s16[16,80,128]{2,1,0:T(8,128)(2,1)S(1)}, u32[]{:S(2)}, u32[]{:S(2)}) async-start(s16[16,80,128]{2,1,0:T(8,128)(2,1)} %get-tuple-element.27), calls=%async_computation.6 | async-start | bytes 655360 | tf_op jit(solution)/shard_map/all_to_all | solution.py:36
  141.3 11.6 %collective-permute-start.1 = (s16[16,80,128]{2,1,0:T(8,128)(2,1)S(1)}, s16[16,80,128]{2,1,0:T(8,128)(2,1)S(1)}, u32[]{:S(2)}, u32[]{:S(2)}) collective-permute-start(s16[16,80,128]{2,1,0:T(8,128)(2,1)S(1)} %all-to-all-done.6.near_ref), channel_id=1, source_target_pairs={{0,4},{4,0},{1,5},{5,1},{2,6},{6,2},{3,7},{7,3},{8,12},{12,8},{9,1... | collective-permute-start | bytes 983048 | tf_op jit(solution)/shard_map/ppermute | solution.py:393
Sparse Core Ops, SparseCore 0:
  10.1 63.3 all-gather.1

commit v8 on v7

--- a/solution.py
+++ b/solution.py
@@ -28,6 +28,8 @@
 i32 = jnp.int32
 LEVELS = 32512.0
 STEPS_PER_OCTAVE = 64.0
+STEPS_PER_OCTAVE_OF_SCORES = 512.0
+LOWEST = 54.0
 NT = (((1,), (1,)), ((), ()))
 TN = (((0,), (0,)), ((), ()))
 
@@ -265,23 +267,19 @@
         scale_ref[y] = scale
         scores.append(whole[:PLACES] * (scale[:1] / math.sqrt(depth)))
     scores = jnp.concatenate(scores, axis=0)
-    peak = jnp.max(jnp.max(jnp.abs(scores), axis=0, keepdims=True), axis=1, keepdims=True)
-    level = jnp.floor(jnp.log2(jnp.maximum(peak, 1e-30)) * STEPS_PER_OCTAVE) + 1.0
-    level = jnp.broadcast_to(level, (PLACES, LANES))
-    count = scores.shape[0]
-    scores = scores * (LEVELS / jnp.exp2(level[:1] / STEPS_PER_OCTAVE))
-    scores = jnp.floor(scores + 0.5).astype(i32).astype(i16)
-    level = level.astype(i32).astype(i16)
+    size = jnp.abs(scores)
+    code = jnp.floor((jnp.log2(jnp.maximum(size, 2.0**-LOWEST)) + LOWEST) * STEPS_PER_OCTAVE_OF_SCORES + 1.5)
+    code = jnp.where(size < 2.0**-LOWEST, 0.0, jnp.minimum(code, 32767.0))
+    code = jnp.where(scores < 0.0, -code, code).astype(i32).astype(i16)
     for place in range(out_ref.shape[0]):
-        out_ref[place, :count, :] = scores
-        out_ref[place, count:, :] = level
+        out_ref[place] = code
 
 
 def finish_scores(parts, ys, zs, depth):
     return pl.pallas_call(
         functools.partial(finish_kernel, depth),
         out_shape=[
-            jax.ShapeDtypeStruct((zs, (ys + 1) * PLACES, LANES), i16),
+            jax.ShapeDtypeStruct((zs, ys * PLACES, LANES), i16),
             jax.ShapeDtypeStruct((ys, 8, LANES), f32),
         ],
         compiler_params=params(),
@@ -291,13 +289,14 @@
 
 
 def pick_kernel(rows_ref, near_ref, far_ref, out_ref, table_ref):
-    planes, held, _ = near_ref.shape
-    count = held - PLACES
+    planes, count, _ = near_ref.shape
     for side, ref in enumerate((near_ref, far_ref)):
         for plane in range(planes):
-            level = ref[plane, count:, :].astype(i32).astype(f32)[:1]
-            scores = ref[plane, :count, :].astype(i32).astype(f32) * (jnp.exp2(level / STEPS_PER_OCTAVE) / LEVELS)
-            table_ref[(side * planes + plane) * count : (side * planes + plane + 1) * count, :] = scores
+            code = ref[plane].astype(i32).astype(f32)
+            size = jnp.exp2((jnp.abs(code) - 1.0) / STEPS_PER_OCTAVE_OF_SCORES - LOWEST)
+            at = (side * planes + plane) * count
+            scores = jnp.where(code < 0.0, -size, size)
+            table_ref[at : at + count, :] = jnp.where(code == 0.0, 0.0, scores)
 
     def step(i, carry):
         for cand in range(2):
@@ -315,13 +314,13 @@
 def pick_scores(rows, near, far):
     queries = rows.shape[0] // 2
     vmem = pl.BlockSpec(memory_space=pltpu.VMEM)
-    planes, held, _ = near.shape
+    planes, count, _ = near.shape
     return pl.pallas_call(
         pick_kernel,
         in_specs=[pl.BlockSpec(memory_space=pltpu.SMEM), vmem, vmem],
         out_specs=vmem,
         out_shape=jax.ShapeDtypeStruct((queries, 2 * LANES), f32),
-        scratch_shapes=[pltpu.VMEM((2 * planes * (held - PLACES), LANES), f32)],
+        scratch_shapes=[pltpu.VMEM((2 * planes * count, LANES), f32)],
         compiler_params=params(),
         interpret=INTERPRET,
         name="pick_scores",

time: 162 us -> 161 us (level)
  no operation moved by 1% of the time
where the time goes in v8:
time: 161 us
  starting transfers between devices  47 us (29%)
  waiting for transfers between devices  39.2 us (24%)
  blocking collectives  36.5 us (23%)
  Pallas kernels  15.2 us (9%)
  between operations  14.4 us (9%)
  local copies, waits for them, and re-layouts  6.14 us (4%)
  other arithmetic  2.02 us (1%)
    all_to_all x3, blocking collectives, exchange(): return lax.all_to_all(parts, axis, split_axis=0, concat_axis=0, tiled=True)  36.5 us
    all_to_all x4, waiting for transfers between devices, exchange(): return lax.all_to_all(parts, axis, split_axis=0, concat_axis=0, tiled=True)  36 us
    all_to_all x4, starting transfers between devices, exchange(): return lax.all_to_all(parts, axis, split_axis=0, concat_axis=0, tiled=True)  34.2 us
    ppermute x1, starting transfers between devices, per_device(): far = lax.ppermute(near, 'core', [(0, 1), (1, 0)])  10.1 us
    pallas_call x1, Pallas kernels, similar_parts(): pl.pallas_call(similar_kernel, in_specs=[outside, vmem, vmem, vmem], out_...  4.89 us
    pallas_call x1, Pallas kernels, weighted_sums(): pl.pallas_call(sum_kernel, in_specs=[pl.BlockSpec(memory_space=HBM), vmem...  3.45 us
    pallas_call x1, Pallas kernels, build_table(): pl.pallas_call(functools.partial(table_kernel, halves), out_shape=[jax.Sh...  3.26 us
  transfers between devices with their start and end apart: 7, of which 5 were waited for; matrix products, arithmetic and copies ran while one was open for 5% of the time, Pallas kernels for 2%

profile of v8, /device:TPU:1, one launch (start us, length us, event | category | flops | bytes accessed | tf_op | source)
XLA Modules:
  0.0 160.7 jit_solution(10198661006780747865)
XLA Ops:
  7.2 0.0 copy-start
  7.2 0.0 copy-start.2
  7.2 0.0 all-gather.2.cloned.1.call-start
  7.2 0.7 all-gather.2.cloned.1.call-update
  7.9 1.7 %broadcast_in_dim.14 = bf16[4,128,512]{2,1,0:T(8,128)(2,1)} broadcast(bf16[128,512]{1,0:T(8,128)(2,1)} %own_ref.1), dimensions={1,2} | broadcast | bytes 655360 | tf_op jit(solution)/shard_map/broadcast_in_dim | solution.py:42
  9.7 5.0 %all-to-all-start.2 = ((bf16[4,128,512]{2,1,0:T(8,128)(2,1)}), bf16[4,128,512]{2,1,0:T(8,128)(2,1)S(1)}, u32[]{:S(2)}, u32[]{:S(2)}) async-start(bf16[4,128,512]{2,1,0:T(8,128)(2,1)} %broadcast_in_dim.14), calls=%async_computation.2 | async-start | bytes 1048576 | tf_op jit(solution)/shard_map/all_to_all | solution.py:38
  14.7 0.8 copy.53.listed_ref
  15.5 0.8 copy.54.owned_ref
  16.3 0.8 copy.65
  17.1 0.1 eq.60
  17.3 3.3 %slot_table.1 = (f32[16,128]{1,0:T(8,128)S(1)}, f32[16,128]{1,0:T(8,128)S(1)}) custom-call(s32[128,10]{1,0:T(8,128)S(1)} %copy.53.listed_ref, s32[128,10]{1,0:T(8,128)S(1)} %copy.54.owned_ref), custom_call_target="tpu_custom_call" | custom-call | tf_op jit(solution)/shard_map/slot_table/pallas_call | solution.py:87
  20.5 0.3 convert_reduce_fusion
  20.8 0.0 copy-done.2
  20.9 0.1 eq.64
  21.0 0.1 reshape.139
  21.1 0.7 reshape.140
  21.8 0.1 copy.66
  21.9 0.0 copy-done
  21.9 0.3 fusion.9
  22.2 0.0 all-to-all-done.2
  22.2 18.0 %all-to-all-start.1 = ((s32[16,1,128]{2,1,0:T(1,128)}), s32[16,1,128]{2,1,0:T(1,128)S(1)}, u32[]{:S(2)}, u32[]{:S(2)}) async-start(s32[16,1,128]{2,1,0:T(1,128)} %bitcast.6), calls=%async_computation.1 | async-start | bytes 16384 | tf_op jit(solution)/shard_map/all_to_all | solution.py:38
  40.2 0.6 maximum_convert_fusion
  40.8 0.1 reshape.145
  41.0 2.7 %collective-permute-start = (bf16[4,128,512]{2,1,0:T(8,128)(2,1)S(1)}, bf16[4,128,512]{2,1,0:T(8,128)(2,1)S(1)}, u32[]{:S(2)}, u32[]{:S(2)}) collective-permute-start(bf16[4,128,512]{2,1,0:T(8,128)(2,1)S(1)} %all-to-all-done.2), channel_id=1, source_target_pairs={{0,8},{8,0},{1,9},{9,1},{2,10},{10,2},{3,11},{11,3},{4,12},{12,4},... | collective-permute-start | bytes 1572872 | tf_op jit(solution)/shard_map/ppermute | solution.py:375
  43.7 9.0 %all-to-all-done.1 = s32[16,1,128]{2,1,0:T(1,128)S(1)} async-done(((s32[16,1,128]{2,1,0:T(1,128)}), s32[16,1,128]{2,1,0:T(1,128)S(1)}, u32[]{:S(2)}, u32[]{:S(2)}) %all-to-all-start.1) | async-done | bytes 8224 | tf_op jit(solution)/shard_map/all_to_all | solution.py:38
  52.6 3.3 %all-to-all-start = ((s32[8,4,128]{2,1,0:T(4,128)}), s32[8,4,128]{2,1,0:T(4,128)S(1)}, u32[]{:S(2)}, u32[]{:S(2)}) async-start(s32[8,4,128]{2,1,0:T(4,128)} %maximum_convert_fusion), calls=%async_computation | async-start | bytes 32768 | tf_op jit(solution)/shard_map/all_to_all | solution.py:38
  56.0 0.1 select_reduce_fusion
  56.1 0.1 select_n.62
  56.2 0.1 stack_reshape.3
  56.3 0.1 select_n.60
  56.4 14.2 %all-to-all-done = s32[8,4,128]{2,1,0:T(4,128)S(1)} async-done(((s32[8,4,128]{2,1,0:T(4,128)}), s32[8,4,128]{2,1,0:T(4,128)S(1)}, u32[]{:S(2)}, u32[]{:S(2)}) %all-to-all-start) | async-done | bytes 16416 | tf_op jit(solution)/shard_map/all_to_all | solution.py:38
  70.6 0.1 select_n.57
  70.7 0.1 copy.60
  70.8 0.2 reshape.141.src_ref
  71.0 0.0 collective-permute-done
  71.0 0.1 select_bitcast_fusion.1
  71.2 0.1 pad_maximum_fusion
  71.3 2.2 %all-gather.2.cloned.1.call-done.all_ref = bf16[2048,512]{1,0:T(8,128)(2,1)} async-done(((bf16[128,512]{1,0:T(8,128)(2,1)}), bf16[2048,512]{1,0:T(8,128)(2,1)}) %all-gather.2.cloned.1.call-update) | async-done | bytes 2097168 | tf_op jit(solution)/shard_map/all_gather | solution.py:373
  73.5 4.9 %similar_parts.1 = (bf16[2,16,128,512]{3,2,1,0:T(8,128)(2,1)}, f32[32,128]{1,0:T(8,128)S(1)}) custom-call(bf16[2048,512]{1,0:T(8,128)(2,1)} %all-gather.2.cloned.1.call-done.all_ref, bf16[1024,512]{1,0:T(8,128)(2,1)S(1)} %bitcast.34, s32[16,256]{1,0:T(8,128)S(1)} %reshape.141.src_ref, s32[32,128]{1,0:T(8,128)S(1)} %bitcast.35), custom_call_target="tpu_custom_call" | custom-call | tf_op jit(solution)/shard_map/similar_parts/pallas_call | solution.py:146
  78.4 7.7 %all_to_all.35.sims_ref.chosen_ref = f32[4,96,128]{2,1,0:T(8,128)S(1)} all-to-all(f32[4,96,128]{2,1,0:T(8,128)S(1)} %pad_maximum_fusion.1), channel_id=1, replica_groups=mesh['y'=4,'z'=8,'half'=2,'core'=2,'x'=4] {'x'}, dimensions={0} | all-to-all | bytes 393216 | tf_op jit(solution)/shard_map/all_to_all | solution.py:38
  86.1 3.4 %weighted_sums.1 = s16[8,528,128]{2,1,0:T(8,128)(2,1)S(1)} custom-call(bf16[2,16,128,512]{3,2,1,0:T(8,128)(2,1)} %get-tuple-element.20.got_ref, f32[4,96,128]{2,1,0:T(8,128)S(1)} %all_to_all.35.sims_ref.chosen_ref, s32[32,128]{1,0:T(8,128)S(1)} %bitcast.36), custom_call_target="tpu_custom_call" | custom-call | tf_op jit(solution)/shard_map/weighted_sums/pallas_call | solution.py:204
  89.5 0.0 copy-start.1
  89.6 18.7 %all_to_all.36.parts_ref = s16[8,528,128]{2,1,0:T(8,128)(2,1)S(1)} all-to-all(s16[8,528,128]{2,1,0:T(8,128)(2,1)S(1)} %weighted_sums.1), channel_id=1, replica_groups=mesh['y'=4,'z'=8,'half'=2,'core'=2,'x'=4] {'y','half'}, dimensions={0} | all-to-all | bytes 2162688 | tf_op jit(solution)/shard_map/all_to_all | solution.py:38
  108.3 0.0 copy-done.1
  108.3 0.7 score_parts.1
  109.0 10.1 %all_to_all.37.parts_ref = f32[16,24,128]{2,1,0:T(8,128)S(1)} all-to-all(f32[16,24,128]{2,1,0:T(8,128)S(1)} %get-tuple-element.24), channel_id=1, replica_groups=mesh['y'=4,'z'=8,'half'=2,'core'=2,'x'=4] {'y','x'}, dimensions={0} | all-to-all | bytes 393216 | tf_op jit(solution)/shard_map/all_to_all | solution.py:38
  119.2 0.8 finish_scores.1
  120.0 7.8 %all-to-all-start.6 = ((s16[16,64,128]{2,1,0:T(8,128)(2,1)}), s16[16,64,128]{2,1,0:T(8,128)(2,1)S(1)}, u32[]{:S(2)}, u32[]{:S(2)}) async-start(s16[16,64,128]{2,1,0:T(8,128)(2,1)} %get-tuple-element.27), calls=%async_computation.6 | async-start | bytes 524288 | tf_op jit(solution)/shard_map/all_to_all | solution.py:38
  127.8 12.8 %all-to-all-done.6.near_ref = s16[16,64,128]{2,1,0:T(8,128)(2,1)S(1)} async-done(((s16[16,64,128]{2,1,0:T(8,128)(2,1)}), s16[16,64,128]{2,1,0:T(8,128)(2,1)S(1)}, u32[]{:S(2)}, u32[]{:S(2)}) %all-to-all-start.6) | async-done | bytes 262176 | tf_op jit(solution)/shard_map/all_to_all | solution.py:38
  140.6 10.1 %collective-permute-start.1 = (s16[16,64,128]{2,1,0:T(8,128)(2,1)S(1)}, s16[16,64,128]{2,1,0:T(8,128)(2,1)S(1)}, u32[]{:S(2)}, u32[]{:S(2)}) collective-permute-start(s16[16,64,128]{2,1,0:T(8,128)(2,1)S(1)} %all-to-all-done.6.near_ref), channel_id=1, source_target_pairs={{0,4},{4,0},{1,5},{5,1},{2,6},{6,2},{3,7},{7,3},{8,12},{12,8},{9,1... | collective-permute-start | bytes 786440 | tf_op jit(solution)/shard_map/ppermute | solution.py:392
  150.6 0.7 multiply_convert_fusion
  151.4 0.4 collective-permute-done.1.far_ref
  151.8 2.1 %pick_scores.1 = f32[256,256]{1,0:T(8,128)} custom-call(s32[512]{0:T(512)S(1)} %multiply_add_fusion.rows_ref, s16[16,64,128]{2,1,0:T(8,128)(2,1)S(1)} %all-to-all-done.6.near_ref, s16[16,64,128]{2,1,0:T(8,128)(2,1)S(1)} %collective-permute-done.1.far_ref), custom_call_target="tpu_custom_call" | custom-call | tf_op jit(solution)/shard_map/pick_scores/pallas_call | solution.py:318
  (19 shorter events, 0.2 us)
Async XLA Ops:
  7.2 14.7 %copy-start = (bf16[256,2048]{1,0:T(8,128)(2,1)S(1)}, bf16[256,2048]{1,0:T(8,128)(2,1)}, u32[]{:S(2)}) copy-start(bf16[256,2048]{1,0:T(8,128)(2,1)} %param.8) | copy-start | bytes 3145732
  7.2 13.7 %copy-start.2 = (s32[256,2]{0,1:T(2,128)S(1)}, s32[256,2]{0,1:T(2,128)}, u32[]{:S(2)}) copy-start(s32[256,2]{0,1:T(2,128)} %param.9) | copy-start | bytes 6148
  7.2 66.3 %all-gather.2.cloned.1.call-start = ((), (), s32[]{:S(2)}) async-start(), calls=%async_computation.7 | async-start | bytes 2228224 | tf_op jit(solution)/shard_map/all_gather | solution.py:373
  9.7 12.5 %all-to-all-start.2 = ((bf16[4,128,512]{2,1,0:T(8,128)(2,1)}), bf16[4,128,512]{2,1,0:T(8,128)(2,1)S(1)}, u32[]{:S(2)}, u32[]{:S(2)}) async-start(bf16[4,128,512]{2,1,0:T(8,128)(2,1)} %broadcast_in_dim.14), calls=%async_computation.2 | async-start | bytes 1048576 | tf_op jit(solution)/shard_map/all_to_all | solution.py:38
  22.2 30.5 %all-to-all-start.1 = ((s32[16,1,128]{2,1,0:T(1,128)}), s32[16,1,128]{2,1,0:T(1,128)S(1)}, u32[]{:S(2)}, u32[]{:S(2)}) async-start(s32[16,1,128]{2,1,0:T(1,128)} %bitcast.6), calls=%async_computation.1 | async-start | bytes 16384 | tf_op jit(solution)/shard_map/all_to_all | solution.py:38
  41.0 30.1 %collective-permute-start = (bf16[4,128,512]{2,1,0:T(8,128)(2,1)S(1)}, bf16[4,128,512]{2,1,0:T(8,128)(2,1)S(1)}, u32[]{:S(2)}, u32[]{:S(2)}) collective-permute-start(bf16[4,128,512]{2,1,0:T(8,128)(2,1)S(1)} %all-to-all-done.2), channel_id=1, source_target_pairs={{0,8},{8,0},{1,9},{9,1},{2,10},{10,2},{3,11},{11,3},{4,12},{12,4},... | collective-permute-start | bytes 1572872 | tf_op jit(solution)/shard_map/ppermute | solution.py:375
  52.6 17.9 %all-to-all-start = ((s32[8,4,128]{2,1,0:T(4,128)}), s32[8,4,128]{2,1,0:T(4,128)S(1)}, u32[]{:S(2)}, u32[]{:S(2)}) async-start(s32[8,4,128]{2,1,0:T(4,128)} %maximum_convert_fusion), calls=%async_computation | async-start | bytes 32768 | tf_op jit(solution)/shard_map/all_to_all | solution.py:38
  89.5 18.8 %copy-start.1 = (bf16[128,512]{1,0:T(8,128)(2,1)S(1)}, bf16[128,512]{1,0:T(8,128)(2,1)}, u32[]{:S(2)}) copy-start(bf16[128,512]{1,0:T(8,128)(2,1)} %own_ref.1) | copy-start | bytes 393220
  120.0 20.6 %all-to-all-start.6 = ((s16[16,64,128]{2,1,0:T(8,128)(2,1)}), s16[16,64,128]{2,1,0:T(8,128)(2,1)S(1)}, u32[]{:S(2)}, u32[]{:S(2)}) async-start(s16[16,64,128]{2,1,0:T(8,128)(2,1)} %get-tuple-element.27), calls=%async_computation.6 | async-start | bytes 524288 | tf_op jit(solution)/shard_map/all_to_all | solution.py:38
  140.6 11.2 %collective-permute-start.1 = (s16[16,64,128]{2,1,0:T(8,128)(2,1)S(1)}, s16[16,64,128]{2,1,0:T(8,128)(2,1)S(1)}, u32[]{:S(2)}, u32[]{:S(2)}) collective-permute-start(s16[16,64,128]{2,1,0:T(8,128)(2,1)S(1)} %all-to-all-done.6.near_ref), channel_id=1, source_target_pairs={{0,4},{4,0},{1,5},{5,1},{2,6},{6,2},{3,7},{7,3},{8,12},{12,8},{9,1... | collective-permute-start | bytes 786440 | tf_op jit(solution)/shard_map/ppermute | solution.py:392
Sparse Core Ops, SparseCore 0:
  10.1 63.3 all-gather.1

commit v9 on v8

--- a/solution.py
+++ b/solution.py
@@ -371,11 +371,10 @@
     zs = 2 * halves
     rows, width = descriptors.shape
     everything = lax.all_gather(descriptors, ("z", "core"), axis=0, tiled=True)
-    near = spread(descriptors, "y", ys)
-    far = lax.ppermute(near, "half", [(0, 1), (1, 0)])
+    other = lax.ppermute(descriptors, "half", [(0, 1), (1, 0)])
     first = lax.axis_index("half") == 0
-    own = jnp.stack([jnp.where(first, near, far), jnp.where(first, far, near)], axis=1)
-    own = own.reshape(2 * ys * rows, width)
+    pair = jnp.concatenate([jnp.where(first, descriptors, other), jnp.where(first, other, descriptors)], axis=0)
+    own = spread(pair, "y", ys).reshape(2 * ys * rows, width)
     high, low = build_table(neighbours, owned, ys * zs * CORES, halves)
     source, at = slot_orders(high, low, ys, halves)
     chosen, score_rows = query_entries(queries, candidates, xs, ys, zs)

time: 161 us -> 157 us (0.975)
  blocking collectives: 36.5 us -> 33.3 us
  starting transfers between devices: 47 us -> 44.9 us
    all_to_all x4, waiting for transfers between devices: 36 us -> 39.3 us  [exchange(): return lax.all_to_all(parts, axis, split_axis=0, concat_axis=0, tiled=True)]
    all_to_all x3, blocking collectives: 36.5 us -> 33.3 us  [exchange(): return lax.all_to_all(parts, axis, split_axis=0, concat_axis=0, tiled=True)]
    all_to_all x4, starting transfers between devices: 34.2 us -> 32 us  [exchange(): return lax.all_to_all(parts, axis, split_axis=0, concat_axis=0, tiled=True)]
    all_gather x1, waiting for transfers between devices: 2.21 us -> 0.01 us  [per_device(): everything = lax.all_gather(descriptors, ('z', 'core'), axis=0, tiled=True)]
    ppermute x1, starting transfers between devices: 2.67 us -> 4.37 us  [per_device(): other = lax.ppermute(descriptors, 'half', [(0, 1), (1, 0)])]
where the time goes in v9:
time: 157 us; the launch traced here: 156 us
  starting transfers between devices  44.9 us (29%)
  waiting for transfers between devices  40.4 us (26%)
  blocking collectives  33.3 us (21%)
  Pallas kernels  15.2 us (10%)
  between operations  14.3 us (9%)
  local copies, waits for them, and re-layouts  5.47 us (3%)
  other arithmetic  2.5 us (2%)
    all_to_all x4, waiting for transfers between devices, exchange(): return lax.all_to_all(parts, axis, split_axis=0, concat_axis=0, tiled=True)  39.3 us
    all_to_all x3, blocking collectives, exchange(): return lax.all_to_all(parts, axis, split_axis=0, concat_axis=0, tiled=True)  33.3 us
    all_to_all x4, starting transfers between devices, exchange(): return lax.all_to_all(parts, axis, split_axis=0, concat_axis=0, tiled=True)  32 us
    ppermute x1, starting transfers between devices, per_device(): far = lax.ppermute(near, 'core', [(0, 1), (1, 0)])  8.54 us
    pallas_call x1, Pallas kernels, similar_parts(): pl.pallas_call(similar_kernel, in_specs=[outside, vmem, vmem, vmem], out_...  4.9 us
    ppermute x1, starting transfers between devices, per_device(): other = lax.ppermute(descriptors, 'half', [(0, 1), (1, 0)])  4.37 us
    pallas_call x1, Pallas kernels, weighted_sums(): pl.pallas_call(sum_kernel, in_specs=[pl.BlockSpec(memory_space=HBM), vmem...  3.45 us
    pallas_call x1, Pallas kernels, build_table(): pl.pallas_call(functools.partial(table_kernel, halves), out_shape=[jax.Sh...  3.26 us
  transfers between devices with their start and end apart: 7, of which 5 were waited for; matrix products, arithmetic and copies ran while one was open for 5% of the time, Pallas kernels for 2%

profile of v9, /device:TPU:1, one launch (start us, length us, event | category | flops | bytes accessed | tf_op | source)
XLA Modules:
  0.0 156.4 jit_solution(12244176103364442891)
XLA Ops:
  7.2 0.0 copy-start
  7.2 0.0 copy-start.1
  7.2 0.0 all-gather.2.cloned.1.call-start
  7.2 0.7 all-gather.2.cloned.1.call-update
  7.9 4.4 %collective-permute-start = (bf16[128,512]{1,0:T(8,128)(2,1)}, bf16[128,512]{1,0:T(8,128)(2,1)S(1)}, u32[]{:S(2)}, u32[]{:S(2)}) collective-permute-start(bf16[128,512]{1,0:T(8,128)(2,1)} %own_ref.1), channel_id=1, source_target_pairs={{0,8},{8,0},{1,9},{9,1},{2,10},{10,2},{3,11},{11,3},{4,12},{12,4},... | collective-permute-start | bytes 393224 | tf_op jit(solution)/shard_map/ppermute | solution.py:374
  12.3 0.8 copy.49.listed_ref
  13.1 0.8 copy.50.owned_ref
  13.9 3.3 %slot_table.1 = (f32[16,128]{1,0:T(8,128)S(1)}, f32[16,128]{1,0:T(8,128)S(1)}) custom-call(s32[128,10]{1,0:T(8,128)S(1)} %copy.49.listed_ref, s32[128,10]{1,0:T(8,128)S(1)} %copy.50.owned_ref), custom_call_target="tpu_custom_call" | custom-call | tf_op jit(solution)/shard_map/slot_table/pallas_call | solution.py:87
  17.2 0.1 reshape.139
  17.3 0.7 reshape.140
  18.0 15.2 %all-to-all-start.1 = ((s32[16,1,128]{2,1,0:T(1,128)}), s32[16,1,128]{2,1,0:T(1,128)S(1)}, u32[]{:S(2)}, u32[]{:S(2)}) async-start(s32[16,1,128]{2,1,0:T(1,128)} %bitcast.6), calls=%async_computation.1 | async-start | bytes 16384 | tf_op jit(solution)/shard_map/all_to_all | solution.py:38
  33.2 0.8 copy.60
  34.0 0.1 eq.60
  34.1 0.3 convert_reduce_fusion
  34.4 0.1 eq.64
  34.5 0.1 copy.61
  34.6 0.7 broadcast_compare_fusion
  35.3 0.0 copy-done
  35.3 0.3 fusion.9
  35.6 0.1 reshape.145
  35.7 0.6 maximum_convert_fusion
  36.4 0.0 collective-permute-done
  36.4 0.0 copy-done.1
  36.4 8.7 %all-to-all-done.1 = s32[16,1,128]{2,1,0:T(1,128)S(1)} async-done(((s32[16,1,128]{2,1,0:T(1,128)}), s32[16,1,128]{2,1,0:T(1,128)S(1)}, u32[]{:S(2)}, u32[]{:S(2)}) %all-to-all-start.1) | async-done | bytes 8224 | tf_op jit(solution)/shard_map/all_to_all | solution.py:38
  45.1 5.1 %all-to-all-start = ((s32[8,4,128]{2,1,0:T(4,128)}), s32[8,4,128]{2,1,0:T(4,128)S(1)}, u32[]{:S(2)}, u32[]{:S(2)}) async-start(s32[8,4,128]{2,1,0:T(4,128)} %maximum_convert_fusion), calls=%async_computation | async-start | bytes 32768 | tf_op jit(solution)/shard_map/all_to_all | solution.py:38
  50.2 5.3 %all-to-all-done = s32[8,4,128]{2,1,0:T(4,128)S(1)} async-done(((s32[8,4,128]{2,1,0:T(4,128)}), s32[8,4,128]{2,1,0:T(4,128)S(1)}, u32[]{:S(2)}, u32[]{:S(2)}) %all-to-all-start) | async-done | bytes 16416 | tf_op jit(solution)/shard_map/all_to_all | solution.py:38
  55.4 1.1 broadcast_in_dim.14
  56.5 3.5 %all-to-all-start.2 = ((bf16[4,256,512]{2,1,0:T(8,128)(2,1)}), bf16[4,256,512]{2,1,0:T(8,128)(2,1)S(1)}, u32[]{:S(2)}, u32[]{:S(2)}) async-start(bf16[4,256,512]{2,1,0:T(8,128)(2,1)} %broadcast_in_dim.14), calls=%async_computation.2 | async-start | bytes 2097152 | tf_op jit(solution)/shard_map/all_to_all | solution.py:38
  60.1 0.1 select_reduce_fusion
  60.1 0.1 select_n.62
  60.2 0.1 stack_reshape.3
  60.3 0.1 select_n.60
  60.5 0.1 select_n.57
  60.6 0.1 copy.56
  60.7 0.2 reshape.141.src_ref
  60.9 12.6 %all-to-all-done.2 = bf16[4,256,512]{2,1,0:T(8,128)(2,1)S(1)} async-done(((bf16[4,256,512]{2,1,0:T(8,128)(2,1)}), bf16[4,256,512]{2,1,0:T(8,128)(2,1)S(1)}, u32[]{:S(2)}, u32[]{:S(2)}) %all-to-all-start.2) | async-done | bytes 1048608 | tf_op jit(solution)/shard_map/all_to_all | solution.py:38
  73.5 0.0 all-gather.2.cloned.1.call-done.all_ref
  73.5 4.9 %similar_parts.1 = (bf16[2,16,128,512]{3,2,1,0:T(8,128)(2,1)}, f32[32,128]{1,0:T(8,128)S(1)}) custom-call(bf16[2048,512]{1,0:T(8,128)(2,1)} %all-gather.2.cloned.1.call-done.all_ref, bf16[1024,512]{1,0:T(8,128)(2,1)S(1)} %bitcast.28, s32[16,256]{1,0:T(8,128)S(1)} %reshape.141.src_ref, s32[32,128]{1,0:T(8,128)S(1)} %bitcast.29), custom_call_target="tpu_custom_call" | custom-call | tf_op jit(solution)/shard_map/similar_parts/pallas_call | solution.py:146
  78.5 8.8 %all_to_all.35.sims_ref.chosen_ref = f32[4,96,128]{2,1,0:T(8,128)S(1)} all-to-all(f32[4,96,128]{2,1,0:T(8,128)S(1)} %pad_maximum_fusion.1), channel_id=1, replica_groups=mesh['y'=4,'z'=8,'half'=2,'core'=2,'x'=4] {'x'}, dimensions={0} | all-to-all | bytes 393216 | tf_op jit(solution)/shard_map/all_to_all | solution.py:38
  87.3 3.5 %weighted_sums.1 = s16[8,528,128]{2,1,0:T(8,128)(2,1)S(1)} custom-call(bf16[2,16,128,512]{3,2,1,0:T(8,128)(2,1)} %get-tuple-element.20.got_ref, f32[4,96,128]{2,1,0:T(8,128)S(1)} %all_to_all.35.sims_ref.chosen_ref, s32[32,128]{1,0:T(8,128)S(1)} %bitcast.30), custom_call_target="tpu_custom_call" | custom-call | tf_op jit(solution)/shard_map/weighted_sums/pallas_call | solution.py:204
  90.7 14.5 %all_to_all.36.parts_ref = s16[8,528,128]{2,1,0:T(8,128)(2,1)S(1)} all-to-all(s16[8,528,128]{2,1,0:T(8,128)(2,1)S(1)} %weighted_sums.1), channel_id=1, replica_groups=mesh['y'=4,'z'=8,'half'=2,'core'=2,'x'=4] {'y','half'}, dimensions={0} | all-to-all | bytes 2162688 | tf_op jit(solution)/shard_map/all_to_all | solution.py:38
  105.2 0.7 score_parts.1
  105.9 10.1 %all_to_all.37.parts_ref = f32[16,24,128]{2,1,0:T(8,128)S(1)} all-to-all(f32[16,24,128]{2,1,0:T(8,128)S(1)} %get-tuple-element.24), channel_id=1, replica_groups=mesh['y'=4,'z'=8,'half'=2,'core'=2,'x'=4] {'y','x'}, dimensions={0} | all-to-all | bytes 393216 | tf_op jit(solution)/shard_map/all_to_all | solution.py:38
  116.0 0.8 finish_scores.1
  116.8 8.2 %all-to-all-start.6 = ((s16[16,64,128]{2,1,0:T(8,128)(2,1)}), s16[16,64,128]{2,1,0:T(8,128)(2,1)S(1)}, u32[]{:S(2)}, u32[]{:S(2)}) async-start(s16[16,64,128]{2,1,0:T(8,128)(2,1)} %get-tuple-element.27), calls=%async_computation.6 | async-start | bytes 524288 | tf_op jit(solution)/shard_map/all_to_all | solution.py:38
  125.0 12.8 %all-to-all-done.6.near_ref = s16[16,64,128]{2,1,0:T(8,128)(2,1)S(1)} async-done(((s16[16,64,128]{2,1,0:T(8,128)(2,1)}), s16[16,64,128]{2,1,0:T(8,128)(2,1)S(1)}, u32[]{:S(2)}, u32[]{:S(2)}) %all-to-all-start.6) | async-done | bytes 262176 | tf_op jit(solution)/shard_map/all_to_all | solution.py:38
  137.8 8.5 %collective-permute-start.1 = (s16[16,64,128]{2,1,0:T(8,128)(2,1)S(1)}, s16[16,64,128]{2,1,0:T(8,128)(2,1)S(1)}, u32[]{:S(2)}, u32[]{:S(2)}) collective-permute-start(s16[16,64,128]{2,1,0:T(8,128)(2,1)S(1)} %all-to-all-done.6.near_ref), channel_id=1, source_target_pairs={{0,4},{4,0},{1,5},{5,1},{2,6},{6,2},{3,7},{7,3},{8,12},{12,8},{9,1... | collective-permute-start | bytes 786440 | tf_op jit(solution)/shard_map/ppermute | solution.py:391
  146.3 0.7 multiply_convert_fusion
  147.1 0.4 collective-permute-done.1.far_ref
  147.4 2.1 %pick_scores.1 = f32[256,256]{1,0:T(8,128)} custom-call(s32[512]{0:T(512)S(1)} %multiply_add_fusion.rows_ref, s16[16,64,128]{2,1,0:T(8,128)(2,1)S(1)} %all-to-all-done.6.near_ref, s16[16,64,128]{2,1,0:T(8,128)(2,1)S(1)} %collective-permute-done.1.far_ref), custom_call_target="tpu_custom_call" | custom-call | tf_op jit(solution)/shard_map/pick_scores/pallas_call | solution.py:318
  (20 shorter events, 0.3 us)
Async XLA Ops:
  7.2 28.2 %copy-start = (bf16[256,2048]{1,0:T(8,128)(2,1)S(1)}, bf16[256,2048]{1,0:T(8,128)(2,1)}, u32[]{:S(2)}) copy-start(bf16[256,2048]{1,0:T(8,128)(2,1)} %param.8) | copy-start | bytes 3145732
  7.2 29.2 %copy-start.1 = (bf16[128,512]{1,0:T(8,128)(2,1)S(1)}, bf16[128,512]{1,0:T(8,128)(2,1)}, u32[]{:S(2)}) copy-start(bf16[128,512]{1,0:T(8,128)(2,1)} %own_ref.1) | copy-start | bytes 393220
  7.2 66.3 %all-gather.2.cloned.1.call-start = ((), (), s32[]{:S(2)}) async-start(), calls=%async_computation.7 | async-start | bytes 2228224 | tf_op jit(solution)/shard_map/all_gather | solution.py:373
  7.9 28.4 %collective-permute-start = (bf16[128,512]{1,0:T(8,128)(2,1)}, bf16[128,512]{1,0:T(8,128)(2,1)S(1)}, u32[]{:S(2)}, u32[]{:S(2)}) collective-permute-start(bf16[128,512]{1,0:T(8,128)(2,1)} %own_ref.1), channel_id=1, source_target_pairs={{0,8},{8,0},{1,9},{9,1},{2,10},{10,2},{3,11},{11,3},{4,12},{12,4},... | collective-permute-start | bytes 393224 | tf_op jit(solution)/shard_map/ppermute | solution.py:374
  18.0 27.1 %all-to-all-start.1 = ((s32[16,1,128]{2,1,0:T(1,128)}), s32[16,1,128]{2,1,0:T(1,128)S(1)}, u32[]{:S(2)}, u32[]{:S(2)}) async-start(s32[16,1,128]{2,1,0:T(1,128)} %bitcast.6), calls=%async_computation.1 | async-start | bytes 16384 | tf_op jit(solution)/shard_map/all_to_all | solution.py:38
  45.1 10.4 %all-to-all-start = ((s32[8,4,128]{2,1,0:T(4,128)}), s32[8,4,128]{2,1,0:T(4,128)S(1)}, u32[]{:S(2)}, u32[]{:S(2)}) async-start(s32[8,4,128]{2,1,0:T(4,128)} %maximum_convert_fusion), calls=%async_computation | async-start | bytes 32768 | tf_op jit(solution)/shard_map/all_to_all | solution.py:38
  56.5 17.0 %all-to-all-start.2 = ((bf16[4,256,512]{2,1,0:T(8,128)(2,1)}), bf16[4,256,512]{2,1,0:T(8,128)(2,1)S(1)}, u32[]{:S(2)}, u32[]{:S(2)}) async-start(bf16[4,256,512]{2,1,0:T(8,128)(2,1)} %broadcast_in_dim.14), calls=%async_computation.2 | async-start | bytes 2097152 | tf_op jit(solution)/shard_map/all_to_all | solution.py:38
  116.8 21.0 %all-to-all-start.6 = ((s16[16,64,128]{2,1,0:T(8,128)(2,1)}), s16[16,64,128]{2,1,0:T(8,128)(2,1)S(1)}, u32[]{:S(2)}, u32[]{:S(2)}) async-start(s16[16,64,128]{2,1,0:T(8,128)(2,1)} %get-tuple-element.27), calls=%async_computation.6 | async-start | bytes 524288 | tf_op jit(solution)/shard_map/all_to_all | solution.py:38
  137.8 9.7 %collective-permute-start.1 = (s16[16,64,128]{2,1,0:T(8,128)(2,1)S(1)}, s16[16,64,128]{2,1,0:T(8,128)(2,1)S(1)}, u32[]{:S(2)}, u32[]{:S(2)}) collective-permute-start(s16[16,64,128]{2,1,0:T(8,128)(2,1)S(1)} %all-to-all-done.6.near_ref), channel_id=1, source_target_pairs={{0,4},{4,0},{1,5},{5,1},{2,6},{6,2},{3,7},{7,3},{8,12},{12,8},{9,1... | collective-permute-start | bytes 786440 | tf_op jit(solution)/shard_map/ppermute | solution.py:391
Sparse Core Ops, SparseCore 0:
  10.1 59.5 all-gather.1

commit v10 on v9

--- a/solution.py
+++ b/solution.py
@@ -94,7 +94,7 @@
 
 
 def similar_kernel(all_ref, own_ref, src_ref, at_ref, got_ref, sims_ref, held_ref, out_ref, in_sems, out_sems):
-    shards = own_ref.shape[0] // BLOCK
+    shards = 2 * own_ref.shape[0]
     kinds = 2 * shards
     slots = kinds * PLACES
     groups = src_ref.shape[0] // GROUP
@@ -119,7 +119,7 @@
                 chunk = jnp.concatenate([part[k * PLACES : (k + 1) * PLACES] for part in parts], axis=0)
                 out_ref[group, k] = chunk
                 chunks.append(chunk)
-            own = own_ref[shard * BLOCK : (shard + 1) * BLOCK, :]
+            own = own_ref[shard // 2, shard % 2 * BLOCK : (shard % 2 + 1) * BLOCK, :]
             dots = lax.dot_general(own, jnp.concatenate(chunks, axis=0), NT, preferred_element_type=f32)
             for kind in range(2):
                 n = group * kinds + 2 * shard + kind
@@ -137,9 +137,9 @@
 
 
 def similar_parts(everything, own, source, at):
-    width = own.shape[1]
+    width = own.shape[2]
     groups = everything.shape[0] // BLOCK // GROUP
-    kinds = 2 * own.shape[0] // BLOCK
+    kinds = 4 * own.shape[0]
     vmem = pl.BlockSpec(memory_space=pltpu.VMEM)
     outside = pl.BlockSpec(memory_space=HBM)
     shape = (groups, kinds, LANES, width)
@@ -327,13 +327,29 @@
     )(rows, near, far)
 
 
-def slot_orders(high, low, ys, halves):
+def own_and_orders(descriptors, high, low, ys, halves):
+    rows, width = descriptors.shape
     shards = 2 * ys
     count = halves * CORES
     groups = count // GROUP
-    codes = jnp.concatenate([high.reshape(shards, -1), low.reshape(shards, -1)], axis=1)
-    codes = exchange(codes.astype(i32).reshape(shards, 2 * groups, LANES), ("y", "half"))
-    codes = codes.reshape(shards, 2, groups, LANES)
+    first = lax.axis_index("half") == 0
+
+    def in_order(mine, other, axis):
+        return jnp.stack([jnp.where(first, mine, other), jnp.where(first, other, mine)], axis=axis)
+
+    def swap(value):
+        return lax.ppermute(value, "half", [(0, 1), (1, 0)])
+
+    pair = in_order(descriptors, swap(descriptors), 0).reshape(2 * rows, width)
+    codes = jnp.concatenate([high.reshape(shards, -1), low.reshape(shards, -1)], axis=1).astype(bf16)
+    codes = codes.reshape(ys, 2, -1)
+    mine = jnp.where(first, codes[:, 0], codes[:, 1])
+    other = swap(jnp.where(first, codes[:, 1], codes[:, 0]))
+    codes = in_order(mine, other, 1)
+    sent = jnp.pad(codes, ((0, 0), (0, PLACES - 2), (0, width - codes.shape[2])))
+    sent = jnp.concatenate([jnp.broadcast_to(pair[None], (ys,) + pair.shape), sent], axis=1)
+    own = exchange(sent, "y")
+    codes = own[:, 2 * rows : 2 * rows + 2, : codes.shape[2]].astype(i32).reshape(shards, 2, groups, LANES)
     ahead_own = codes[:, 0] - 1
     ahead_src = jnp.where(ahead_own >= 0, lax.shift_right_logical(codes[:, 1], 1), -1)
     back = jnp.where(high > 0, (high - 1) * 256 + low, -1).astype(i32)
@@ -345,7 +361,7 @@
     source = jnp.stack([ahead_src.reshape(shards, count, PLACES).transpose(1, 0, 2), back_src], axis=2)
     at = jnp.stack([ahead_own, back_own.transpose(1, 0, 2).reshape(shards, groups, LANES)], axis=1)
     at = at.reshape(2 * shards, groups, LANES).transpose(1, 0, 2).reshape(groups * 2 * shards, LANES)
-    return source.reshape(count, 2 * shards * PLACES), at
+    return own, source.reshape(count, 2 * shards * PLACES), at
 
 
 def query_entries(queries, candidates, xs, ys, zs):
@@ -371,12 +387,8 @@
     zs = 2 * halves
     rows, width = descriptors.shape
     everything = lax.all_gather(descriptors, ("z", "core"), axis=0, tiled=True)
-    other = lax.ppermute(descriptors, "half", [(0, 1), (1, 0)])
-    first = lax.axis_index("half") == 0
-    pair = jnp.concatenate([jnp.where(first, descriptors, other), jnp.where(first, other, descriptors)], axis=0)
-    own = spread(pair, "y", ys).reshape(2 * ys * rows, width)
     high, low = build_table(neighbours, owned, ys * zs * CORES, halves)
-    source, at = slot_orders(high, low, ys, halves)
+    own, source, at = own_and_orders(descriptors, high, low, ys, halves)
     chosen, score_rows = query_entries(queries, candidates, xs, ys, zs)
     source, at, own, chosen, score_rows = lax.optimization_barrier((source, at, own, chosen, score_rows))
     got, sims = similar_parts(everything, own, source, at)

time: 157 us -> 156 us (level)
  blocking collectives: 33.3 us -> 39.1 us
  starting transfers between devices: 44.9 us -> 41.6 us
  waiting for transfers between devices: 40.4 us -> 38.2 us
    all_to_all x3, blocking collectives: 33.3 us -> 39.1 us  [exchange(): return lax.all_to_all(parts, axis, split_axis=0, concat_axis=0, tiled=True)]
    all_to_all x4 -> x3, starting transfers between devices: 32 us -> 26.7 us  [exchange(): return lax.all_to_all(parts, axis, split_axis=0, concat_axis=0, tiled=True)]
    all_to_all x4 -> x3, waiting for transfers between devices: 39.3 us -> 35.8 us  [exchange(): return lax.all_to_all(parts, axis, split_axis=0, concat_axis=0, tiled=True)]
    ppermute x1 -> x2, starting transfers between devices: 4.37 us -> 6.3 us  [swap(): return lax.ppermute(value, 'half', [(0, 1), (1, 0)])]
where the time goes in v10:
time: 156 us
  starting transfers between devices  41.6 us (27%)
  blocking collectives  39.1 us (25%)
  waiting for transfers between devices  38.2 us (24%)
  Pallas kernels  15.2 us (10%)
  between operations  14.4 us (9%)
  local copies, waits for them, and re-layouts  4.55 us (3%)
  other arithmetic  2.4 us (2%)
    all_to_all x3, blocking collectives, exchange(): return lax.all_to_all(parts, axis, split_axis=0, concat_axis=0, tiled=True)  39.1 us
    all_to_all x3, waiting for transfers between devices, exchange(): return lax.all_to_all(parts, axis, split_axis=0, concat_axis=0, tiled=True)  35.8 us
    all_to_all x3, starting transfers between devices, exchange(): return lax.all_to_all(parts, axis, split_axis=0, concat_axis=0, tiled=True)  26.7 us
    ppermute x1, starting transfers between devices, per_device(): far = lax.ppermute(near, 'core', [(0, 1), (1, 0)])  8.54 us
    ppermute x2, starting transfers between devices, swap(): return lax.ppermute(value, 'half', [(0, 1), (1, 0)])  6.3 us
    pallas_call x1, Pallas kernels, similar_parts(): pl.pallas_call(similar_kernel, in_specs=[outside, vmem, vmem, vmem], out_...  4.88 us
    pallas_call x1, Pallas kernels, weighted_sums(): pl.pallas_call(sum_kernel, in_specs=[pl.BlockSpec(memory_space=HBM), vmem...  3.46 us
    pallas_call x1, Pallas kernels, build_table(): pl.pallas_call(functools.partial(table_kernel, halves), out_shape=[jax.Sh...  3.26 us
  transfers between devices with their start and end apart: 7, of which 5 were waited for; matrix products, arithmetic and copies ran while one was open for 5% of the time, Pallas kernels for 2%

profile of v10, /device:TPU:1, one launch (start us, length us, event | category | flops | bytes accessed | tf_op | source)
XLA Modules:
  0.0 155.7 jit_solution(8302854036517222257)
XLA Ops:
  7.2 0.0 copy-start
  7.2 0.0 copy-start.1
  7.2 0.0 all-gather.2.cloned.1.call-start
  7.2 0.7 all-gather.2.cloned.1.call-update
  7.9 4.4 %collective-permute-start = (bf16[128,512]{1,0:T(8,128)(2,1)}, bf16[128,512]{1,0:T(8,128)(2,1)S(1)}, u32[]{:S(2)}, u32[]{:S(2)}) collective-permute-start(bf16[128,512]{1,0:T(8,128)(2,1)} %own_ref.1), channel_id=1, source_target_pairs={{0,8},{8,0},{1,9},{9,1},{2,10},{10,2},{3,11},{11,3},{4,12},{12,4},... | collective-permute-start | bytes 393224 | tf_op jit(solution)/shard_map/ppermute | solution.py:341
  12.3 0.8 copy.87.listed_ref
  13.1 0.8 copy.88.owned_ref
  13.9 3.3 %slot_table.1 = (f32[16,128]{1,0:T(8,128)S(1)}, f32[16,128]{1,0:T(8,128)S(1)}) custom-call(s32[128,10]{1,0:T(8,128)S(1)} %copy.87.listed_ref, s32[128,10]{1,0:T(8,128)S(1)} %copy.88.owned_ref), custom_call_target="tpu_custom_call" | custom-call | tf_op jit(solution)/shard_map/slot_table/pallas_call | solution.py:87
  17.3 1.9 %collective-permute-start.1 = (bf16[4,512]{1,0:T(4,128)(2,1)S(1)}, bf16[4,512]{1,0:T(4,128)(2,1)S(1)}, u32[]{:S(2)}, u32[]{:S(2)}) collective-permute-start(bf16[4,512]{1,0:T(4,128)(2,1)S(1)} %bitcast.62), channel_id=1, source_target_pairs={{0,8},{8,0},{1,9},{9,1},{2,10},{10,2},{3,11},{11,3},{4,12},{12,4},... | collective-permute-start | bytes 12296 | tf_op jit(solution)/shard_map/ppermute | solution.py:341
  19.2 0.1 reshape.146
  19.4 0.7 reshape.147
  20.0 16.2 %all-to-all-start.1 = ((s32[16,1,128]{2,1,0:T(1,128)}), s32[16,1,128]{2,1,0:T(1,128)S(1)}, u32[]{:S(2)}, u32[]{:S(2)}) async-start(s32[16,1,128]{2,1,0:T(1,128)} %bitcast.8), calls=%async_computation.1 | async-start | bytes 16384 | tf_op jit(solution)/shard_map/all_to_all | solution.py:38
  36.2 0.8 copy.99
  37.0 0.1 eq.60
  37.2 0.3 convert_reduce_fusion
  37.4 0.1 eq.64
  37.6 0.1 copy.100
  37.6 0.0 collective-permute-done.1
  37.7 0.0 collective-permute-done
  37.7 0.0 copy-done.1
  37.8 0.1 broadcast_in_dim.16
  37.9 1.1 pad_maximum_fusion
  39.0 0.0 copy-start.2
  39.0 8.9 %all-to-all-done.1 = s32[16,1,128]{2,1,0:T(1,128)S(1)} async-done(((s32[16,1,128]{2,1,0:T(1,128)}), s32[16,1,128]{2,1,0:T(1,128)S(1)}, u32[]{:S(2)}, u32[]{:S(2)}) %all-to-all-start.1) | async-done | bytes 8224 | tf_op jit(solution)/shard_map/all_to_all | solution.py:38
  48.0 4.2 %all-to-all-start = ((bf16[4,272,512]{2,1,0:T(8,128)(2,1)}), bf16[4,272,512]{2,1,0:T(8,128)(2,1)S(1)}, u32[]{:S(2)}, u32[]{:S(2)}) async-start(bf16[4,272,512]{2,1,0:T(8,128)(2,1)} %pad_maximum_fusion), calls=%async_computation | async-start | bytes 2228224 | tf_op jit(solution)/shard_map/all_to_all | solution.py:38
  52.2 0.0 copy-done.2
  52.2 0.0 copy-done
  52.2 0.3 fusion.16
  52.5 0.1 reshape.151
  52.6 0.1 select_reduce_fusion
  52.7 0.1 select_n.101
  52.8 0.1 stack_reshape.3
  52.9 0.1 select_n.99
  53.0 14.1 %all-to-all-done.own_ref = bf16[4,272,512]{2,1,0:T(8,128)(2,1)S(1)} async-done(((bf16[4,272,512]{2,1,0:T(8,128)(2,1)}), bf16[4,272,512]{2,1,0:T(8,128)(2,1)S(1)}, u32[]{:S(2)}, u32[]{:S(2)}) %all-to-all-start) | async-done | bytes 1114144 | tf_op jit(solution)/shard_map/all_to_all | solution.py:38
  67.2 0.1 select_n.96
  67.3 0.1 copy.96
  67.4 0.2 reshape.148.src_ref
  67.6 1.4 all-gather.2.cloned.1.call-done.all_ref
  69.0 4.9 %similar_parts.1 = (bf16[2,16,128,512]{3,2,1,0:T(8,128)(2,1)}, f32[32,128]{1,0:T(8,128)S(1)}) custom-call(bf16[2048,512]{1,0:T(8,128)(2,1)} %all-gather.2.cloned.1.call-done.all_ref, bf16[4,272,512]{2,1,0:T(8,128)(2,1)S(1)} %all-to-all-done.own_ref, s32[16,256]{1,0:T(8,128)S(1)} %reshape.148.src_ref, s32[32,128]{1,0:T(8,128)S(1)} %bitcast.55), custom_call_target="tpu_custom_call" | custom-call | tf_op jit(solution)/shard_map/similar_parts/pallas_call | solution.py:146
  73.9 9.8 %all_to_all.30.sims_ref.chosen_ref = f32[4,96,128]{2,1,0:T(8,128)S(1)} all-to-all(f32[4,96,128]{2,1,0:T(8,128)S(1)} %pad_maximum_fusion.2), channel_id=1, replica_groups=mesh['y'=4,'z'=8,'half'=2,'core'=2,'x'=4] {'x'}, dimensions={0} | all-to-all | bytes 393216 | tf_op jit(solution)/shard_map/all_to_all | solution.py:38
  83.7 3.5 %weighted_sums.1 = s16[8,528,128]{2,1,0:T(8,128)(2,1)S(1)} custom-call(bf16[2,16,128,512]{3,2,1,0:T(8,128)(2,1)} %get-tuple-element.20.got_ref, f32[4,96,128]{2,1,0:T(8,128)S(1)} %all_to_all.30.sims_ref.chosen_ref, s32[32,128]{1,0:T(8,128)S(1)} %bitcast.56), custom_call_target="tpu_custom_call" | custom-call | tf_op jit(solution)/shard_map/weighted_sums/pallas_call | solution.py:204
  87.2 19.1 %all_to_all.31.parts_ref = s16[8,528,128]{2,1,0:T(8,128)(2,1)S(1)} all-to-all(s16[8,528,128]{2,1,0:T(8,128)(2,1)S(1)} %weighted_sums.1), channel_id=1, replica_groups=mesh['y'=4,'z'=8,'half'=2,'core'=2,'x'=4] {'y','half'}, dimensions={0} | all-to-all | bytes 2162688 | tf_op jit(solution)/shard_map/all_to_all | solution.py:38
  106.3 0.7 score_parts.1
  107.0 10.2 %all_to_all.32.parts_ref = f32[16,24,128]{2,1,0:T(8,128)S(1)} all-to-all(f32[16,24,128]{2,1,0:T(8,128)S(1)} %get-tuple-element.24), channel_id=1, replica_groups=mesh['y'=4,'z'=8,'half'=2,'core'=2,'x'=4] {'y','x'}, dimensions={0} | all-to-all | bytes 393216 | tf_op jit(solution)/shard_map/all_to_all | solution.py:38
  117.1 0.8 finish_scores.1
  117.9 6.3 %all-to-all-start.5 = ((s16[16,64,128]{2,1,0:T(8,128)(2,1)}), s16[16,64,128]{2,1,0:T(8,128)(2,1)S(1)}, u32[]{:S(2)}, u32[]{:S(2)}) async-start(s16[16,64,128]{2,1,0:T(8,128)(2,1)} %get-tuple-element.27), calls=%async_computation.5 | async-start | bytes 524288 | tf_op jit(solution)/shard_map/all_to_all | solution.py:38
  124.3 12.8 %all-to-all-done.5.near_ref = s16[16,64,128]{2,1,0:T(8,128)(2,1)S(1)} async-done(((s16[16,64,128]{2,1,0:T(8,128)(2,1)}), s16[16,64,128]{2,1,0:T(8,128)(2,1)S(1)}, u32[]{:S(2)}, u32[]{:S(2)}) %all-to-all-start.5) | async-done | bytes 262176 | tf_op jit(solution)/shard_map/all_to_all | solution.py:38
  137.0 8.5 %collective-permute-start.2 = (s16[16,64,128]{2,1,0:T(8,128)(2,1)S(1)}, s16[16,64,128]{2,1,0:T(8,128)(2,1)S(1)}, u32[]{:S(2)}, u32[]{:S(2)}) collective-permute-start(s16[16,64,128]{2,1,0:T(8,128)(2,1)S(1)} %all-to-all-done.5.near_ref), channel_id=1, source_target_pairs={{0,4},{4,0},{1,5},{5,1},{2,6},{6,2},{3,7},{7,3},{8,12},{12,8},{9,1... | collective-permute-start | bytes 786440 | tf_op jit(solution)/shard_map/ppermute | solution.py:403
  145.6 0.7 multiply_convert_fusion
  146.3 0.4 collective-permute-done.2.far_ref
  146.7 2.1 %pick_scores.1 = f32[256,256]{1,0:T(8,128)} custom-call(s32[512]{0:T(512)S(1)} %multiply_add_fusion.rows_ref, s16[16,64,128]{2,1,0:T(8,128)(2,1)S(1)} %all-to-all-done.5.near_ref, s16[16,64,128]{2,1,0:T(8,128)(2,1)S(1)} %collective-permute-done.2.far_ref), custom_call_target="tpu_custom_call" | custom-call | tf_op jit(solution)/shard_map/pick_scores/pallas_call | solution.py:318
  (30 shorter events, 0.4 us)
Async XLA Ops:
  7.2 45.0 %copy-start = (bf16[256,2048]{1,0:T(8,128)(2,1)S(1)}, bf16[256,2048]{1,0:T(8,128)(2,1)}, u32[]{:S(2)}) copy-start(bf16[256,2048]{1,0:T(8,128)(2,1)} %param.8) | copy-start | bytes 3145732
  7.2 30.6 %copy-start.1 = (bf16[128,512]{1,0:T(8,128)(2,1)S(1)}, bf16[128,512]{1,0:T(8,128)(2,1)}, u32[]{:S(2)}) copy-start(bf16[128,512]{1,0:T(8,128)(2,1)} %own_ref.1) | copy-start | bytes 393220
  7.2 61.8 %all-gather.2.cloned.1.call-start = ((), (), s32[]{:S(2)}) async-start(), calls=%async_computation.6 | async-start | bytes 2228224 | tf_op jit(solution)/shard_map/all_gather | solution.py:389
  7.9 29.8 %collective-permute-start = (bf16[128,512]{1,0:T(8,128)(2,1)}, bf16[128,512]{1,0:T(8,128)(2,1)S(1)}, u32[]{:S(2)}, u32[]{:S(2)}) collective-permute-start(bf16[128,512]{1,0:T(8,128)(2,1)} %own_ref.1), channel_id=1, source_target_pairs={{0,8},{8,0},{1,9},{9,1},{2,10},{10,2},{3,11},{11,3},{4,12},{12,4},... | collective-permute-start | bytes 393224 | tf_op jit(solution)/shard_map/ppermute | solution.py:341
  17.3 20.3 %collective-permute-start.1 = (bf16[4,512]{1,0:T(4,128)(2,1)S(1)}, bf16[4,512]{1,0:T(4,128)(2,1)S(1)}, u32[]{:S(2)}, u32[]{:S(2)}) collective-permute-start(bf16[4,512]{1,0:T(4,128)(2,1)S(1)} %bitcast.62), channel_id=1, source_target_pairs={{0,8},{8,0},{1,9},{9,1},{2,10},{10,2},{3,11},{11,3},{4,12},{12,4},... | collective-permute-start | bytes 12296 | tf_op jit(solution)/shard_map/ppermute | solution.py:341
  20.0 27.9 %all-to-all-start.1 = ((s32[16,1,128]{2,1,0:T(1,128)}), s32[16,1,128]{2,1,0:T(1,128)S(1)}, u32[]{:S(2)}, u32[]{:S(2)}) async-start(s32[16,1,128]{2,1,0:T(1,128)} %bitcast.8), calls=%async_computation.1 | async-start | bytes 16384 | tf_op jit(solution)/shard_map/all_to_all | solution.py:38
  39.0 13.2 %copy-start.2 = (s32[256,2]{0,1:T(2,128)S(1)}, s32[256,2]{0,1:T(2,128)}, u32[]{:S(2)}) copy-start(s32[256,2]{0,1:T(2,128)} %param.9) | copy-start | bytes 6148
  48.0 19.1 %all-to-all-start = ((bf16[4,272,512]{2,1,0:T(8,128)(2,1)}), bf16[4,272,512]{2,1,0:T(8,128)(2,1)S(1)}, u32[]{:S(2)}, u32[]{:S(2)}) async-start(bf16[4,272,512]{2,1,0:T(8,128)(2,1)} %pad_maximum_fusion), calls=%async_computation | async-start | bytes 2228224 | tf_op jit(solution)/shard_map/all_to_all | solution.py:38
  117.9 19.1 %all-to-all-start.5 = ((s16[16,64,128]{2,1,0:T(8,128)(2,1)}), s16[16,64,128]{2,1,0:T(8,128)(2,1)S(1)}, u32[]{:S(2)}, u32[]{:S(2)}) async-start(s16[16,64,128]{2,1,0:T(8,128)(2,1)} %get-tuple-element.27), calls=%async_computation.5 | async-start | bytes 524288 | tf_op jit(solution)/shard_map/all_to_all | solution.py:38
  137.0 9.7 %collective-permute-start.2 = (s16[16,64,128]{2,1,0:T(8,128)(2,1)S(1)}, s16[16,64,128]{2,1,0:T(8,128)(2,1)S(1)}, u32[]{:S(2)}, u32[]{:S(2)}) collective-permute-start(s16[16,64,128]{2,1,0:T(8,128)(2,1)S(1)} %all-to-all-done.5.near_ref), channel_id=1, source_target_pairs={{0,4},{4,0},{1,5},{5,1},{2,6},{6,2},{3,7},{7,3},{8,12},{12,8},{9,1... | collective-permute-start | bytes 786440 | tf_op jit(solution)/shard_map/ppermute | solution.py:403
Sparse Core Ops, SparseCore 0:
  10.1 58.7 all-gather.1

commit v11 on v10

--- a/solution.py
+++ b/solution.py
@@ -373,7 +373,14 @@
     hits = (flat == here)[None, :] & (rank[None, :] == jnp.arange(PLACES, dtype=i32)[:, None])
     hits = jnp.sum(hits.reshape(PLACES, -1, 2).astype(f32), axis=2).astype(bf16)
     chosen = jnp.dot(hits, queries, preferred_element_type=f32)
-    chosen = chosen.reshape(PLACES, xs, -1, LANES).transpose(1, 2, 0, 3).reshape(xs, -1, LANES)
+    chosen = chosen.reshape(PLACES, xs, -1, LANES).transpose(1, 2, 0, 3).reshape(xs, -1, LANES).astype(bf16)
+    x = lax.axis_index("x")
+    came = []
+    for step in range(xs):
+        piece = lax.dynamic_index_in_dim(chosen, lax.rem(x + step, xs), 0, keepdims=False)
+        came.append(lax.ppermute(piece, "x", [(i, (i + step) % xs) for i in range(xs)]) if step else piece)
+    came = jnp.stack([came[(xs - 1 - i) % xs] for i in range(2 * xs - 1)], axis=0)
+    chosen = lax.dynamic_slice_in_dim(came, xs - 1 - x, xs, 0)
     plane = flat // CORES
     core = flat - plane * CORES
     far = (core != lax.axis_index("core")).astype(i32)
@@ -392,10 +399,9 @@
     chosen, score_rows = query_entries(queries, candidates, xs, ys, zs)
     source, at, own, chosen, score_rows = lax.optimization_barrier((source, at, own, chosen, score_rows))
     got, sims = similar_parts(everything, own, source, at)
-    sims = jnp.concatenate([jnp.broadcast_to(sims[None], (xs,) + sims.shape), chosen], axis=1)
-    sims = exchange(sims, "x")
+    sims = spread(sims, "x", xs)
     parts = exchange(weighted_sums(got, sims, at), ("y", "half"))
-    summed, parts = score_parts(parts, descriptors, sims, ys * xs)
+    summed, parts = score_parts(parts, descriptors, chosen, ys * xs)
     mine, scales = finish_scores(exchange(parts, ("y", "x")), ys, zs, xs * width)
     scale = lax.dynamic_index_in_dim(scales, lax.axis_index("y"), 0, keepdims=False)[0]
     augmented = (summed * scale[:, None]).astype(bf16)

time: 156 us -> 158 us (1.013)
  starting transfers between devices: 41.6 us -> 56.9 us
  waiting for transfers between devices: 38.2 us -> 29 us
  blocking collectives: 39.1 us -> 34.2 us
    ppermute x0 -> x3, starting transfers between devices: none -> 10.6 us  [query_entries(): lax.ppermute(piece, 'x', [(i, (i + step) % xs) for i in range(xs)])]
    all_to_all x3, waiting for transfers between devices: 35.8 us -> 26.6 us  [exchange(): return lax.all_to_all(parts, axis, split_axis=0, concat_axis=0, tiled=True)]
    all_to_all x3, blocking collectives: 39.1 us -> 34.2 us  [exchange(): return lax.all_to_all(parts, axis, split_axis=0, concat_axis=0, tiled=True)]
    all_to_all x3, starting transfers between devices: 26.7 us -> 29.6 us  [exchange(): return lax.all_to_all(parts, axis, split_axis=0, concat_axis=0, tiled=True)]
    ppermute x1, starting transfers between devices: 8.54 us -> 10.3 us  [per_device(): far = lax.ppermute(near, 'core', [(0, 1), (1, 0)])]
  transfers between devices with their start and end apart: 7 -> 10, of which waited for: 5 -> 4; matrix products, arithmetic and copies ran while one was open for 5% -> 5% of each run, Pallas kernels for 2% -> 2%
where the time goes in v11:
time: 158 us
  starting transfers between devices  56.9 us (36%)
  blocking collectives  34.2 us (22%)
  waiting for transfers between devices  29 us (18%)
  Pallas kernels  15.2 us (10%)
  between operations  14.5 us (9%)
  local copies, waits for them, and re-layouts  4.54 us (3%)
  other arithmetic  3.07 us (2%)
    all_to_all x3, blocking collectives, exchange(): return lax.all_to_all(parts, axis, split_axis=0, concat_axis=0, tiled=True)  34.2 us
    all_to_all x3, starting transfers between devices, exchange(): return lax.all_to_all(parts, axis, split_axis=0, concat_axis=0, tiled=True)  29.6 us
    all_to_all x3, waiting for transfers between devices, exchange(): return lax.all_to_all(parts, axis, split_axis=0, concat_axis=0, tiled=True)  26.6 us
    ppermute x3, starting transfers between devices, query_entries(): lax.ppermute(piece, 'x', [(i, (i + step) % xs) for i in range(xs)])  10.6 us
    ppermute x1, starting transfers between devices, per_device(): far = lax.ppermute(near, 'core', [(0, 1), (1, 0)])  10.3 us
    ppermute x2, starting transfers between devices, swap(): return lax.ppermute(value, 'half', [(0, 1), (1, 0)])  6.3 us
    pallas_call x1, Pallas kernels, similar_parts(): pl.pallas_call(similar_kernel, in_specs=[outside, vmem, vmem, vmem], out_...  4.9 us
    pallas_call x1, Pallas kernels, weighted_sums(): pl.pallas_call(sum_kernel, in_specs=[pl.BlockSpec(memory_space=HBM), vmem...  3.46 us
  transfers between devices with their start and end apart: 10, of which 4 were waited for; matrix products, arithmetic and copies ran while one was open for 5% of the time, Pallas kernels for 2%

profile of v11, /device:TPU:1, one launch (start us, length us, event | category | flops | bytes accessed | tf_op | source)
XLA Modules:
  0.0 157.7 jit_solution(2971203320900910560)
XLA Ops:
  7.2 0.0 copy-start
  7.2 0.0 all-gather.2.cloned.1.call-start
  7.2 0.7 all-gather.2.cloned.1.call-update
  7.9 4.4 %collective-permute-start = (bf16[128,512]{1,0:T(8,128)(2,1)}, bf16[128,512]{1,0:T(8,128)(2,1)S(1)}, u32[]{:S(2)}, u32[]{:S(2)}) collective-permute-start(bf16[128,512]{1,0:T(8,128)(2,1)} %own_ref.1), channel_id=1, source_target_pairs={{0,8},{8,0},{1,9},{9,1},{2,10},{10,2},{3,11},{11,3},{4,12},{12,4},... | collective-permute-start | bytes 393224 | tf_op jit(solution)/shard_map/ppermute | solution.py:341
  12.3 0.8 copy.87.listed_ref
  13.1 0.8 copy.88.owned_ref
  13.9 3.3 %slot_table.1 = (f32[16,128]{1,0:T(8,128)S(1)}, f32[16,128]{1,0:T(8,128)S(1)}) custom-call(s32[128,10]{1,0:T(8,128)S(1)} %copy.87.listed_ref, s32[128,10]{1,0:T(8,128)S(1)} %copy.88.owned_ref), custom_call_target="tpu_custom_call" | custom-call | tf_op jit(solution)/shard_map/slot_table/pallas_call | solution.py:87
  17.3 1.9 %collective-permute-start.1 = (bf16[4,512]{1,0:T(4,128)(2,1)S(1)}, bf16[4,512]{1,0:T(4,128)(2,1)S(1)}, u32[]{:S(2)}, u32[]{:S(2)}) collective-permute-start(bf16[4,512]{1,0:T(4,128)(2,1)S(1)} %bitcast.78), channel_id=1, source_target_pairs={{0,8},{8,0},{1,9},{9,1},{2,10},{10,2},{3,11},{11,3},{4,12},{12,4},... | collective-permute-start | bytes 12296 | tf_op jit(solution)/shard_map/ppermute | solution.py:341
  19.2 0.1 reshape.144
  19.3 0.7 reshape.145
  20.0 16.2 %all-to-all-start.1 = ((s32[16,1,128]{2,1,0:T(1,128)}), s32[16,1,128]{2,1,0:T(1,128)S(1)}, u32[]{:S(2)}, u32[]{:S(2)}) async-start(s32[16,1,128]{2,1,0:T(1,128)} %bitcast.8), calls=%async_computation.1 | async-start | bytes 16384 | tf_op jit(solution)/shard_map/all_to_all | solution.py:38
  36.2 0.8 copy.99
  37.0 0.7 broadcast_compare_fusion
  37.7 0.0 copy-start.1
  37.7 0.1 eq.60
  37.8 0.3 convert_reduce_fusion
  38.1 0.1 eq.64
  38.3 0.1 copy.100
  38.4 0.0 copy-done
  38.4 0.2 convolution_convert_fusion
  38.7 3.1 %collective-permute-start.4 = (bf16[64,128]{1,0:T(8,128)(2,1)S(1)}, bf16[64,128]{1,0:T(8,128)(2,1)S(1)}, u32[]{:S(2)}, u32[]{:S(2)}) collective-permute-start(bf16[64,128]{1,0:T(8,128)(2,1)S(1)} %get-tuple-element.32), channel_id=1, source_target_pairs={{0,1},{1,2},{2,3},{3,0},{4,5},{5,6},{6,7},{7,4},{8,9},{9,10},{10,1... | collective-permute-start | bytes 49160 | tf_op jit(solution)/shard_map/ppermute | solution.py:381
  41.9 4.4 %collective-permute-start.3 = (bf16[64,128]{1,0:T(8,128)(2,1)S(1)}, bf16[64,128]{1,0:T(8,128)(2,1)S(1)}, u32[]{:S(2)}, u32[]{:S(2)}) collective-permute-start(bf16[64,128]{1,0:T(8,128)(2,1)S(1)} %get-tuple-element.33), channel_id=1, source_target_pairs={{0,2},{1,3},{2,0},{3,1},{4,6},{5,7},{6,4},{7,5},{8,10},{9,11},{10,... | collective-permute-start | bytes 49160 | tf_op jit(solution)/shard_map/ppermute | solution.py:381
  46.3 3.1 %collective-permute-start.2 = (bf16[64,128]{1,0:T(8,128)(2,1)S(1)}, bf16[64,128]{1,0:T(8,128)(2,1)S(1)}, u32[]{:S(2)}, u32[]{:S(2)}) collective-permute-start(bf16[64,128]{1,0:T(8,128)(2,1)S(1)} %get-tuple-element.34), channel_id=1, source_target_pairs={{0,3},{1,0},{2,1},{3,2},{4,7},{5,4},{6,5},{7,6},{8,11},{9,8},{10,9... | collective-permute-start | bytes 49160 | tf_op jit(solution)/shard_map/ppermute | solution.py:381
  49.4 0.0 collective-permute-done.1
  49.5 1.3 collective-permute-done.2
  50.7 0.0 collective-permute-done.3
  50.8 0.0 collective-permute-done.4
  50.8 0.0 collective-permute-done
  50.8 0.0 copy-done.1
  50.9 0.1 broadcast_in_dim.16
  51.0 1.1 pad_maximum_fusion
  52.1 0.0 all-to-all-done.1
  52.1 4.6 %all-to-all-start = ((bf16[4,272,512]{2,1,0:T(8,128)(2,1)}), bf16[4,272,512]{2,1,0:T(8,128)(2,1)S(1)}, u32[]{:S(2)}, u32[]{:S(2)}) async-start(bf16[4,272,512]{2,1,0:T(8,128)(2,1)} %pad_maximum_fusion), calls=%async_computation | async-start | bytes 2228224 | tf_op jit(solution)/shard_map/all_to_all | solution.py:38
  56.7 0.1 select_reduce_fusion
  56.8 0.1 select_n.117
  56.9 0.1 stack_reshape.3
  57.0 0.1 select_n.115
  57.1 13.7 %all-to-all-done.own_ref = bf16[4,272,512]{2,1,0:T(8,128)(2,1)S(1)} async-done(((bf16[4,272,512]{2,1,0:T(8,128)(2,1)}), bf16[4,272,512]{2,1,0:T(8,128)(2,1)S(1)}, u32[]{:S(2)}, u32[]{:S(2)}) %all-to-all-start) | async-done | bytes 1114144 | tf_op jit(solution)/shard_map/all_to_all | solution.py:38
  70.9 0.1 select_n.112
  71.0 0.1 copy.96
  71.1 0.2 reshape.146.src_ref
  71.3 0.0 all-gather.2.cloned.1.call-done.all_ref
  71.3 4.9 %similar_parts.1 = (bf16[2,16,128,512]{3,2,1,0:T(8,128)(2,1)}, f32[32,128]{1,0:T(8,128)S(1)}) custom-call(bf16[2048,512]{1,0:T(8,128)(2,1)} %all-gather.2.cloned.1.call-done.all_ref, bf16[4,272,512]{2,1,0:T(8,128)(2,1)S(1)} %all-to-all-done.own_ref, s32[16,256]{1,0:T(8,128)S(1)} %reshape.146.src_ref, s32[32,128]{1,0:T(8,128)S(1)} %bitcast.70), custom_call_target="tpu_custom_call" | custom-call | tf_op jit(solution)/shard_map/similar_parts/pallas_call | solution.py:146
  76.3 7.1 %all_to_all.30.sims_ref = f32[4,32,128]{2,1,0:T(8,128)S(1)} all-to-all(f32[4,32,128]{2,1,0:T(8,128)S(1)} %broadcast_in_dim.30), channel_id=1, replica_groups=mesh['y'=4,'z'=8,'half'=2,'core'=2,'x'=4] {'x'}, dimensions={0} | all-to-all | bytes 131072 | tf_op jit(solution)/shard_map/all_to_all | solution.py:38
  83.4 3.5 %weighted_sums.1 = s16[8,528,128]{2,1,0:T(8,128)(2,1)S(1)} custom-call(bf16[2,16,128,512]{3,2,1,0:T(8,128)(2,1)} %get-tuple-element.20.got_ref, f32[4,32,128]{2,1,0:T(8,128)S(1)} %all_to_all.30.sims_ref, s32[32,128]{1,0:T(8,128)S(1)} %bitcast.71), custom_call_target="tpu_custom_call" | custom-call | tf_op jit(solution)/shard_map/weighted_sums/pallas_call | solution.py:204
  86.8 17.1 %all_to_all.31.parts_ref = s16[8,528,128]{2,1,0:T(8,128)(2,1)S(1)} all-to-all(s16[8,528,128]{2,1,0:T(8,128)(2,1)S(1)} %weighted_sums.1), channel_id=1, replica_groups=mesh['y'=4,'z'=8,'half'=2,'core'=2,'x'=4] {'y','half'}, dimensions={0} | all-to-all | bytes 2162688 | tf_op jit(solution)/shard_map/all_to_all | solution.py:38
  104.0 0.7 score_parts.1
  104.7 10.0 %all_to_all.32.parts_ref = f32[16,24,128]{2,1,0:T(8,128)S(1)} all-to-all(f32[16,24,128]{2,1,0:T(8,128)S(1)} %get-tuple-element.24), channel_id=1, replica_groups=mesh['y'=4,'z'=8,'half'=2,'core'=2,'x'=4] {'y','x'}, dimensions={0} | all-to-all | bytes 393216 | tf_op jit(solution)/shard_map/all_to_all | solution.py:38
  114.6 0.8 finish_scores.1
  115.4 8.9 %all-to-all-start.5 = ((s16[16,64,128]{2,1,0:T(8,128)(2,1)}), s16[16,64,128]{2,1,0:T(8,128)(2,1)S(1)}, u32[]{:S(2)}, u32[]{:S(2)}) async-start(s16[16,64,128]{2,1,0:T(8,128)(2,1)} %get-tuple-element.27), calls=%async_computation.5 | async-start | bytes 524288 | tf_op jit(solution)/shard_map/all_to_all | solution.py:38
  124.4 12.8 %all-to-all-done.5.near_ref = s16[16,64,128]{2,1,0:T(8,128)(2,1)S(1)} async-done(((s16[16,64,128]{2,1,0:T(8,128)(2,1)}), s16[16,64,128]{2,1,0:T(8,128)(2,1)S(1)}, u32[]{:S(2)}, u32[]{:S(2)}) %all-to-all-start.5) | async-done | bytes 262176 | tf_op jit(solution)/shard_map/all_to_all | solution.py:38
  137.2 10.3 %collective-permute-start.5 = (s16[16,64,128]{2,1,0:T(8,128)(2,1)S(1)}, s16[16,64,128]{2,1,0:T(8,128)(2,1)S(1)}, u32[]{:S(2)}, u32[]{:S(2)}) collective-permute-start(s16[16,64,128]{2,1,0:T(8,128)(2,1)S(1)} %all-to-all-done.5.near_ref), channel_id=1, source_target_pairs={{0,4},{4,0},{1,5},{5,1},{2,6},{6,2},{3,7},{7,3},{8,12},{12,8},{9,1... | collective-permute-start | bytes 786440 | tf_op jit(solution)/shard_map/ppermute | solution.py:409
  147.5 0.7 multiply_convert_fusion
  148.3 0.4 collective-permute-done.5.far_ref
  148.7 2.1 %pick_scores.1 = f32[256,256]{1,0:T(8,128)} custom-call(s32[512]{0:T(512)S(1)} %multiply_add_fusion.rows_ref, s16[16,64,128]{2,1,0:T(8,128)(2,1)S(1)} %all-to-all-done.5.near_ref, s16[16,64,128]{2,1,0:T(8,128)(2,1)S(1)} %collective-permute-done.5.far_ref), custom_call_target="tpu_custom_call" | custom-call | tf_op jit(solution)/shard_map/pick_scores/pallas_call | solution.py:318
  (38 shorter events, 0.5 us)
Async XLA Ops:
  7.2 31.2 %copy-start = (bf16[256,2048]{1,0:T(8,128)(2,1)S(1)}, bf16[256,2048]{1,0:T(8,128)(2,1)}, u32[]{:S(2)}) copy-start(bf16[256,2048]{1,0:T(8,128)(2,1)} %param.8) | copy-start | bytes 3145732
  7.2 64.2 %all-gather.2.cloned.1.call-start = ((), (), s32[]{:S(2)}) async-start(), calls=%async_computation.6 | async-start | bytes 2228224 | tf_op jit(solution)/shard_map/all_gather | solution.py:396
  7.9 42.9 %collective-permute-start = (bf16[128,512]{1,0:T(8,128)(2,1)}, bf16[128,512]{1,0:T(8,128)(2,1)S(1)}, u32[]{:S(2)}, u32[]{:S(2)}) collective-permute-start(bf16[128,512]{1,0:T(8,128)(2,1)} %own_ref.1), channel_id=1, source_target_pairs={{0,8},{8,0},{1,9},{9,1},{2,10},{10,2},{3,11},{11,3},{4,12},{12,4},... | collective-permute-start | bytes 393224 | tf_op jit(solution)/shard_map/ppermute | solution.py:341
  17.3 32.1 %collective-permute-start.1 = (bf16[4,512]{1,0:T(4,128)(2,1)S(1)}, bf16[4,512]{1,0:T(4,128)(2,1)S(1)}, u32[]{:S(2)}, u32[]{:S(2)}) collective-permute-start(bf16[4,512]{1,0:T(4,128)(2,1)S(1)} %bitcast.78), channel_id=1, source_target_pairs={{0,8},{8,0},{1,9},{9,1},{2,10},{10,2},{3,11},{11,3},{4,12},{12,4},... | collective-permute-start | bytes 12296 | tf_op jit(solution)/shard_map/ppermute | solution.py:341
  20.0 32.1 %all-to-all-start.1 = ((s32[16,1,128]{2,1,0:T(1,128)}), s32[16,1,128]{2,1,0:T(1,128)S(1)}, u32[]{:S(2)}, u32[]{:S(2)}) async-start(s32[16,1,128]{2,1,0:T(1,128)} %bitcast.8), calls=%async_computation.1 | async-start | bytes 16384 | tf_op jit(solution)/shard_map/all_to_all | solution.py:38
  37.7 13.1 %copy-start.1 = (bf16[128,512]{1,0:T(8,128)(2,1)S(1)}, bf16[128,512]{1,0:T(8,128)(2,1)}, u32[]{:S(2)}) copy-start(bf16[128,512]{1,0:T(8,128)(2,1)} %own_ref.1) | copy-start | bytes 393220
  38.7 12.0 %collective-permute-start.4 = (bf16[64,128]{1,0:T(8,128)(2,1)S(1)}, bf16[64,128]{1,0:T(8,128)(2,1)S(1)}, u32[]{:S(2)}, u32[]{:S(2)}) collective-permute-start(bf16[64,128]{1,0:T(8,128)(2,1)S(1)} %get-tuple-element.32), channel_id=1, source_target_pairs={{0,1},{1,2},{2,3},{3,0},{4,5},{5,6},{6,7},{7,4},{8,9},{9,10},{10,1... | collective-permute-start | bytes 49160 | tf_op jit(solution)/shard_map/ppermute | solution.py:381
  41.9 8.9 %collective-permute-start.3 = (bf16[64,128]{1,0:T(8,128)(2,1)S(1)}, bf16[64,128]{1,0:T(8,128)(2,1)S(1)}, u32[]{:S(2)}, u32[]{:S(2)}) collective-permute-start(bf16[64,128]{1,0:T(8,128)(2,1)S(1)} %get-tuple-element.33), channel_id=1, source_target_pairs={{0,2},{1,3},{2,0},{3,1},{4,6},{5,7},{6,4},{7,5},{8,10},{9,11},{10,... | collective-permute-start | bytes 49160 | tf_op jit(solution)/shard_map/ppermute | solution.py:381
  46.3 4.5 %collective-permute-start.2 = (bf16[64,128]{1,0:T(8,128)(2,1)S(1)}, bf16[64,128]{1,0:T(8,128)(2,1)S(1)}, u32[]{:S(2)}, u32[]{:S(2)}) collective-permute-start(bf16[64,128]{1,0:T(8,128)(2,1)S(1)} %get-tuple-element.34), channel_id=1, source_target_pairs={{0,3},{1,0},{2,1},{3,2},{4,7},{5,4},{6,5},{7,6},{8,11},{9,8},{10,9... | collective-permute-start | bytes 49160 | tf_op jit(solution)/shard_map/ppermute | solution.py:381
  52.1 18.7 %all-to-all-start = ((bf16[4,272,512]{2,1,0:T(8,128)(2,1)}), bf16[4,272,512]{2,1,0:T(8,128)(2,1)S(1)}, u32[]{:S(2)}, u32[]{:S(2)}) async-start(bf16[4,272,512]{2,1,0:T(8,128)(2,1)} %pad_maximum_fusion), calls=%async_computation | async-start | bytes 2228224 | tf_op jit(solution)/shard_map/all_to_all | solution.py:38
  115.4 21.8 %all-to-all-start.5 = ((s16[16,64,128]{2,1,0:T(8,128)(2,1)}), s16[16,64,128]{2,1,0:T(8,128)(2,1)S(1)}, u32[]{:S(2)}, u32[]{:S(2)}) async-start(s16[16,64,128]{2,1,0:T(8,128)(2,1)} %get-tuple-element.27), calls=%async_computation.5 | async-start | bytes 524288 | tf_op jit(solution)/shard_map/all_to_all | solution.py:38
  137.2 11.5 %collective-permute-start.5 = (s16[16,64,128]{2,1,0:T(8,128)(2,1)S(1)}, s16[16,64,128]{2,1,0:T(8,128)(2,1)S(1)}, u32[]{:S(2)}, u32[]{:S(2)}) collective-permute-start(s16[16,64,128]{2,1,0:T(8,128)(2,1)S(1)} %all-to-all-done.5.near_ref), channel_id=1, source_target_pairs={{0,4},{4,0},{1,5},{5,1},{2,6},{6,2},{3,7},{7,3},{8,12},{12,8},{9,1... | collective-permute-start | bytes 786440 | tf_op jit(solution)/shard_map/ppermute | solution.py:409
Sparse Core Ops, SparseCore 0:
  10.1 58.7 all-gather.1
